TPU v7x, 32 devices: a whole 2x2x4 slice. The times are simulated.
32 devices in a mesh: node: 8 (over y, x, core), local: 4 (over z).
Axes of the slice: x: 2, y: 2, z: 4, core: 2. Of those that a mesh axis runs over, the one named last changes fastest.
Arguments:
- tokens: bfloat16 [8192, 4096], P(('node', 'local')), may hold values from -6 to 6
- queries: bfloat16 [8192, 4096], P(('node', 'local')), may hold values from -240 to 240
- values: bfloat16 [8192, 512], P(('node', 'local')), may hold values from -6 to 6
- upstream: bfloat16 [8192, 4096], P(('node', 'local')), may hold values from -6 to 6
- key_weight: bfloat16 [4096, 512], P(('node', 'local')), may hold values from -0.09375 to 0.09375
- positions: int32 [8192], P(('node', 'local')), may hold values from 0 to 255, as said below
Outputs:
- grad_tokens: bfloat16 [8192, 4096], P(('node', 'local'))
- grad_weight: float32 [4096, 512], P(('node', 'local'))
Inputs may be any that keep to these rules, and one draw needn't show every extreme that they name: positions[i] counts the earlier tokens of token i's document; every block of 256 rows starts a document, and no document crosses such a block.
All inputs are finite; a program needn't handle non-finite values.
Results may differ from a plain program's by a relative error of at most 0.033.
Values may be sent and summed in bfloat16 or wider, within the bound.
No kernel may reach another device: no remote copies, remote signals or barrier semaphores. Data moves between devices by JAX's collectives and lax.ppermute only.
A program may use at most 128 MiB of HBM per device.

v0:
```python
import jax
import jax.numpy as jnp
from jax import lax
from jax.sharding import PartitionSpec as P

HEAD_SIZE = 128


def angle_tables(positions, head_width):
    half = head_width // 2
    freq = jnp.exp(
        -(jnp.arange(half, dtype=jnp.float32) * 2.0 / head_width) * jnp.log(jnp.float32(1000000.0))
    )
    angle = positions.astype(jnp.float32)[:, None] * freq[None, :]
    return (jnp.cos(angle)[:, None, :], jnp.sin(angle)[:, None, :])


def rotate(raw_keys, cosine, sine_part, head_width, sign):
    item_count, width = raw_keys.shape
    shaped = raw_keys.reshape(item_count, width // head_width, head_width)
    half = head_width // 2
    first, second = (shaped[..., :half], shaped[..., half:])
    joined = jnp.concatenate(
        [first * cosine - sign * second * sine_part, second * cosine + sign * first * sine_part],
        axis=-1,
    )
    return joined.reshape(item_count, width)


def attend_back(queries, keys, values, upstream, positions, head_width):
    item_count, width = keys.shape
    key_value_count = width // head_width
    group_size = queries.shape[1] // width
    scale = head_width ** (-0.5)
    qmat = queries.reshape(item_count, key_value_count, group_size, head_width)
    kmat = keys.reshape(item_count, key_value_count, head_width)
    value_matrix = values.reshape(item_count, key_value_count, head_width)
    upper_matrix = upstream.reshape(item_count, key_value_count, group_size, head_width)
    scores = jnp.einsum("yxru,oxu->xryo", qmat, kmat, preferred_element_type=jnp.float32) * scale
    place = jnp.arange(item_count, dtype=jnp.int32)
    allowed = (place[None, :] <= place[:, None]) & (place[None, :] >= (place - positions)[:, None])
    scores = jnp.where(allowed, scores, jnp.float32(-1e30))
    top = jnp.max(scores, axis=-1, keepdims=True)
    expo = jnp.exp(scores - top)
    probs = expo / jnp.sum(expo, axis=-1, keepdims=True)
    slope_values = jnp.einsum(
        "yxru,oxu->xryo", upper_matrix, value_matrix, preferred_element_type=jnp.float32
    )
    inner = jnp.sum(probs * slope_values, axis=-1, keepdims=True)
    dscores = (probs * (slope_values - inner) * scale).astype(jnp.bfloat16)
    grad_rot = jnp.einsum("kgts,tkgd->skd", dscores, qmat, preferred_element_type=jnp.float32)
    return grad_rot.reshape(item_count, width)


def per_device(tokens, queries, values, upstream, key_weight, positions):
    node_count = lax.axis_size("node")
    local_count = lax.axis_size("local")
    shard_rows = key_weight.shape[0]
    item_count = tokens.shape[0]
    model_width = tokens.shape[1]
    head_width = HEAD_SIZE
    columns = tokens
    raw_keys = jnp.dot(
        columns,
        lax.all_gather(key_weight, ("node", "local"), axis=0, tiled=True),
        preferred_element_type=jnp.float32,
    )
    quarter = lax.all_gather(key_weight, "node", axis=0, tiled=True)
    cosine, sine_part = angle_tables(positions, head_width)
    keys = rotate(raw_keys, cosine, sine_part, head_width, 1.0).astype(jnp.bfloat16)
    grad_rot = attend_back(queries, keys, values, upstream, positions, head_width)
    grad_keys = rotate(grad_rot, cosine, sine_part, head_width, -1.0).astype(jnp.bfloat16)
    mixed = lax.dot_general(
        grad_keys,
        lax.all_gather(quarter, "local", axis=0, tiled=True),
        (((1,), (1,)), ((), ())),
        preferred_element_type=jnp.float32,
    ).astype(jnp.bfloat16)
    grad_tokens = mixed.reshape(item_count, local_count, node_count, shard_rows)
    grad_tokens = jnp.transpose(grad_tokens, (0, 2, 1, 3)).reshape(item_count, model_width)
    columns = tokens
    sectioned = lax.psum_scatter(
        lax.dot_general(
            columns, grad_keys, (((0,), (0,)), ((), ())), preferred_element_type=jnp.float32
        ),
        "node",
        scatter_dimension=0,
        tiled=True,
    )
    grad_weight = lax.psum_scatter(sectioned, "local", scatter_dimension=0, tiled=True)
    return (grad_tokens, grad_weight)


def solution(mesh):
    placed = (
        P(("node", "local"), None),
        P(("node", "local"), None),
        P(("node", "local"), None),
        P(("node", "local"), None),
        P(("node", "local"), None),
        P(("node", "local")),
    )
    return jax.shard_map(
        per_device,
        mesh=mesh,
        in_specs=placed,
        out_specs=(P(("node", "local"), None), P(("node", "local"), None)),
        check_vma=False,
    )
```

profile of v0, /device:TPU:0, one launch (start us, length us, event | category | flops | bytes accessed | tf_op | source)
XLA Modules:
  0.0 305.9 jit_solution(15466371574386477604)
XLA Ops:
  7.2 0.7 all-gather.4.cloned.1.call-update
  8.0 0.7 all-gather.6.cloned.1.call-update
  8.7 0.8 iota_subtract_fusion
  9.5 4.1 %copy.38 = bf16[256,4096]{0,1:T(8,128)(2,1)} copy(bf16[256,4096]{1,0:T(8,128)(2,1)} %param.7) | data formatting | bytes 4194304 | tf_op jit(solution)/shard_map/reshape | solution.py:35
  13.6 0.7 fusion.25
  14.3 3.4 %copy.39 = bf16[32,8,32,128]{3,2,1,0:T(8,128)(2,1)} copy(bf16[32,8,32,128]{3,1,2,0:T(8,128)(2,1)} %bitcast.68) | data formatting | bytes 4194304
  17.7 0.5 broadcast_multiply_fusion
  18.3 6.2 %fusion.15 = f32[4,256,256,8]{2,1,3,0:T(8,128)} fusion(bf16[256,4,8,128]{3,2,1,0:T(8,128)(2,1)} %bitcast.62, bf16[256,4,128,1]{2,1,0,3:T(4,128)(2,1)S(1)} %bitcast.69), kind=kOutput, calls=%fused_computation.20 | convolution fusion | flops 536870912 | bytes 10747904 | tf_op jit(solution)/shard_map/yxru,oxu->xryo/dot_general | solution.py:46
  24.5 51.4 %all-gather.4.cloned.1.call-done = bf16[4096,512]{1,0:T(8,128)(2,1)} async-done(((bf16[128,512]{1,0:T(8,128)(2,1)}), bf16[4096,512]{1,0:T(8,128)(2,1)}) %all-gather.4.cloned.1.call-update) | async-done | bytes 4194320 | tf_op jit(solution)/shard_map/all_gather | solution.py:65
  75.8 3.4 %fusion.32 = f32[256,512]{1,0:T(8,128)S(1)} fusion(bf16[256,4096]{1,0:T(8,128)(2,1)S(1)} %copy-done, bf16[4096,512]{1,0:T(8,128)(2,1)} %all-gather.4.cloned.1.call-done), kind=kOutput, calls=%fused_computation.48 | convolution fusion | flops 1073741824 | bytes 6815744 | tf_op jit(solution)/shard_map/dot_general | solution.py:63
  80.0 1.1 copy-done.1
  81.1 4.5 %fusion.21 = f32[4,256,256,8]{2,1,3,0:T(8,128)} fusion(bf16[256,4,8,128]{0,3,2,1:T(8,128)(2,1)S(1)} %bitcast.65, bf16[256,4,64]{2,0,1:T(8,128)(2,1)S(1)} %get-tuple-element.7, bf16[256,4,64]{2,0,1:T(8,128)(2,1)S(1)} %get-tuple-element.6), kind=kOutput, calls=%fused_computation.29 | convolution fusion | flops 537395200 | bytes 10747904 | tf_op jit(solution)/shard_map/yxru,oxu->xryo/dot_general | solution.py:39
  85.6 12.9 %fusion.13 = f32[4,8,256,256]{2,3,1,0:T(8,128)} fusion(f32[4,256,256,8]{2,1,3,0:T(8,128)} %fusion.21, pred[256,256]{0,1:T(8,128)(4,1)} %fusion.25), kind=kOutput, calls=%fused_computation.18 | output fusion | flops 12599806 | bytes 16842752 | tf_op jit(solution)/shard_map/div | solution.py:45
  98.5 13.5 %fusion.18 = f32[256,4,128]{2,0,1:T(8,128)S(1)} fusion(bf16[256,4,8,128]{0,3,2,1:T(8,128)(2,1)} %bitcast.64, f32[4,8,256,256]{2,3,1,0:T(8,128)} %fusion.13, f32[4,256,256,8]{2,1,3,0:T(8,128)} %fusion.15), kind=kOutput, calls=%fused_computation.23 | convolution fusion | flops 547365120 | bytes 19398656 | tf_op jit(solution)/shard_map/kgts,tkgd->skd/dot_general | solution.py:51
  112.5 4.7 %convolution_bitcast_fusion = f32[4096,512]{0,1:T(8,128)} fusion(bf16[256,512]{0,1:T(8,128)(2,1)S(1)} %bitcast.66, bf16[256,4096]{1,0:T(8,128)(2,1)S(1)} %copy-done), kind=kOutput, calls=%fused_computation.10 | convolution fusion | flops 1073741824 | bytes 10747904 | tf_op jit(solution)/shard_map/dot_general | solution.py:83
  117.3 0.5 all-gather.8.cloned.1.call-update
  117.9 69.5 %reduce-scatter.3.cloned.1.call-done = f32[512,512]{0,1:T(8,128)} async-done(((f32[4096,512]{0,1:T(8,128)}), f32[512,512]{0,1:T(8,128)}) %reduce-scatter.3.cloned.1.call-update) | async-done | bytes 1048592 | tf_op jit(solution)/shard_map/reduce_scatter | solution.py:82
  187.4 82.3 %all-gather.8.cloned.1.call-done = bf16[4096,512]{1,0:T(8,128)(2,1)} async-done(((bf16[1024,512]{1,0:T(8,128)(2,1)}), bf16[4096,512]{1,0:T(8,128)(2,1)}) %all-gather.8.cloned.1.call-update) | async-done | bytes 4194320 | tf_op jit(solution)/shard_map/all_gather | solution.py:75
  269.6 3.5 %fusion.17 = bf16[32,8,32,128]{3,1,2,0:T(8,128)(2,1)S(1)} fusion(bf16[256,512]{0,1:T(8,128)(2,1)S(1)} %bitcast.67, bf16[4096,512]{1,0:T(8,128)(2,1)} %all-gather.8.cloned.1.call-done), kind=kOutput, calls=%fused_computation.22 | convolution fusion | flops 1074790400 | bytes 6553600 | tf_op jit(solution)/shard_map/dot_general | solution.py:73
  273.1 0.5 copy.40
  273.6 2.4 copy.27
  276.0 4.5 %reshape.87 = bf16[256,4096]{1,0:T(8,128)(2,1)} reshape(bf16[256,8,4,128]{3,2,1,0:T(4,128)(2,1)} %copy.27) | data formatting | bytes 4194304 | tf_op jit(solution)/shard_map/reshape | solution.py:80
  280.5 17.1 %reduce-scatter.5.cloned.1.call-done = f32[128,512]{0,1:T(8,128)} async-done(((f32[512,512]{0,1:T(8,128)}), f32[128,512]{0,1:T(8,128)}) %reduce-scatter.5.cloned.1.call-update) | async-done | bytes 262160 | tf_op jit(solution)/shard_map/reduce_scatter | solution.py:90
  297.6 1.8 copy.28
  (21 shorter events, 1.5 us)
Async XLA Ops:
  7.2 68.7 %copy-start = (bf16[256,4096]{1,0:T(8,128)(2,1)S(1)}, bf16[256,4096]{1,0:T(8,128)(2,1)}, u32[]{:S(2)}) copy-start(bf16[256,4096]{1,0:T(8,128)(2,1)} %param.6) | copy-start | bytes 6291460
  7.2 68.7 %all-gather.4.cloned.1.call-start = ((), (), s32[]{:S(2)}) async-start(), calls=%async_computation.2 | async-start | bytes 4325376 | tf_op jit(solution)/shard_map/all_gather | solution.py:65
  7.9 109.4 %all-gather.6.cloned.1.call-start = ((), (), s32[]{:S(2)}) async-start(), calls=%async_computation.3 | async-start | bytes 1179648 | tf_op jit(solution)/shard_map/all_gather | solution.py:68
  8.7 178.7 %reduce-scatter.3.cloned.1.call-start = ((), (), s32[]{:S(2)}) async-start(), calls=%async_computation.5 | async-start | bytes 9437184 | tf_op jit(solution)/shard_map/reduce_scatter | solution.py:82
  9.5 8.2 %copy-start.2 = (bf16[256,512]{1,0:T(8,128)(2,1)S(1)}, bf16[256,512]{1,0:T(8,128)(2,1)}, u32[]{:S(2)}) copy-start(bf16[256,512]{1,0:T(8,128)(2,1)} %param.8) | copy-start | bytes 786436
  79.5 1.6 copy-start.1
  117.2 152.4 %all-gather.8.cloned.1.call-start = ((), (), s32[]{:S(2)}) async-start(), calls=%async_computation.4 | async-start | bytes 5242880 | tf_op jit(solution)/shard_map/all_gather | solution.py:75
  117.8 179.8 %reduce-scatter.5.cloned.1.call-start = ((), (), s32[]{:S(2)}) async-start(), calls=%async_computation.6 | async-start | bytes 1310720 | tf_op jit(solution)/shard_map/reduce_scatter | solution.py:90
Sparse Core Ops, SparseCore 0:
  11.0 64.7 all-gather.3
  77.7 22.0 all-gather.5
  117.4 69.9 reduce-scatter.2
  188.9 80.7 all-gather.7
  271.9 25.6 reduce-scatter.4
where the time goes:
time: 306 us
  waiting for transfers between devices  222 us (73%)
  matrix products  35.8 us (12%)
  local copies, waits for them, and re-layouts  18.5 us (6%)
  other arithmetic  15.4 us (5%)
  between operations  13.9 us (5%)
    all_gather x1, waiting for transfers between devices, per_device(): lax.all_gather(quarter, 'local', axis=0, tiled=True)  82.3 us
    reduce_scatter x1, waiting for transfers between devices, per_device(): lax.psum_scatter(lax.dot_general(columns, grad_keys, (((0,), (0,)), ((),...  69.5 us
    all_gather x1, waiting for transfers between devices, per_device(): lax.all_gather(key_weight, ('node', 'local'), axis=0, tiled=True)  51.4 us
    reduce_scatter x1, waiting for transfers between devices, per_device(): lax.psum_scatter(sectioned, 'local', scatter_dimension=0, tiled=True)  17.1 us
    dot_general x1, matrix products, attend_back(): jnp.einsum('kgts,tkgd->skd', dscores, qmat, preferred_element_type=jnp.fl...  13.5 us
    div x1, other arithmetic, attend_back(): probs = expo / jnp.sum(expo, axis=-1, keepdims=True)  12.9 us
    unnamed x9, local copies, waits for them, and re-layouts  6.77 us
    dot_general x1, matrix products, attend_back(): jnp.einsum('yxru,oxu->xryo', upper_matrix, value_matrix, preferred_elemen...  6.18 us
  transfers between devices with their start and end apart: 5, of which 4 were waited for; matrix products, arithmetic and copies ran while one was open for 22% of the time, Pallas kernels for 0%

commit v1 on v0

v1 whole, which is shorter than its diff:
```python
import functools
import math

import jax
import jax.numpy as jnp
from jax import lax
from jax.experimental import pallas as pl
from jax.experimental.pallas import tpu as pltpu
from jax.sharding import PartitionSpec as P

HEAD_SIZE = 128
PAIRS = 2
BATCH = 4
HBM = pl.BlockSpec(memory_space=pltpu.HBM)
VMEM = pl.BlockSpec(memory_space=pltpu.VMEM)
SMEM = pl.BlockSpec(memory_space=pltpu.SMEM)
LAST_LAST = (((1,), (1,)), ((), ()))
MIB = 1 << 20
CHEAP = pl.CostEstimate(flops=1, bytes_accessed=1, transcendentals=0)
PARAMS = pltpu.CompilerParams(vmem_limit_bytes=12 * MIB)


def angle_tables(positions):
    half = HEAD_SIZE // 2
    freq = jnp.exp(
        -(jnp.arange(half, dtype=jnp.float32) * 2.0 / HEAD_SIZE) * jnp.log(jnp.float32(1000000.0))
    )
    angle = positions.astype(jnp.float32)[:, None] * freq[None, :]
    cosine, sine = jnp.cos(angle), jnp.sin(angle)
    return jnp.concatenate([cosine, cosine], axis=1), jnp.concatenate([-sine, sine], axis=1)


def flip(x, axis, mask, size):
    return lax.ppermute(x, axis, [(i, i ^ mask) for i in range(size)])


def line_kernel(place_ref, *refs):
    shards, out_ref = refs[:-1], refs[-1]
    for k, shard in enumerate(shards):
        out_ref[place_ref[1] ^ k] = shard[...]


def put_in_line(place, shards):
    return pl.pallas_call(
        line_kernel,
        out_shape=jax.ShapeDtypeStruct((len(shards), *shards[0].shape), shards[0].dtype),
        in_specs=[SMEM] + [VMEM] * len(shards),
        out_specs=VMEM,
        compiler_params=PARAMS,
        cost_estimate=CHEAP,
        name="line",
    )(place, *shards)


def turn_kernel(*refs):
    half = len(refs) // 2
    for x_ref, out_ref in zip(refs[:half], refs[half:]):
        for chip in range(x_ref.shape[0]):
            out_ref[chip] = x_ref[chip].T


def turn(*arrays):
    chips, count, block = arrays[0].shape
    return pl.pallas_call(
        turn_kernel,
        out_shape=[jax.ShapeDtypeStruct((chips, block, count), arrays[0].dtype)] * len(arrays),
        in_specs=[VMEM] * len(arrays),
        out_specs=[VMEM] * len(arrays),
        compiler_params=PARAMS,
        cost_estimate=CHEAP,
        name="turn",
    )(*arrays)


def raw_kernel(place_ref, x_ref, *refs):
    pieces, out_ref = refs[:-1], refs[-1]
    chip = place_ref[0] // 2
    total = jnp.zeros(out_ref.shape, jnp.float32)
    for m, piece in enumerate(pieces):
        locs, rows, width = piece.shape
        total += jnp.dot(
            x_ref[chip ^ m], piece[...].reshape(locs * rows, width), preferred_element_type=jnp.float32
        )
    out_ref[...] = total


def raw_terms(place, x, pieces):
    chips, count, block = x.shape
    width = pieces[0].shape[2]
    return pl.pallas_call(
        raw_kernel,
        out_shape=jax.ShapeDtypeStruct((count, width), jnp.float32),
        in_specs=[SMEM] + [VMEM] * (1 + len(pieces)),
        out_specs=VMEM,
        compiler_params=PARAMS,
        cost_estimate=CHEAP,
        name="raw",
    )(place, x, *pieces)


def attend_kernel(pair, heads, group, pos_ref, cos_ref, sin_ref, raw_ref, raw2_ref, q, v, u, gk_ref):
    width = heads * HEAD_SIZE
    count = gk_ref.shape[0]
    block = count // 2
    biases = []
    for part in range(2):
        span = block * (part + 1)
        j = lax.broadcasted_iota(jnp.int32, (span, block), 0)
        i = lax.broadcasted_iota(jnp.int32, (span, block), 1) + part * block
        low = i - pos_ref[:, part * block : (part + 1) * block]
        biases.append(jnp.where((j <= i) & (j >= low), jnp.float32(0.0), jnp.float32(-1e30)))
    raw = raw_ref[...] + raw2_ref[...]
    cosine, sine = cos_ref[...], sin_ref[...]
    scale = HEAD_SIZE ** (-0.5)
    slope = scale * math.log2(math.e)
    for head in range(heads):
        cols = slice(head * HEAD_SIZE, (head + 1) * HEAD_SIZE)
        mine = raw[:, cols]
        keys = (mine * cosine + pltpu.roll(mine, HEAD_SIZE // 2, 1) * sine).astype(jnp.bfloat16)
        vals = v[:, pair * width + head * HEAD_SIZE : pair * width + (head + 1) * HEAD_SIZE]
        totals = []
        for part in range(2):
            span = block * (part + 1)
            lines = slice(part * block, (part + 1) * block)
            bias = jnp.concatenate([biases[part]] * BATCH, axis=1)
            total = jnp.zeros((span, HEAD_SIZE), jnp.float32)
            for g in range(0, group, BATCH):
                starts = [((pair * heads + head) * group + g + t) * HEAD_SIZE for t in range(BATCH)]
                at = [slice(start, start + HEAD_SIZE) for start in starts]
                qs = jnp.concatenate([q[lines, a] for a in at], axis=0)
                us = jnp.concatenate([u[lines, a] for a in at], axis=0)
                scores = lax.dot_general(keys[:span], qs, LAST_LAST, preferred_element_type=jnp.float32) + bias
                slopes = lax.dot_general(vals[:span], us, LAST_LAST, preferred_element_type=jnp.float32)
                top = jnp.max(scores, axis=0, keepdims=True)
                expo = jnp.exp2((scores - top) * slope)
                inv = 1.0 / jnp.sum(expo, axis=0, keepdims=True)
                inner = jnp.sum(expo * slopes, axis=0, keepdims=True) * inv
                dscores = (expo * (slopes - inner) * (inv * scale)).astype(jnp.bfloat16)
                total += jnp.dot(dscores, qs, preferred_element_type=jnp.float32)
            totals.append(total)
        drot = jnp.concatenate([totals[0] + totals[1][:block], totals[1][block:]], axis=0)
        gk_ref[:, cols] = (drot * cosine - pltpu.roll(drot, HEAD_SIZE // 2, 1) * sine).astype(jnp.bfloat16)


def attend(pair, group, pos, cosine, sine, raw, raw2, q, v, u):
    count, width = raw.shape
    q, v, u = (pltpu.with_memory_space_constraint(x, pltpu.VMEM) for x in (q, v, u))
    return pl.pallas_call(
        functools.partial(attend_kernel, pair, width // HEAD_SIZE, group),
        out_shape=jax.ShapeDtypeStruct((count, width), jnp.bfloat16),
        in_specs=[VMEM] * 8,
        out_specs=VMEM,
        compiler_params=PARAMS,
        cost_estimate=CHEAP,
        name="attend",
    )(pos, cosine, sine, raw, raw2, q, v, u)


def terms_kernel(place_ref, own_ref, sib_ref, gk_ref, sib_gk_ref, *outs):
    chip = place_ref[0] // 2
    gk, sib_gk = gk_ref[...], sib_gk_ref[...]

    def term(m, dtype):
        total = jnp.dot(own_ref[chip ^ m], gk, preferred_element_type=jnp.float32)
        total += jnp.dot(sib_ref[chip ^ m], sib_gk, preferred_element_type=jnp.float32)
        return total.reshape(outs[0].shape).astype(dtype)

    for m in list(range(1, len(outs))) + [0]:
        outs[m][...] = term(m, outs[m].dtype)


def terms(locs, place, own, sib, gk, sib_gk):
    chips, block, count = own.shape
    width = gk.shape[1]
    outs = [
        jax.ShapeDtypeStruct((locs, block // locs, width), jnp.bfloat16 if m else jnp.float32) for m in range(chips)
    ]
    return pl.pallas_call(
        terms_kernel,
        out_shape=outs,
        in_specs=[SMEM] + [VMEM] * 4,
        out_specs=[VMEM] * len(outs),
        compiler_params=PARAMS,
        cost_estimate=CHEAP,
        name="terms",
    )(place, own, sib, gk, sib_gk)


def add_kernel(locs, place_ref, *refs):
    parts, keep, sends = refs[:-locs], refs[-locs], refs[len(refs) - locs + 1 :]
    for k in range(locs):
        total = parts[0][place_ref[1] ^ k]
        for part in parts[1:]:
            total += part[place_ref[1] ^ k].astype(jnp.float32)
        if k == 0:
            keep[...] = total
        else:
            sends[k - 1][...] = total.astype(jnp.bfloat16)


def add(locs, place, parts):
    rows, width = parts[0].shape[1:]
    return pl.pallas_call(
        functools.partial(add_kernel, locs),
        out_shape=[jax.ShapeDtypeStruct((rows, width), jnp.float32 if k == 0 else jnp.bfloat16) for k in range(locs)],
        in_specs=[SMEM] + [VMEM] * len(parts),
        out_specs=[VMEM] * locs,
        compiler_params=PARAMS,
        cost_estimate=CHEAP,
        name="add",
    )(place, *parts)


def back_kernel(pairs, parts, place_ref, *refs):
    grads, pieces, outs = [g[...] for g in refs[:pairs]], refs[pairs : len(refs) - parts], refs[len(refs) - parts :]
    chips = len(pieces) // pairs
    for m in range(chips):
        total = None
        for pair in range(pairs):
            piece = pieces[pair * chips + m]
            locs, rows, width = piece.shape
            term = lax.dot_general(
                grads[pair], piece[...].reshape(locs * rows, width), LAST_LAST, preferred_element_type=jnp.float32
            )
            total = term if total is None else total + term
        outs[m * parts // chips][m % (chips // parts)] = total.astype(jnp.bfloat16)


def back(place, gks, pieces, block, parts):
    pairs, chips = len(pieces), len(pieces[0])
    return pl.pallas_call(
        functools.partial(back_kernel, pairs, parts),
        out_shape=[jax.ShapeDtypeStruct((chips // parts, gks[0].shape[0], block), jnp.bfloat16)] * parts,
        in_specs=[SMEM] + [VMEM] * (pairs + pairs * chips),
        out_specs=[VMEM] * parts,
        compiler_params=PARAMS,
        cost_estimate=CHEAP,
        name="back",
    )(place, *gks, *[piece for group in pieces for piece in group])


def columns_of(array, chip, core, block):
    return array.at[:, pl.ds(pl.multiple_of((2 * chip + core) * block, block), block)]


def cut_kernel(place_ref, x_hbm, sib_hbm, own_ref, sib_ref, sems):
    core = place_ref[0] & 1
    copies = []
    for chip in range(own_ref.shape[0]):
        for n, (array, out_ref) in enumerate(((x_hbm, own_ref), (sib_hbm, sib_ref))):
            source = columns_of(array, chip, core, own_ref.shape[2])
            copies.append(pltpu.make_async_copy(source, out_ref.at[chip], sems.at[2 * chip + n]))
    for copy in copies:
        copy.start()
    for copy in copies:
        copy.wait()


def cut(place, x, sib_x, chips, block, core):
    count = x.shape[0]
    if block % 128:
        blocks = [array.reshape(count, chips, 2, block).transpose(2, 1, 0, 3) for array in (x, sib_x)]
        return [lax.dynamic_index_in_dim(array, core, axis=0, keepdims=False) for array in blocks]
    return pl.pallas_call(
        cut_kernel,
        out_shape=[jax.ShapeDtypeStruct((chips, count, block), x.dtype)] * 2,
        in_specs=[SMEM, HBM, HBM],
        out_specs=[VMEM] * 2,
        scratch_shapes=[pltpu.SemaphoreType.DMA((2 * chips,))],
        compiler_params=PARAMS,
        cost_estimate=CHEAP,
        name="cut",
    )(place, pin(x), pin(sib_x))


def join_kernel(place_ref, *refs):
    parts, out_hbm, sems = refs[:-2], refs[-2], refs[-1]
    chip, core = place_ref[0] // 2, place_ref[0] & 1
    block = parts[0].shape[2]
    copies = []
    for n, same in enumerate((parts[:1], parts[1:])):
        m = 0
        for part in same:
            for i in range(part.shape[0]):
                target = columns_of(out_hbm, chip ^ m, core ^ n, block)
                copies.append(pltpu.make_async_copy(part.at[i], target, sems.at[2 * m + n]))
                m += 1
    for copy in copies:
        copy.start()
    for copy in copies:
        copy.wait()


def join(place, own, sib, core):
    (own,) = own
    chips, count, block = own.shape
    if block % 128:
        sib = jnp.concatenate(sib)
        both = jnp.where(core == 0, jnp.stack([own, sib]), jnp.stack([sib, own]))
        both = jnp.take(both, jnp.arange(chips) ^ (place[0] // 2), axis=1)
        return both.transpose(2, 1, 0, 3).reshape(count, 2 * chips * block)
    return pl.pallas_call(
        join_kernel,
        out_shape=jax.ShapeDtypeStruct((count, 2 * chips * block), own.dtype),
        in_specs=[SMEM] + [VMEM] * (1 + len(sib)),
        out_specs=HBM,
        scratch_shapes=[pltpu.SemaphoreType.DMA((2 * chips,))],
        compiler_params=PARAMS,
        cost_estimate=CHEAP,
        name="join",
    )(place, own, *sib)


def pin(x):
    return pltpu.with_memory_space_constraint(x, pltpu.HBM)


def after(x, *others):
    return lax.optimization_barrier((x, *others))[0]


def per_device(tokens, queries, values, upstream, key_weight, positions):
    nodes, locs = lax.axis_size("node"), lax.axis_size("local")
    chips = nodes // 2
    key_width = key_weight.shape[1]
    count, model = tokens.shape
    block = model // nodes
    group = queries.shape[1] // key_width
    width = key_width // PAIRS
    node, local = lax.axis_index("node"), lax.axis_index("local")
    core = node & 1
    place = jnp.stack([node, local]).astype(jnp.int32)

    def swap(x):
        return flip(x, "node", 1, nodes)

    sib_tokens = swap(tokens)
    lines, pieces = [], []
    for pair in range(PAIRS):
        own = after(key_weight, lines[-1]) if pair else key_weight
        own = own[:, pair * width : (pair + 1) * width]
        shards = [own] + [flip(own, "local", k, locs) for k in range(1, locs)]
        if pair:
            shards[0] = after(shards[0], own_x, *pieces[-1][1:])
        lines.append(put_in_line(place, shards))
        pieces.append([lines[-1]] + [flip(lines[-1], "node", 2 * m, nodes) for m in range(1, chips)])
        if not pair:
            own_x, sib_x = cut(place, tokens, after(sib_tokens, lines[0]), chips, block, core)
    own_turned, sib_turned = turn(own_x, sib_x)

    cosine, sine = angle_tables(positions)
    pos = positions.reshape(1, count)

    def raw_of(pair, *others):
        sib, own = (after(x, *others) if others else x for x in (sib_x, own_x))
        return raw_terms(place, own, pieces[pair]), swap(raw_terms(place, sib, pieces[pair]))

    gks, sib_gks, sums = [], [], []
    raw, sib_raw = raw_of(0)
    for pair in range(PAIRS):
        last = pair == PAIRS - 1
        if not last:
            raw = after(raw, *pieces[pair + 1][1:3])
        gk = attend(pair, group, pos, cosine, sine, raw, sib_raw, queries, values, upstream)
        gks.append(gk)
        sib_gks.append(swap(gk))
        if not last:
            raw, sib_raw = raw_of(pair + 1, gk)
            gk = after(gk, raw, sib_raw)
        else:
            gk = after(gk, sums[-1][0])
        outs = list(terms(locs, place, own_turned, sib_turned, gk, sib_gks[-1]))
        parts = outs[:1] + [flip(outs[m], "node", 2 * m, nodes) for m in range(1, chips)]
        sums.append(add(locs, place, parts))
        raw = after(raw, outs[0])

    theirs = [swap(part) for part in back(place, sib_gks, pieces, block, 2)]
    mine = back(place, [after(gks[0], outs[0])] + gks[1:], pieces, block, 1)
    grad_tokens = join(place, mine, theirs, core)
    keeps = []
    for total, *sends in sums:
        got = [flip(part, "local", k + 1, locs) for k, part in enumerate(sends)]
        if keeps:
            total = after(total, grad_tokens)
        for part in got:
            total = total + part.astype(jnp.float32)
        keeps.append(total)
    return grad_tokens, jnp.concatenate(keeps, axis=1)


def solution(mesh):
    split = P(("node", "local"), None)
    return jax.shard_map(
        per_device,
        mesh=mesh,
        in_specs=(split, split, split, split, split, P(("node", "local"))),
        out_specs=(split, split),
        check_vma=False,
    )
```

time: 306 us -> 94.2 us (0.31)
  waiting for transfers between devices: 222 us -> 31.4 us
  matrix products: 35.8 us -> 0 us
  starting transfers between devices: 0.19 us -> 35.7 us
  Pallas kernels: 0 us -> 21.9 us
  local copies, waits for them, and re-layouts: 18.5 us -> 1.71 us
  other arithmetic: 15.4 us -> 2.23 us
  between operations: 13.9 us -> 0.97 us
    all_gather x3 -> x0, waiting for transfers between devices: 134 us -> none  [the longest x1 82.3 us: per_device(): lax.all_gather(quarter, 'local', axis=0, tiled=True)]
    reduce_scatter x2 -> x0, waiting for transfers between devices: 86.6 us -> none  [the longest x1 69.5 us: per_device(): lax.psum_scatter(lax.dot_general(columns, grad_keys, (((0,), (0,)), ((),...]
    dot_general x6 -> x0, matrix products: 35.8 us -> none  [the longest x1 13.5 us: attend_back(): jnp.einsum('kgts,tkgd->skd', dscores, qmat, preferred_element_type=jnp.fl...]
    ppermute x0 -> x31, starting transfers between devices: none -> 35.7 us  [flip(): return lax.ppermute(x, axis, [(i, i ^ mask) for i in range(size)])]
    ppermute x0 -> x31, waiting for transfers between devices: none -> 31.4 us  [flip(): return lax.ppermute(x, axis, [(i, i ^ mask) for i in range(size)])]
    pallas_call x0 -> x17, Pallas kernels: none -> 21.9 us  [the longest x2 5.79 us: attend(): pl.pallas_call(functools.partial(attend_kernel, pair, width // HEAD_SIZE,...]
    div x1 -> x0, other arithmetic: 12.9 us -> none  [attend_back(): probs = expo / jnp.sum(expo, axis=-1, keepdims=True)]
    reshape x4 -> x0, local copies, waits for them, and re-layouts: 8.84 us -> none  [the longest x1 4.48 us: per_device(): jnp.transpose(grad_tokens, (0, 2, 1, 3)).reshape(item_count, model_width)]
  transfers between devices with their start and end apart: 5 -> 31, of which waited for: 4 -> 15; matrix products, arithmetic and copies ran while one was open for 22% -> 3% of each run, Pallas kernels for 0% -> 19%
where the time goes in v1:
time: 94.2 us; the launch traced here: 93.9 us
  starting transfers between devices  35.7 us (38%)
  waiting for transfers between devices  31.4 us (33%)
  Pallas kernels  21.9 us (23%)
  other arithmetic  2.23 us (2%)
  local copies, waits for them, and re-layouts  1.71 us (2%)
  between operations  0.97 us (1%)
    ppermute x31, starting transfers between devices, flip(): return lax.ppermute(x, axis, [(i, i ^ mask) for i in range(size)])  35.7 us
    ppermute x31, waiting for transfers between devices, flip(): return lax.ppermute(x, axis, [(i, i ^ mask) for i in range(size)])  31.4 us
    pallas_call x2, Pallas kernels, attend(): pl.pallas_call(functools.partial(attend_kernel, pair, width // HEAD_SIZE,...  5.79 us
    pallas_call x4, Pallas kernels, raw_terms(): pl.pallas_call(raw_kernel, out_shape=jax.ShapeDtypeStruct((count, width),...  3.91 us
    pallas_call x2, Pallas kernels, back(): pl.pallas_call(functools.partial(back_kernel, pairs, parts), out_shape=[j...  2.56 us
    pallas_call x2, Pallas kernels, terms(): pl.pallas_call(terms_kernel, out_shape=outs, in_specs=[SMEM] + [VMEM] * 4...  2.5 us
    pallas_call x1, Pallas kernels, cut(): pl.pallas_call(cut_kernel, out_shape=[jax.ShapeDtypeStruct((chips, count,...  2.18 us
    pallas_call x1, Pallas kernels, join(): pl.pallas_call(join_kernel, out_shape=jax.ShapeDtypeStruct((count, 2 * ch...  1.93 us
  transfers between devices with their start and end apart: 31, of which 15 were waited for; matrix products, arithmetic and copies ran while one was open for 3% of the time, Pallas kernels for 19%

profile of v1, /device:TPU:0, one launch (start us, length us, event | category | flops | bytes accessed | tf_op | source)
XLA Modules:
  0.0 93.9 jit_solution(2946677652187082313)
XLA Ops:
  2.0 2.6 %collective-permute-start.1 = (bf16[128,256]{1,0:T(8,128)(2,1)S(1)}, bf16[128,256]{1,0:T(8,128)(2,1)S(1)}, u32[]{:S(2)}, u32[]{:S(2)}) collective-permute-start(bf16[128,256]{1,0:T(8,128)(2,1)S(1)} %slice.6.refs_0_), channel_id=1, source_target_pairs={{0,1},{1,0},{2,3},{3,2},{4,5},{5,4},{6,7},{7,6},{8,9},{9,8},{10,11... | collective-permute-start | bytes 196616 | tf_op jit(solution)/shard_map/ppermute | solution.py:34
  4.6 2.6 %collective-permute-start.2 = (bf16[128,256]{1,0:T(8,128)(2,1)S(1)}, bf16[128,256]{1,0:T(8,128)(2,1)S(1)}, u32[]{:S(2)}, u32[]{:S(2)}) collective-permute-start(bf16[128,256]{1,0:T(8,128)(2,1)S(1)} %slice.6.refs_0_), channel_id=1, source_target_pairs={{0,2},{1,3},{2,0},{3,1},{4,6},{5,7},{6,4},{7,5},{8,10},{9,11},{10,... | collective-permute-start | bytes 196616 | tf_op jit(solution)/shard_map/ppermute | solution.py:34
  7.3 4.2 %collective-permute-done.2.refs_2_ = bf16[128,256]{1,0:T(8,128)(2,1)S(1)} collective-permute-done((bf16[128,256]{1,0:T(8,128)(2,1)S(1)}, bf16[128,256]{1,0:T(8,128)(2,1)S(1)}, u32[]{:S(2)}, u32[]{:S(2)}) %collective-permute-start.2) | collective-permute-done | bytes 65568 | tf_op jit(solution)/shard_map/ppermute | solution.py:34
  11.6 1.7 %collective-permute-done.3.refs_3_ = bf16[128,256]{1,0:T(8,128)(2,1)S(1)} collective-permute-done((bf16[128,256]{1,0:T(8,128)(2,1)S(1)}, bf16[128,256]{1,0:T(8,128)(2,1)S(1)}, u32[]{:S(2)}, u32[]{:S(2)}) %collective-permute-start.3) | collective-permute-done | bytes 65568 | tf_op jit(solution)/shard_map/ppermute | solution.py:34
  13.9 1.6 %collective-permute-start.4 = (bf16[4,128,256]{2,1,0:T(8,128)(2,1)S(1)}, bf16[4,128,256]{2,1,0:T(8,128)(2,1)S(1)}, u32[]{:S(2)}, u32[]{:S(2)}) collective-permute-start(bf16[4,128,256]{2,1,0:T(8,128)(2,1)S(1)} %line.2.refs_0_.refs_2_), channel_id=1, source_target_pairs={{0,8},{4,12},{8,0},{12,4},{16,24},{20,28},{24,16},{28,20},{1,9},{5... | collective-permute-start | bytes 786440 | tf_op jit(solution)/shard_map/ppermute | solution.py:34
  20.2 3.0 %collective-permute-done.4.refs_1_.refs_3_ = bf16[4,128,256]{2,1,0:T(8,128)(2,1)S(1)} collective-permute-done((bf16[4,128,256]{2,1,0:T(8,128)(2,1)S(1)}, bf16[4,128,256]{2,1,0:T(8,128)(2,1)S(1)}, u32[]{:S(2)}, u32[]{:S(2)}) %collective-permute-start.4) | collective-permute-done | bytes 262176 | tf_op jit(solution)/shard_map/ppermute | solution.py:34
  23.2 2.2 %collective-permute-start.8 = (bf16[128,256]{1,0:T(8,128)(2,1)S(1)}, bf16[128,256]{1,0:T(8,128)(2,1)S(1)}, u32[]{:S(2)}, u32[]{:S(2)}) collective-permute-start(bf16[128,256]{1,0:T(8,128)(2,1)S(1)} %slice.7.refs_0_), channel_id=1, source_target_pairs={{0,2},{1,3},{2,0},{3,1},{4,6},{5,7},{6,4},{7,5},{8,10},{9,11},{10,... | collective-permute-start | bytes 196616 | tf_op jit(solution)/shard_map/ppermute | solution.py:34
  26.7 2.2 %cut.1 = (bf16[4,256,512]{2,1,0:T(8,128)(2,1)S(1)}, bf16[4,256,512]{2,1,0:T(8,128)(2,1)S(1)}) custom-call(s32[2]{0:T(128)S(1)} %pad_add_fusion.place_ref, bf16[256,4096]{1,0:T(8,128)(2,1)} %x_hbm.1, bf16[256,4096]{1,0:T(8,128)(2,1)} %copy-done.4), custom_call_target="tpu_custom_call" | custom-call | flops 1 | bytes 1 | tf_op jit(solution)/shard_map/cut/pallas_call | solution.py:264
  29.0 2.4 %collective-permute-done.9.refs_3_ = bf16[128,256]{1,0:T(8,128)(2,1)S(1)} collective-permute-done((bf16[128,256]{1,0:T(8,128)(2,1)S(1)}, bf16[128,256]{1,0:T(8,128)(2,1)S(1)}, u32[]{:S(2)}, u32[]{:S(2)}) %collective-permute-start.9) | collective-permute-done | bytes 65568 | tf_op jit(solution)/shard_map/ppermute | solution.py:34
  32.0 1.6 %collective-permute-start.10 = (bf16[4,128,256]{2,1,0:T(8,128)(2,1)S(1)}, bf16[4,128,256]{2,1,0:T(8,128)(2,1)S(1)}, u32[]{:S(2)}, u32[]{:S(2)}) collective-permute-start(bf16[4,128,256]{2,1,0:T(8,128)(2,1)S(1)} %line.3.refs_0_.refs_6_), channel_id=1, source_target_pairs={{0,8},{4,12},{8,0},{12,4},{16,24},{20,28},{24,16},{28,20},{1,9},{5... | collective-permute-start | bytes 786440 | tf_op jit(solution)/shard_map/ppermute | solution.py:34
  38.4 4.3 %collective-permute-done.11.refs_2_.refs_8_ = bf16[4,128,256]{2,1,0:T(8,128)(2,1)S(1)} collective-permute-done((bf16[4,128,256]{2,1,0:T(8,128)(2,1)S(1)}, bf16[4,128,256]{2,1,0:T(8,128)(2,1)S(1)}, u32[]{:S(2)}, u32[]{:S(2)}) %collective-permute-start.11) | collective-permute-done | bytes 262176 | tf_op jit(solution)/shard_map/ppermute | solution.py:34
  42.8 2.9 %attend.2.gk_ref.refs_0_ = bf16[256,256]{1,0:T(8,128)(2,1)S(1)} custom-call(s32[1,256]{1,0:T(1,128)S(1)} %bitcast.3, f32[256,128]{1,0:T(8,128)S(1)} %get-tuple-element.71.cos_ref, f32[256,128]{1,0:T(8,128)S(1)} %get-tuple-element.72.sin_ref, f32[256,256]{1,0:T(8,128)S(1)} %raw.4.raw_ref, f32[256,256]{1,0:T(8,128)S(1)} %collective-permute-done.12.raw2_ref, ...), custom_call_target="tpu_custom_call" | custom-call | flops 1 | bytes 1 | tf_op jit(solution)/shard_map/attend/pallas_call | solution.py:148
  50.2 2.0 %collective-permute-start.17 = (bf16[4,128,256]{2,1,0:T(8,128)(2,1)S(1)}, bf16[4,128,256]{2,1,0:T(8,128)(2,1)S(1)}, u32[]{:S(2)}, u32[]{:S(2)}) collective-permute-start(bf16[4,128,256]{2,1,0:T(8,128)(2,1)S(1)} %get-tuple-element.49), channel_id=1, source_target_pairs={{0,16},{4,20},{8,24},{12,28},{16,0},{20,4},{24,8},{28,12},{1,17},{... | collective-permute-start | bytes 786440 | tf_op jit(solution)/shard_map/ppermute | solution.py:34
  53.7 2.9 %attend.3.gk_ref.refs_1_ = bf16[256,256]{1,0:T(8,128)(2,1)S(1)} custom-call(s32[1,256]{1,0:T(1,128)S(1)} %bitcast.4, f32[256,128]{1,0:T(8,128)S(1)} %get-tuple-element.71.cos_ref, f32[256,128]{1,0:T(8,128)S(1)} %get-tuple-element.72.sin_ref, f32[256,256]{1,0:T(8,128)S(1)} %raw.6.raw_ref, f32[256,256]{1,0:T(8,128)S(1)} %collective-permute-done.14.raw2_ref, ...), custom_call_target="tpu_custom_call" | custom-call | flops 1 | bytes 1 | tf_op jit(solution)/shard_map/attend/pallas_call | solution.py:148
  56.6 2.7 %collective-permute-done.16.refs_1_ = bf16[4,128,256]{2,1,0:T(8,128)(2,1)S(1)} collective-permute-done((bf16[4,128,256]{2,1,0:T(8,128)(2,1)S(1)}, bf16[4,128,256]{2,1,0:T(8,128)(2,1)S(1)}, u32[]{:S(2)}, u32[]{:S(2)}) %collective-permute-start.16) | collective-permute-done | bytes 262176 | tf_op jit(solution)/shard_map/ppermute | solution.py:34
  59.3 4.1 %collective-permute-done.17.refs_2_ = bf16[4,128,256]{2,1,0:T(8,128)(2,1)S(1)} collective-permute-done((bf16[4,128,256]{2,1,0:T(8,128)(2,1)S(1)}, bf16[4,128,256]{2,1,0:T(8,128)(2,1)S(1)}, u32[]{:S(2)}, u32[]{:S(2)}) %collective-permute-start.17) | collective-permute-done | bytes 262176 | tf_op jit(solution)/shard_map/ppermute | solution.py:34
  63.4 1.6 %collective-permute-done.18.refs_3_ = bf16[4,128,256]{2,1,0:T(8,128)(2,1)S(1)} collective-permute-done((bf16[4,128,256]{2,1,0:T(8,128)(2,1)S(1)}, bf16[4,128,256]{2,1,0:T(8,128)(2,1)S(1)}, u32[]{:S(2)}, u32[]{:S(2)}) %collective-permute-start.18) | collective-permute-done | bytes 262176 | tf_op jit(solution)/shard_map/ppermute | solution.py:34
  67.8 1.5 %collective-permute-start.26 = (bf16[4,128,256]{2,1,0:T(8,128)(2,1)S(1)}, bf16[4,128,256]{2,1,0:T(8,128)(2,1)S(1)}, u32[]{:S(2)}, u32[]{:S(2)}) collective-permute-start(bf16[4,128,256]{2,1,0:T(8,128)(2,1)S(1)} %get-tuple-element.61), channel_id=1, source_target_pairs={{0,16},{4,20},{8,24},{12,28},{16,0},{20,4},{24,8},{28,12},{1,17},{... | collective-permute-start | bytes 786440 | tf_op jit(solution)/shard_map/ppermute | solution.py:34
  72.4 3.9 %collective-permute-done.25.refs_1_ = bf16[4,128,256]{2,1,0:T(8,128)(2,1)S(1)} collective-permute-done((bf16[4,128,256]{2,1,0:T(8,128)(2,1)S(1)}, bf16[4,128,256]{2,1,0:T(8,128)(2,1)S(1)}, u32[]{:S(2)}, u32[]{:S(2)}) %collective-permute-start.25) | collective-permute-done | bytes 262176 | tf_op jit(solution)/shard_map/ppermute | solution.py:34
  76.3 1.8 %collective-permute-start.24 = (bf16[128,256]{1,0:T(8,128)(2,1)S(1)}, bf16[128,256]{1,0:T(8,128)(2,1)S(1)}, u32[]{:S(2)}, u32[]{:S(2)}) collective-permute-start(bf16[128,256]{1,0:T(8,128)(2,1)S(1)} %get-tuple-element.59), channel_id=1, source_target_pairs={{0,3},{1,2},{2,1},{3,0},{4,7},{5,6},{6,5},{7,4},{8,11},{9,10},{10,... | collective-permute-start | bytes 196616 | tf_op jit(solution)/shard_map/ppermute | solution.py:34
  78.1 2.3 %collective-permute-done.26.refs_2_ = bf16[4,128,256]{2,1,0:T(8,128)(2,1)S(1)} collective-permute-done((bf16[4,128,256]{2,1,0:T(8,128)(2,1)S(1)}, bf16[4,128,256]{2,1,0:T(8,128)(2,1)S(1)}, u32[]{:S(2)}, u32[]{:S(2)}) %collective-permute-start.26) | collective-permute-done | bytes 262176 | tf_op jit(solution)/shard_map/ppermute | solution.py:34
  84.8 2.0 %collective-permute-start.30 = (bf16[128,256]{1,0:T(8,128)(2,1)S(1)}, bf16[128,256]{1,0:T(8,128)(2,1)S(1)}, u32[]{:S(2)}, u32[]{:S(2)}) collective-permute-start(bf16[128,256]{1,0:T(8,128)(2,1)S(1)} %get-tuple-element.67), channel_id=1, source_target_pairs={{0,3},{1,2},{2,1},{3,0},{4,7},{5,6},{6,5},{7,4},{8,11},{9,10},{10,... | collective-permute-start | bytes 196616 | tf_op jit(solution)/shard_map/ppermute | solution.py:34
  87.6 2.9 %collective-permute-start.28 = (bf16[128,256]{1,0:T(8,128)(2,1)S(1)}, bf16[128,256]{1,0:T(8,128)(2,1)S(1)}, u32[]{:S(2)}, u32[]{:S(2)}) collective-permute-start(bf16[128,256]{1,0:T(8,128)(2,1)S(1)} %get-tuple-element.65), channel_id=1, source_target_pairs={{0,1},{1,0},{2,3},{3,2},{4,5},{5,4},{6,7},{7,6},{8,9},{9,8},{10,11... | collective-permute-start | bytes 196616 | tf_op jit(solution)/shard_map/ppermute | solution.py:34
  90.6 1.9 %join.1 = bf16[256,4096]{1,0:T(8,128)(2,1)} custom-call(s32[2]{0:T(128)S(1)} %pad_add_fusion.place_ref, bf16[4,256,512]{2,1,0:T(8,128)(2,1)S(1)} %back.2.refs_0_, bf16[2,256,512]{2,1,0:T(8,128)(2,1)S(1)} %collective-permute-done.20.refs_1_, bf16[2,256,512]{2,1,0:T(8,128)(2,1)S(1)} %collective-permute-done.21.refs_2_), custom_call_target="tpu_custom_call" | custom-call | flops 1 | bytes 1 | tf_op jit(solution)/shard_map/join/pallas_call | solution.py:302
  (75 shorter events, 31.9 us)
Async XLA Ops:
  0.6 24.7 %collective-permute-start = (bf16[256,4096]{1,0:T(8,128)(2,1)}, bf16[256,4096]{1,0:T(8,128)(2,1)S(1)}, u32[]{:S(2)}, u32[]{:S(2)}) collective-permute-start(bf16[256,4096]{1,0:T(8,128)(2,1)} %x_hbm.1), channel_id=1, source_target_pairs={{0,4},{4,0},{8,12},{12,8},{16,20},{20,16},{24,28},{28,24},{1,5},{5... | collective-permute-start | bytes 6291464 | tf_op jit(solution)/shard_map/ppermute | solution.py:34
  4.6 7.0 %collective-permute-start.2 = (bf16[128,256]{1,0:T(8,128)(2,1)S(1)}, bf16[128,256]{1,0:T(8,128)(2,1)S(1)}, u32[]{:S(2)}, u32[]{:S(2)}) collective-permute-start(bf16[128,256]{1,0:T(8,128)(2,1)S(1)} %slice.6.refs_0_), channel_id=1, source_target_pairs={{0,2},{1,3},{2,0},{3,1},{4,6},{5,7},{6,4},{7,5},{8,10},{9,11},{10,... | collective-permute-start | bytes 196616 | tf_op jit(solution)/shard_map/ppermute | solution.py:34
  7.2 6.1 %collective-permute-start.3 = (bf16[128,256]{1,0:T(8,128)(2,1)S(1)}, bf16[128,256]{1,0:T(8,128)(2,1)S(1)}, u32[]{:S(2)}, u32[]{:S(2)}) collective-permute-start(bf16[128,256]{1,0:T(8,128)(2,1)S(1)} %slice.6.refs_0_), channel_id=1, source_target_pairs={{0,3},{1,2},{2,1},{3,0},{4,7},{5,6},{6,5},{7,4},{8,11},{9,10},{10,... | collective-permute-start | bytes 196616 | tf_op jit(solution)/shard_map/ppermute | solution.py:34
  13.9 9.3 %collective-permute-start.4 = (bf16[4,128,256]{2,1,0:T(8,128)(2,1)S(1)}, bf16[4,128,256]{2,1,0:T(8,128)(2,1)S(1)}, u32[]{:S(2)}, u32[]{:S(2)}) collective-permute-start(bf16[4,128,256]{2,1,0:T(8,128)(2,1)S(1)} %line.2.refs_0_.refs_2_), channel_id=1, source_target_pairs={{0,8},{4,12},{8,0},{12,4},{16,24},{20,28},{24,16},{28,20},{1,9},{5... | collective-permute-start | bytes 786440 | tf_op jit(solution)/shard_map/ppermute | solution.py:34
  15.4 13.5 %collective-permute-start.5 = (bf16[4,128,256]{2,1,0:T(8,128)(2,1)S(1)}, bf16[4,128,256]{2,1,0:T(8,128)(2,1)S(1)}, u32[]{:S(2)}, u32[]{:S(2)}) collective-permute-start(bf16[4,128,256]{2,1,0:T(8,128)(2,1)S(1)} %line.2.refs_0_.refs_2_), channel_id=1, source_target_pairs={{0,16},{4,20},{8,24},{12,28},{16,0},{20,4},{24,8},{28,12},{1,17},{... | collective-permute-start | bytes 786440 | tf_op jit(solution)/shard_map/ppermute | solution.py:34
  16.9 12.0 %collective-permute-start.6 = (bf16[4,128,256]{2,1,0:T(8,128)(2,1)S(1)}, bf16[4,128,256]{2,1,0:T(8,128)(2,1)S(1)}, u32[]{:S(2)}, u32[]{:S(2)}) collective-permute-start(bf16[4,128,256]{2,1,0:T(8,128)(2,1)S(1)} %line.2.refs_0_.refs_2_), channel_id=1, source_target_pairs={{0,24},{4,28},{8,16},{12,20},{16,8},{20,12},{24,0},{28,4},{1,25},{... | collective-permute-start | bytes 786440 | tf_op jit(solution)/shard_map/ppermute | solution.py:34
  18.9 10.0 %collective-permute-start.7 = (bf16[128,256]{1,0:T(8,128)(2,1)S(1)}, bf16[128,256]{1,0:T(8,128)(2,1)S(1)}, u32[]{:S(2)}, u32[]{:S(2)}) collective-permute-start(bf16[128,256]{1,0:T(8,128)(2,1)S(1)} %slice.7.refs_0_), channel_id=1, source_target_pairs={{0,1},{1,0},{2,3},{3,2},{4,5},{5,4},{6,7},{7,6},{8,9},{9,8},{10,11... | collective-permute-start | bytes 196616 | tf_op jit(solution)/shard_map/ppermute | solution.py:34
  32.0 6.4 %collective-permute-start.10 = (bf16[4,128,256]{2,1,0:T(8,128)(2,1)S(1)}, bf16[4,128,256]{2,1,0:T(8,128)(2,1)S(1)}, u32[]{:S(2)}, u32[]{:S(2)}) collective-permute-start(bf16[4,128,256]{2,1,0:T(8,128)(2,1)S(1)} %line.3.refs_0_.refs_6_), channel_id=1, source_target_pairs={{0,8},{4,12},{8,0},{12,4},{16,24},{20,28},{24,16},{28,20},{1,9},{5... | collective-permute-start | bytes 786440 | tf_op jit(solution)/shard_map/ppermute | solution.py:34
  33.6 9.2 %collective-permute-start.11 = (bf16[4,128,256]{2,1,0:T(8,128)(2,1)S(1)}, bf16[4,128,256]{2,1,0:T(8,128)(2,1)S(1)}, u32[]{:S(2)}, u32[]{:S(2)}) collective-permute-start(bf16[4,128,256]{2,1,0:T(8,128)(2,1)S(1)} %line.3.refs_0_.refs_6_), channel_id=1, source_target_pairs={{0,16},{4,20},{8,24},{12,28},{16,0},{20,4},{24,8},{28,12},{1,17},{... | collective-permute-start | bytes 786440 | tf_op jit(solution)/shard_map/ppermute | solution.py:34
  35.1 10.6 %collective-permute-start.13 = (bf16[4,128,256]{2,1,0:T(8,128)(2,1)S(1)}, bf16[4,128,256]{2,1,0:T(8,128)(2,1)S(1)}, u32[]{:S(2)}, u32[]{:S(2)}) collective-permute-start(bf16[4,128,256]{2,1,0:T(8,128)(2,1)S(1)} %line.3.refs_0_.refs_6_), channel_id=1, source_target_pairs={{0,24},{4,28},{8,16},{12,20},{16,8},{20,12},{24,0},{28,4},{1,25},{... | collective-permute-start | bytes 786440 | tf_op jit(solution)/shard_map/ppermute | solution.py:34
  36.6 6.2 %collective-permute-start.12 = (f32[256,256]{1,0:T(8,128)S(1)}, f32[256,256]{1,0:T(8,128)S(1)}, u32[]{:S(2)}, u32[]{:S(2)}) collective-permute-start(f32[256,256]{1,0:T(8,128)S(1)} %raw.5), channel_id=1, source_target_pairs={{0,4},{4,0},{8,12},{12,8},{16,20},{20,16},{24,28},{28,24},{1,5},{5... | collective-permute-start | bytes 786440 | tf_op jit(solution)/shard_map/ppermute | solution.py:34
  50.1 9.2 %collective-permute-start.16 = (bf16[4,128,256]{2,1,0:T(8,128)(2,1)S(1)}, bf16[4,128,256]{2,1,0:T(8,128)(2,1)S(1)}, u32[]{:S(2)}, u32[]{:S(2)}) collective-permute-start(bf16[4,128,256]{2,1,0:T(8,128)(2,1)S(1)} %get-tuple-element.48), channel_id=1, source_target_pairs={{0,8},{4,12},{8,0},{12,4},{16,24},{20,28},{24,16},{28,20},{1,9},{5... | collective-permute-start | bytes 786440 | tf_op jit(solution)/shard_map/ppermute | solution.py:34
  50.2 13.2 %collective-permute-start.17 = (bf16[4,128,256]{2,1,0:T(8,128)(2,1)S(1)}, bf16[4,128,256]{2,1,0:T(8,128)(2,1)S(1)}, u32[]{:S(2)}, u32[]{:S(2)}) collective-permute-start(bf16[4,128,256]{2,1,0:T(8,128)(2,1)S(1)} %get-tuple-element.49), channel_id=1, source_target_pairs={{0,16},{4,20},{8,24},{12,28},{16,0},{20,4},{24,8},{28,12},{1,17},{... | collective-permute-start | bytes 786440 | tf_op jit(solution)/shard_map/ppermute | solution.py:34
  52.2 12.8 %collective-permute-start.18 = (bf16[4,128,256]{2,1,0:T(8,128)(2,1)S(1)}, bf16[4,128,256]{2,1,0:T(8,128)(2,1)S(1)}, u32[]{:S(2)}, u32[]{:S(2)}) collective-permute-start(bf16[4,128,256]{2,1,0:T(8,128)(2,1)S(1)} %get-tuple-element.50), channel_id=1, source_target_pairs={{0,24},{4,28},{8,16},{12,20},{16,8},{20,12},{24,0},{28,4},{1,25},{... | collective-permute-start | bytes 786440 | tf_op jit(solution)/shard_map/ppermute | solution.py:34
  56.6 9.2 %collective-permute-start.19 = (bf16[256,256]{1,0:T(8,128)(2,1)S(1)}, bf16[256,256]{1,0:T(8,128)(2,1)S(1)}, u32[]{:S(2)}, u32[]{:S(2)}) collective-permute-start(bf16[256,256]{1,0:T(8,128)(2,1)S(1)} %attend.3.gk_ref.refs_1_), channel_id=1, source_target_pairs={{0,4},{4,0},{8,12},{12,8},{16,20},{20,16},{24,28},{28,24},{1,5},{5... | collective-permute-start | bytes 393224 | tf_op jit(solution)/shard_map/ppermute | solution.py:34
  67.0 9.3 %collective-permute-start.25 = (bf16[4,128,256]{2,1,0:T(8,128)(2,1)S(1)}, bf16[4,128,256]{2,1,0:T(8,128)(2,1)S(1)}, u32[]{:S(2)}, u32[]{:S(2)}) collective-permute-start(bf16[4,128,256]{2,1,0:T(8,128)(2,1)S(1)} %get-tuple-element.60), channel_id=1, source_target_pairs={{0,8},{4,12},{8,0},{12,4},{16,24},{20,28},{24,16},{28,20},{1,9},{5... | collective-permute-start | bytes 786440 | tf_op jit(solution)/shard_map/ppermute | solution.py:34
  67.8 12.6 %collective-permute-start.26 = (bf16[4,128,256]{2,1,0:T(8,128)(2,1)S(1)}, bf16[4,128,256]{2,1,0:T(8,128)(2,1)S(1)}, u32[]{:S(2)}, u32[]{:S(2)}) collective-permute-start(bf16[4,128,256]{2,1,0:T(8,128)(2,1)S(1)} %get-tuple-element.61), channel_id=1, source_target_pairs={{0,16},{4,20},{8,24},{12,28},{16,0},{20,4},{24,8},{28,12},{1,17},{... | collective-permute-start | bytes 786440 | tf_op jit(solution)/shard_map/ppermute | solution.py:34
  69.3 12.1 %collective-permute-start.27 = (bf16[4,128,256]{2,1,0:T(8,128)(2,1)S(1)}, bf16[4,128,256]{2,1,0:T(8,128)(2,1)S(1)}, u32[]{:S(2)}, u32[]{:S(2)}) collective-permute-start(bf16[4,128,256]{2,1,0:T(8,128)(2,1)S(1)} %get-tuple-element.62), channel_id=1, source_target_pairs={{0,24},{4,28},{8,16},{12,20},{16,8},{20,12},{24,0},{28,4},{1,25},{... | collective-permute-start | bytes 786440 | tf_op jit(solution)/shard_map/ppermute | solution.py:34
  71.8 18.7 %collective-permute-start.20 = (bf16[2,256,512]{2,1,0:T(8,128)(2,1)S(1)}, bf16[2,256,512]{2,1,0:T(8,128)(2,1)S(1)}, u32[]{:S(2)}, u32[]{:S(2)}) collective-permute-start(bf16[2,256,512]{2,1,0:T(8,128)(2,1)S(1)} %get-tuple-element.55), channel_id=1, source_target_pairs={{0,4},{4,0},{8,12},{12,8},{16,20},{20,16},{24,28},{28,24},{1,5},{5... | collective-permute-start | bytes 1572872 | tf_op jit(solution)/shard_map/ppermute | solution.py:34
  71.9 18.7 %collective-permute-start.21 = (bf16[2,256,512]{2,1,0:T(8,128)(2,1)S(1)}, bf16[2,256,512]{2,1,0:T(8,128)(2,1)S(1)}, u32[]{:S(2)}, u32[]{:S(2)}) collective-permute-start(bf16[2,256,512]{2,1,0:T(8,128)(2,1)S(1)} %get-tuple-element.56), channel_id=1, source_target_pairs={{0,4},{4,0},{8,12},{12,8},{16,20},{20,16},{24,28},{28,24},{1,5},{5... | collective-permute-start | bytes 1572872 | tf_op jit(solution)/shard_map/ppermute | solution.py:34
  76.3 8.5 %collective-permute-start.24 = (bf16[128,256]{1,0:T(8,128)(2,1)S(1)}, bf16[128,256]{1,0:T(8,128)(2,1)S(1)}, u32[]{:S(2)}, u32[]{:S(2)}) collective-permute-start(bf16[128,256]{1,0:T(8,128)(2,1)S(1)} %get-tuple-element.59), channel_id=1, source_target_pairs={{0,3},{1,2},{2,1},{3,0},{4,7},{5,6},{6,5},{7,4},{8,11},{9,10},{10,... | collective-permute-start | bytes 196616 | tf_op jit(solution)/shard_map/ppermute | solution.py:34
  80.4 6.4 %collective-permute-start.23 = (bf16[128,256]{1,0:T(8,128)(2,1)S(1)}, bf16[128,256]{1,0:T(8,128)(2,1)S(1)}, u32[]{:S(2)}, u32[]{:S(2)}) collective-permute-start(bf16[128,256]{1,0:T(8,128)(2,1)S(1)} %get-tuple-element.58), channel_id=1, source_target_pairs={{0,2},{1,3},{2,0},{3,1},{4,6},{5,7},{6,4},{7,5},{8,10},{9,11},{10,... | collective-permute-start | bytes 196616 | tf_op jit(solution)/shard_map/ppermute | solution.py:34
  81.5 6.1 %collective-permute-start.22 = (bf16[128,256]{1,0:T(8,128)(2,1)S(1)}, bf16[128,256]{1,0:T(8,128)(2,1)S(1)}, u32[]{:S(2)}, u32[]{:S(2)}) collective-permute-start(bf16[128,256]{1,0:T(8,128)(2,1)S(1)} %get-tuple-element.57), channel_id=1, source_target_pairs={{0,1},{1,0},{2,3},{3,2},{4,5},{5,4},{6,7},{7,6},{8,9},{9,8},{10,11... | collective-permute-start | bytes 196616 | tf_op jit(solution)/shard_map/ppermute | solution.py:34
  84.8 7.7 %collective-permute-start.30 = (bf16[128,256]{1,0:T(8,128)(2,1)S(1)}, bf16[128,256]{1,0:T(8,128)(2,1)S(1)}, u32[]{:S(2)}, u32[]{:S(2)}) collective-permute-start(bf16[128,256]{1,0:T(8,128)(2,1)S(1)} %get-tuple-element.67), channel_id=1, source_target_pairs={{0,3},{1,2},{2,1},{3,0},{4,7},{5,6},{6,5},{7,4},{8,11},{9,10},{10,... | collective-permute-start | bytes 196616 | tf_op jit(solution)/shard_map/ppermute | solution.py:34
  (12 other events, 60.2 us)

commit v2 on v1

--- a/solution.py
+++ b/solution.py
@@ -34,16 +34,18 @@
     return lax.ppermute(x, axis, [(i, i ^ mask) for i in range(size)])
 
 
-def line_kernel(place_ref, *refs):
+def line_kernel(pair, place_ref, *refs):
     shards, out_ref = refs[:-1], refs[-1]
+    width = out_ref.shape[2]
     for k, shard in enumerate(shards):
-        out_ref[place_ref[1] ^ k] = shard[...]
-
-
-def put_in_line(place, shards):
-    return pl.pallas_call(
-        line_kernel,
-        out_shape=jax.ShapeDtypeStruct((len(shards), *shards[0].shape), shards[0].dtype),
+        first = pair * width if shard.shape[1] > width else 0
+        out_ref[place_ref[1] ^ k] = shard[:, first : first + width]
+
+
+def put_in_line(pair, width, place, shards):
+    return pl.pallas_call(
+        functools.partial(line_kernel, pair),
+        out_shape=jax.ShapeDtypeStruct((len(shards), shards[0].shape[0], width), shards[0].dtype),
         in_specs=[SMEM] + [VMEM] * len(shards),
         out_specs=VMEM,
         compiler_params=PARAMS,
@@ -73,15 +75,17 @@
 
 
 def raw_kernel(place_ref, x_ref, *refs):
-    pieces, out_ref = refs[:-1], refs[-1]
+    pieces, outs = refs[: x_ref.shape[0]], refs[x_ref.shape[0] :]
     chip = place_ref[0] // 2
-    total = jnp.zeros(out_ref.shape, jnp.float32)
+    total = jnp.zeros((x_ref.shape[1], pieces[0].shape[2]), jnp.float32)
     for m, piece in enumerate(pieces):
         locs, rows, width = piece.shape
         total += jnp.dot(
             x_ref[chip ^ m], piece[...].reshape(locs * rows, width), preferred_element_type=jnp.float32
         )
-    out_ref[...] = total
+    width = outs[0].shape[1]
+    for n, out_ref in enumerate(outs):
+        out_ref[...] = total[:, n * width : (n + 1) * width]
 
 
 def raw_terms(place, x, pieces):
@@ -89,16 +93,17 @@
     width = pieces[0].shape[2]
     return pl.pallas_call(
         raw_kernel,
-        out_shape=jax.ShapeDtypeStruct((count, width), jnp.float32),
+        out_shape=[jax.ShapeDtypeStruct((count, HEAD_SIZE), jnp.float32)] * (width // HEAD_SIZE),
         in_specs=[SMEM] + [VMEM] * (1 + len(pieces)),
-        out_specs=VMEM,
+        out_specs=[VMEM] * (width // HEAD_SIZE),
         compiler_params=PARAMS,
         cost_estimate=CHEAP,
         name="raw",
     )(place, x, *pieces)
 
 
-def attend_kernel(pair, heads, group, pos_ref, cos_ref, sin_ref, raw_ref, raw2_ref, q, v, u, gk_ref):
+def attend_kernel(pair, heads, group, pos_ref, cos_ref, sin_ref, *refs):
+    raws, sib_raws, (q, v, u, gk_ref) = refs[:heads], refs[heads : 2 * heads], refs[2 * heads :]
     width = heads * HEAD_SIZE
     count = gk_ref.shape[0]
     block = count // 2
@@ -109,13 +114,12 @@
         i = lax.broadcasted_iota(jnp.int32, (span, block), 1) + part * block
         low = i - pos_ref[:, part * block : (part + 1) * block]
         biases.append(jnp.where((j <= i) & (j >= low), jnp.float32(0.0), jnp.float32(-1e30)))
-    raw = raw_ref[...] + raw2_ref[...]
     cosine, sine = cos_ref[...], sin_ref[...]
     scale = HEAD_SIZE ** (-0.5)
     slope = scale * math.log2(math.e)
     for head in range(heads):
         cols = slice(head * HEAD_SIZE, (head + 1) * HEAD_SIZE)
-        mine = raw[:, cols]
+        mine = raws[head][...] + sib_raws[head][...]
         keys = (mine * cosine + pltpu.roll(mine, HEAD_SIZE // 2, 1) * sine).astype(jnp.bfloat16)
         vals = v[:, pair * width + head * HEAD_SIZE : pair * width + (head + 1) * HEAD_SIZE]
         totals = []
@@ -142,18 +146,18 @@
         gk_ref[:, cols] = (drot * cosine - pltpu.roll(drot, HEAD_SIZE // 2, 1) * sine).astype(jnp.bfloat16)
 
 
-def attend(pair, group, pos, cosine, sine, raw, raw2, q, v, u):
-    count, width = raw.shape
+def attend(pair, group, pos, cosine, sine, raw, sib_raw, q, v, u):
+    heads, (count, width) = len(raw), raw[0].shape
     q, v, u = (pltpu.with_memory_space_constraint(x, pltpu.VMEM) for x in (q, v, u))
     return pl.pallas_call(
-        functools.partial(attend_kernel, pair, width // HEAD_SIZE, group),
-        out_shape=jax.ShapeDtypeStruct((count, width), jnp.bfloat16),
-        in_specs=[VMEM] * 8,
+        functools.partial(attend_kernel, pair, heads, group),
+        out_shape=jax.ShapeDtypeStruct((count, heads * width), jnp.bfloat16),
+        in_specs=[VMEM] * (6 + 2 * heads),
         out_specs=VMEM,
         compiler_params=PARAMS,
         cost_estimate=CHEAP,
         name="attend",
-    )(pos, cosine, sine, raw, raw2, q, v, u)
+    )(pos, cosine, sine, *raw, *sib_raw, q, v, u)
 
 
 def terms_kernel(place_ref, own_ref, sib_ref, gk_ref, sib_gk_ref, *outs):
@@ -186,29 +190,34 @@
     )(place, own, sib, gk, sib_gk)
 
 
-def add_kernel(locs, place_ref, *refs):
-    parts, keep, sends = refs[:-locs], refs[-locs], refs[len(refs) - locs + 1 :]
+def add_kernel(locs, count, place_ref, *refs):
+    parts, earlier, outs = refs[:count], refs[count:-locs], refs[-locs:]
+    width = outs[0].shape[1]
     for k in range(locs):
         total = parts[0][place_ref[1] ^ k]
         for part in parts[1:]:
             total += part[place_ref[1] ^ k].astype(jnp.float32)
-        if k == 0:
-            keep[...] = total
+        if k == 1:
+            for n, ref in enumerate(earlier):
+                outs[k][:, n * width : (n + 1) * width] = ref[...]
+            outs[k][:, len(earlier) * width :] = total.astype(jnp.bfloat16)
         else:
-            sends[k - 1][...] = total.astype(jnp.bfloat16)
-
-
-def add(locs, place, parts):
+            outs[k][...] = total.astype(outs[k].dtype)
+
+
+def add(locs, place, parts, earlier):
     rows, width = parts[0].shape[1:]
-    return pl.pallas_call(
-        functools.partial(add_kernel, locs),
-        out_shape=[jax.ShapeDtypeStruct((rows, width), jnp.float32 if k == 0 else jnp.bfloat16) for k in range(locs)],
-        in_specs=[SMEM] + [VMEM] * len(parts),
+    outs = [jax.ShapeDtypeStruct((rows, width), jnp.bfloat16 if k else jnp.float32) for k in range(locs)]
+    outs[1] = jax.ShapeDtypeStruct((rows, (len(earlier) + 1) * width), jnp.bfloat16)
+    return pl.pallas_call(
+        functools.partial(add_kernel, locs, len(parts)),
+        out_shape=outs,
+        in_specs=[SMEM] + [VMEM] * (len(parts) + len(earlier)),
         out_specs=[VMEM] * locs,
         compiler_params=PARAMS,
         cost_estimate=CHEAP,
         name="add",
-    )(place, *parts)
+    )(place, *parts, *earlier)
 
 
 def back_kernel(pairs, parts, place_ref, *refs):
@@ -264,13 +273,13 @@
     return pl.pallas_call(
         cut_kernel,
         out_shape=[jax.ShapeDtypeStruct((chips, count, block), x.dtype)] * 2,
-        in_specs=[SMEM, HBM, HBM],
+        in_specs=[SMEM, HBM, pl.BlockSpec(memory_space=pl.ANY)],
         out_specs=[VMEM] * 2,
         scratch_shapes=[pltpu.SemaphoreType.DMA((2 * chips,))],
         compiler_params=PARAMS,
         cost_estimate=CHEAP,
         name="cut",
-    )(place, pin(x), pin(sib_x))
+    )(place, pin(x), sib_x)
 
 
 def join_kernel(place_ref, *refs):
@@ -336,13 +345,14 @@
 
     sib_tokens = swap(tokens)
     lines, pieces = [], []
+    beside = flip(key_weight, "local", 1, locs)
     for pair in range(PAIRS):
-        own = after(key_weight, lines[-1]) if pair else key_weight
-        own = own[:, pair * width : (pair + 1) * width]
-        shards = [own] + [flip(own, "local", k, locs) for k in range(1, locs)]
+        own = key_weight[:, pair * width : (pair + 1) * width]
         if pair:
-            shards[0] = after(shards[0], own_x, *pieces[-1][1:])
-        lines.append(put_in_line(place, shards))
+            own = after(own, lines[-1])
+        shards = [own, beside] + [flip(own, "local", k, locs) for k in range(2, locs)]
+        shards[-1] = after(shards[-1], *((own_x, pieces[-1][-1]) if pair else (sib_tokens,)))
+        lines.append(put_in_line(pair, width, place, shards))
         pieces.append([lines[-1]] + [flip(lines[-1], "node", 2 * m, nodes) for m in range(1, chips)])
         if not pair:
             own_x, sib_x = cut(place, tokens, after(sib_tokens, lines[0]), chips, block, core)
@@ -353,39 +363,37 @@
 
     def raw_of(pair, *others):
         sib, own = (after(x, *others) if others else x for x in (sib_x, own_x))
-        return raw_terms(place, own, pieces[pair]), swap(raw_terms(place, sib, pieces[pair]))
-
-    gks, sib_gks, sums = [], [], []
+        return raw_terms(place, own, pieces[pair]), [swap(part) for part in raw_terms(place, sib, pieces[pair])]
+
+    gks, sib_gks, sums, got = [], [], [], []
     raw, sib_raw = raw_of(0)
     for pair in range(PAIRS):
-        last = pair == PAIRS - 1
-        if not last:
-            raw = after(raw, *pieces[pair + 1][1:3])
         gk = attend(pair, group, pos, cosine, sine, raw, sib_raw, queries, values, upstream)
         gks.append(gk)
         sib_gks.append(swap(gk))
-        if not last:
-            raw, sib_raw = raw_of(pair + 1, gk)
-            gk = after(gk, raw, sib_raw)
-        else:
+        if pair:
             gk = after(gk, sums[-1][0])
         outs = list(terms(locs, place, own_turned, sib_turned, gk, sib_gks[-1]))
+        if pair + 1 < PAIRS:
+            raw, sib_raw = raw_of(pair + 1, outs[0])
         parts = outs[:1] + [flip(outs[m], "node", 2 * m, nodes) for m in range(1, chips)]
-        sums.append(add(locs, place, parts))
-        raw = after(raw, outs[0])
-
-    theirs = [swap(part) for part in back(place, sib_gks, pieces, block, 2)]
-    mine = back(place, [after(gks[0], outs[0])] + gks[1:], pieces, block, 1)
-    grad_tokens = join(place, mine, theirs, core)
-    keeps = []
-    for total, *sends in sums:
-        got = [flip(part, "local", k + 1, locs) for k, part in enumerate(sends)]
-        if keeps:
-            total = after(total, grad_tokens)
-        for part in got:
-            total = total + part.astype(jnp.float32)
-        keeps.append(total)
-    return grad_tokens, jnp.concatenate(keeps, axis=1)
+        if pair + 1 == PAIRS:
+            theirs, mine = (
+                back(place, [after(grads[0], outs[0])] + grads[1:], pieces, block, 1)[0] for grads in (sib_gks, gks)
+            )
+            parts[0] = after(parts[0], theirs, mine, *got[-1])
+        sums.append(add(locs, place, parts, [part[1] for part in sums]))
+        got.append([flip(sums[-1][k], "local", k, locs) for k in range(2, locs)])
+
+    beside = flip(sums[-1][1], "local", 1, locs)
+    grad_tokens = join(place, [mine], [swap(after(theirs, sums[-1][0]))], core)
+    wholes = []
+    for pair, parts in enumerate(got):
+        whole = after(sums[pair][0], grad_tokens)
+        for part in [beside[:, pair * width : (pair + 1) * width]] + parts:
+            whole = whole + part.astype(jnp.float32)
+        wholes.append(whole)
+    return grad_tokens, jnp.concatenate(wholes, axis=1)
 
 
 def solution(mesh):

time: 94.2 us -> 82.5 us (0.88)
  waiting for transfers between devices: 31.4 us -> 25.8 us
  starting transfers between devices: 35.7 us -> 30.9 us
    ppermute x31 -> x30, waiting for transfers between devices: 31.4 us -> 25.8 us  [flip(): return lax.ppermute(x, axis, [(i, i ^ mask) for i in range(size)])]
    ppermute x31 -> x30, starting transfers between devices: 35.7 us -> 30.9 us  [flip(): return lax.ppermute(x, axis, [(i, i ^ mask) for i in range(size)])]
  transfers between devices with their start and end apart: 31 -> 30, of which waited for: 15 -> 10; matrix products, arithmetic and copies ran while one was open for 3% -> 3% of each run, Pallas kernels for 19% -> 23%
where the time goes in v2:
time: 82.5 us; the launch traced here: 82.3 us
  starting transfers between devices  30.9 us (37%)
  waiting for transfers between devices  25.8 us (31%)
  Pallas kernels  21.5 us (26%)
  other arithmetic  2.22 us (3%)
  between operations  0.93 us (1%)
  local copies, waits for them, and re-layouts  0.91 us (1%)
    ppermute x30, starting transfers between devices, flip(): return lax.ppermute(x, axis, [(i, i ^ mask) for i in range(size)])  30.9 us
    ppermute x30, waiting for transfers between devices, flip(): return lax.ppermute(x, axis, [(i, i ^ mask) for i in range(size)])  25.8 us
    pallas_call x2, Pallas kernels, attend(): pl.pallas_call(functools.partial(attend_kernel, pair, heads, group), out_...  5.79 us
    pallas_call x4, Pallas kernels, raw_terms(): pl.pallas_call(raw_kernel, out_shape=[jax.ShapeDtypeStruct((count, HEAD_S...  3.9 us
    pallas_call x2, Pallas kernels, back(): pl.pallas_call(functools.partial(back_kernel, pairs, parts), out_shape=[j...  2.56 us
    pallas_call x2, Pallas kernels, terms(): pl.pallas_call(terms_kernel, out_shape=outs, in_specs=[SMEM] + [VMEM] * 4...  2.5 us
    pallas_call x1, Pallas kernels, join(): pl.pallas_call(join_kernel, out_shape=jax.ShapeDtypeStruct((count, 2 * ch...  1.93 us
    pallas_call x1, Pallas kernels, cut(): pl.pallas_call(cut_kernel, out_shape=[jax.ShapeDtypeStruct((chips, count,...  1.83 us
  transfers between devices with their start and end apart: 30, of which 10 were waited for; matrix products, arithmetic and copies ran while one was open for 3% of the time, Pallas kernels for 23%

profile of v2, /device:TPU:0, one launch (start us, length us, event | category | flops | bytes accessed | tf_op | source)
XLA Modules:
  0.0 82.3 jit_solution(3398312727348284694)
XLA Ops:
  1.1 2.7 %collective-permute-start.1 = (bf16[128,512]{1,0:T(8,128)(2,1)}, bf16[128,512]{1,0:T(8,128)(2,1)S(1)}, u32[]{:S(2)}, u32[]{:S(2)}) collective-permute-start(bf16[128,512]{1,0:T(8,128)(2,1)} %param.10), channel_id=1, source_target_pairs={{0,1},{1,0},{2,3},{3,2},{4,5},{5,4},{6,7},{7,6},{8,9},{9,8},{10,11... | collective-permute-start | bytes 393224 | tf_op jit(solution)/shard_map/ppermute | solution.py:34
  4.7 2.5 %collective-permute-start.3 = (bf16[128,256]{1,0:T(8,128)(2,1)S(1)}, bf16[128,256]{1,0:T(8,128)(2,1)S(1)}, u32[]{:S(2)}, u32[]{:S(2)}) collective-permute-start(bf16[128,256]{1,0:T(8,128)(2,1)S(1)} %get-tuple-element.87.refs_0_), channel_id=1, source_target_pairs={{0,3},{1,2},{2,1},{3,0},{4,7},{5,6},{6,5},{7,4},{8,11},{9,10},{10,... | collective-permute-start | bytes 196616 | tf_op jit(solution)/shard_map/ppermute | solution.py:34
  7.5 4.8 %collective-permute-done.3.refs_3_ = bf16[128,256]{1,0:T(8,128)(2,1)S(1)} collective-permute-done((bf16[128,256]{1,0:T(8,128)(2,1)S(1)}, bf16[128,256]{1,0:T(8,128)(2,1)S(1)}, u32[]{:S(2)}, u32[]{:S(2)}) %collective-permute-start.3) | collective-permute-done | bytes 65568 | tf_op jit(solution)/shard_map/ppermute | solution.py:34
  12.3 2.2 %collective-permute-done.2.refs_2_ = bf16[128,256]{1,0:T(8,128)(2,1)S(1)} collective-permute-done((bf16[128,256]{1,0:T(8,128)(2,1)S(1)}, bf16[128,256]{1,0:T(8,128)(2,1)S(1)}, u32[]{:S(2)}, u32[]{:S(2)}) %collective-permute-start.2) | collective-permute-done | bytes 65568 | tf_op jit(solution)/shard_map/ppermute | solution.py:34
  15.0 2.5 %collective-permute-start.6 = (bf16[4,128,256]{2,1,0:T(8,128)(2,1)S(1)}, bf16[4,128,256]{2,1,0:T(8,128)(2,1)S(1)}, u32[]{:S(2)}, u32[]{:S(2)}) collective-permute-start(bf16[4,128,256]{2,1,0:T(8,128)(2,1)S(1)} %line.2.refs_0_.refs_2_), channel_id=1, source_target_pairs={{0,24},{4,28},{8,16},{12,20},{16,8},{20,12},{24,0},{28,4},{1,25},{... | collective-permute-start | bytes 786440 | tf_op jit(solution)/shard_map/ppermute | solution.py:34
  19.3 2.3 %collective-permute-start.11 = (bf16[128,256]{1,0:T(8,128)(2,1)S(1)}, bf16[128,256]{1,0:T(8,128)(2,1)S(1)}, u32[]{:S(2)}, u32[]{:S(2)}) collective-permute-start(bf16[128,256]{1,0:T(8,128)(2,1)S(1)} %get-tuple-element.55.refs_0_), channel_id=1, source_target_pairs={{0,3},{1,2},{2,1},{3,0},{4,7},{5,6},{6,5},{7,4},{8,11},{9,10},{10,... | collective-permute-start | bytes 196616 | tf_op jit(solution)/shard_map/ppermute | solution.py:34
  21.5 1.8 %cut.1 = (bf16[4,256,512]{2,1,0:T(8,128)(2,1)S(1)}, bf16[4,256,512]{2,1,0:T(8,128)(2,1)S(1)}) custom-call(s32[2]{0:T(128)S(1)} %pad_add_fusion.place_ref, bf16[256,4096]{1,0:T(8,128)(2,1)} %x_hbm.1, bf16[256,4096]{1,0:T(8,128)(2,1)S(1)} %collective-permute-done.sib_hbm), custom_call_target="tpu_custom_call" | custom-call | flops 1 | bytes 1 | tf_op jit(solution)/shard_map/cut/pallas_call | solution.py:273
  23.4 2.0 %collective-permute-done.11.refs_3_ = bf16[128,256]{1,0:T(8,128)(2,1)S(1)} collective-permute-done((bf16[128,256]{1,0:T(8,128)(2,1)S(1)}, bf16[128,256]{1,0:T(8,128)(2,1)S(1)}, u32[]{:S(2)}, u32[]{:S(2)}) %collective-permute-start.11) | collective-permute-done | bytes 65568 | tf_op jit(solution)/shard_map/ppermute | solution.py:34
  25.3 1.6 %collective-permute-done.10.refs_2_ = bf16[128,256]{1,0:T(8,128)(2,1)S(1)} collective-permute-done((bf16[128,256]{1,0:T(8,128)(2,1)S(1)}, bf16[128,256]{1,0:T(8,128)(2,1)S(1)}, u32[]{:S(2)}, u32[]{:S(2)}) %collective-permute-start.10) | collective-permute-done | bytes 65568 | tf_op jit(solution)/shard_map/ppermute | solution.py:34
  27.5 1.6 %collective-permute-start.12 = (bf16[4,128,256]{2,1,0:T(8,128)(2,1)S(1)}, bf16[4,128,256]{2,1,0:T(8,128)(2,1)S(1)}, u32[]{:S(2)}, u32[]{:S(2)}) collective-permute-start(bf16[4,128,256]{2,1,0:T(8,128)(2,1)S(1)} %line.3.refs_0_.refs_6_), channel_id=1, source_target_pairs={{0,8},{4,12},{8,0},{12,4},{16,24},{20,28},{24,16},{28,20},{1,9},{5... | collective-permute-start | bytes 786440 | tf_op jit(solution)/shard_map/ppermute | solution.py:34
  29.1 1.5 %collective-permute-start.13 = (bf16[4,128,256]{2,1,0:T(8,128)(2,1)S(1)}, bf16[4,128,256]{2,1,0:T(8,128)(2,1)S(1)}, u32[]{:S(2)}, u32[]{:S(2)}) collective-permute-start(bf16[4,128,256]{2,1,0:T(8,128)(2,1)S(1)} %line.3.refs_0_.refs_6_), channel_id=1, source_target_pairs={{0,16},{4,20},{8,24},{12,28},{16,0},{20,4},{24,8},{28,12},{1,17},{... | collective-permute-start | bytes 786440 | tf_op jit(solution)/shard_map/ppermute | solution.py:34
  34.4 2.9 %attend.2.gk_ref.refs_0_ = bf16[256,256]{1,0:T(8,128)(2,1)S(1)} custom-call(s32[1,256]{1,0:T(1,128)S(1)} %bitcast.3, f32[256,128]{1,0:T(8,128)S(1)} %get-tuple-element.91.cos_ref, f32[256,128]{1,0:T(8,128)S(1)} %get-tuple-element.92.sin_ref, f32[256,128]{1,0:T(8,128)S(1)} %get-tuple-element.46.refs_0_, f32[256,128]{1,0:T(8,128)S(1)} %get-tuple-element.47.refs_1_, ...), custom_call_target="tpu_custom_call" | custom-call | flops 1 | bytes 1 | tf_op jit(solution)/shard_map/attend/pallas_call | solution.py:152
  40.0 1.6 %collective-permute-start.17 = (bf16[4,128,256]{2,1,0:T(8,128)(2,1)S(1)}, bf16[4,128,256]{2,1,0:T(8,128)(2,1)S(1)}, u32[]{:S(2)}, u32[]{:S(2)}) collective-permute-start(bf16[4,128,256]{2,1,0:T(8,128)(2,1)S(1)} %get-tuple-element.62), channel_id=1, source_target_pairs={{0,8},{4,12},{8,0},{12,4},{16,24},{20,28},{24,16},{28,20},{1,9},{5... | collective-permute-start | bytes 786440 | tf_op jit(solution)/shard_map/ppermute | solution.py:34
  41.5 1.5 %collective-permute-start.18 = (bf16[4,128,256]{2,1,0:T(8,128)(2,1)S(1)}, bf16[4,128,256]{2,1,0:T(8,128)(2,1)S(1)}, u32[]{:S(2)}, u32[]{:S(2)}) collective-permute-start(bf16[4,128,256]{2,1,0:T(8,128)(2,1)S(1)} %get-tuple-element.63), channel_id=1, source_target_pairs={{0,16},{4,20},{8,24},{12,28},{16,0},{20,4},{24,8},{28,12},{1,17},{... | collective-permute-start | bytes 786440 | tf_op jit(solution)/shard_map/ppermute | solution.py:34
  46.1 2.9 %attend.3.gk_ref.refs_1_ = bf16[256,256]{1,0:T(8,128)(2,1)S(1)} custom-call(s32[1,256]{1,0:T(1,128)S(1)} %bitcast.4, f32[256,128]{1,0:T(8,128)S(1)} %get-tuple-element.91.cos_ref, f32[256,128]{1,0:T(8,128)S(1)} %get-tuple-element.92.sin_ref, f32[256,128]{1,0:T(8,128)S(1)} %get-tuple-element.57.refs_0_, f32[256,128]{1,0:T(8,128)S(1)} %get-tuple-element.58.refs_1_, ...), custom_call_target="tpu_custom_call" | custom-call | flops 1 | bytes 1 | tf_op jit(solution)/shard_map/attend/pallas_call | solution.py:152
  49.4 5.8 %collective-permute-done.18.refs_2_ = bf16[4,128,256]{2,1,0:T(8,128)(2,1)S(1)} collective-permute-done((bf16[4,128,256]{2,1,0:T(8,128)(2,1)S(1)}, bf16[4,128,256]{2,1,0:T(8,128)(2,1)S(1)}, u32[]{:S(2)}, u32[]{:S(2)}) %collective-permute-start.18) | collective-permute-done | bytes 262176 | tf_op jit(solution)/shard_map/ppermute | solution.py:34
  57.2 1.3 %collective-permute-start.23 = (bf16[4,128,256]{2,1,0:T(8,128)(2,1)S(1)}, bf16[4,128,256]{2,1,0:T(8,128)(2,1)S(1)}, u32[]{:S(2)}, u32[]{:S(2)}) collective-permute-start(bf16[4,128,256]{2,1,0:T(8,128)(2,1)S(1)} %get-tuple-element.73), channel_id=1, source_target_pairs={{0,8},{4,12},{8,0},{12,4},{16,24},{20,28},{24,16},{28,20},{1,9},{5... | collective-permute-start | bytes 786440 | tf_op jit(solution)/shard_map/ppermute | solution.py:34
  59.3 1.4 %collective-permute-start.25 = (bf16[4,128,256]{2,1,0:T(8,128)(2,1)S(1)}, bf16[4,128,256]{2,1,0:T(8,128)(2,1)S(1)}, u32[]{:S(2)}, u32[]{:S(2)}) collective-permute-start(bf16[4,128,256]{2,1,0:T(8,128)(2,1)S(1)} %get-tuple-element.75), channel_id=1, source_target_pairs={{0,24},{4,28},{8,16},{12,20},{16,8},{20,12},{24,0},{28,4},{1,25},{... | collective-permute-start | bytes 786440 | tf_op jit(solution)/shard_map/ppermute | solution.py:34
  61.2 1.8 %collective-permute-start.22 = (bf16[128,256]{1,0:T(8,128)(2,1)S(1)}, bf16[128,256]{1,0:T(8,128)(2,1)S(1)}, u32[]{:S(2)}, u32[]{:S(2)}) collective-permute-start(bf16[128,256]{1,0:T(8,128)(2,1)S(1)} %get-tuple-element.71), channel_id=1, source_target_pairs={{0,3},{1,2},{2,1},{3,0},{4,7},{5,6},{6,5},{7,4},{8,11},{9,10},{10,... | collective-permute-start | bytes 196616 | tf_op jit(solution)/shard_map/ppermute | solution.py:34
  67.4 4.0 %collective-permute-done.24.refs_2_ = bf16[4,128,256]{2,1,0:T(8,128)(2,1)S(1)} collective-permute-done((bf16[4,128,256]{2,1,0:T(8,128)(2,1)S(1)}, bf16[4,128,256]{2,1,0:T(8,128)(2,1)S(1)}, u32[]{:S(2)}, u32[]{:S(2)}) %collective-permute-start.24) | collective-permute-done | bytes 262176 | tf_op jit(solution)/shard_map/ppermute | solution.py:34
  72.2 2.9 %collective-permute-start.28 = (bf16[128,256]{1,0:T(8,128)(2,1)S(1)}, bf16[128,256]{1,0:T(8,128)(2,1)S(1)}, u32[]{:S(2)}, u32[]{:S(2)}) collective-permute-start(bf16[128,256]{1,0:T(8,128)(2,1)S(1)} %get-tuple-element.82), channel_id=1, source_target_pairs={{0,2},{1,3},{2,0},{3,1},{4,6},{5,7},{6,4},{7,5},{8,10},{9,11},{10,... | collective-permute-start | bytes 196616 | tf_op jit(solution)/shard_map/ppermute | solution.py:34
  75.1 1.5 %collective-permute-start.29 = (bf16[128,256]{1,0:T(8,128)(2,1)S(1)}, bf16[128,256]{1,0:T(8,128)(2,1)S(1)}, u32[]{:S(2)}, u32[]{:S(2)}) collective-permute-start(bf16[128,256]{1,0:T(8,128)(2,1)S(1)} %get-tuple-element.83), channel_id=1, source_target_pairs={{0,3},{1,2},{2,1},{3,0},{4,7},{5,6},{6,5},{7,4},{8,11},{9,10},{10,... | collective-permute-start | bytes 196616 | tf_op jit(solution)/shard_map/ppermute | solution.py:34
  76.6 1.9 %join.1 = bf16[256,4096]{1,0:T(8,128)(2,1)} custom-call(s32[2]{0:T(128)S(1)} %pad_add_fusion.place_ref, bf16[4,256,512]{2,1,0:T(8,128)(2,1)S(1)} %back.2.refs_0_, bf16[4,256,512]{2,1,0:T(8,128)(2,1)S(1)} %collective-permute-done.26.refs_1_), custom_call_target="tpu_custom_call" | custom-call | flops 1 | bytes 1 | tf_op jit(solution)/shard_map/join/pallas_call | solution.py:311
  78.5 3.0 %collective-permute-done.29 = bf16[128,256]{1,0:T(8,128)(2,1)S(1)} collective-permute-done((bf16[128,256]{1,0:T(8,128)(2,1)S(1)}, bf16[128,256]{1,0:T(8,128)(2,1)S(1)}, u32[]{:S(2)}, u32[]{:S(2)}) %collective-permute-start.29) | collective-permute-done | bytes 65568 | tf_op jit(solution)/shard_map/ppermute | solution.py:34
  (69 shorter events, 23.5 us)
Async XLA Ops:
  0.6 11.6 %collective-permute-start = (bf16[256,4096]{1,0:T(8,128)(2,1)}, bf16[256,4096]{1,0:T(8,128)(2,1)S(1)}, u32[]{:S(2)}, u32[]{:S(2)}) collective-permute-start(bf16[256,4096]{1,0:T(8,128)(2,1)} %x_hbm.1), channel_id=1, source_target_pairs={{0,4},{4,0},{8,12},{12,8},{16,20},{20,16},{24,28},{28,24},{1,5},{5... | collective-permute-start | bytes 6291464 | tf_op jit(solution)/shard_map/ppermute | solution.py:34
  1.1 13.3 %collective-permute-start.1 = (bf16[128,512]{1,0:T(8,128)(2,1)}, bf16[128,512]{1,0:T(8,128)(2,1)S(1)}, u32[]{:S(2)}, u32[]{:S(2)}) collective-permute-start(bf16[128,512]{1,0:T(8,128)(2,1)} %param.10), channel_id=1, source_target_pairs={{0,1},{1,0},{2,3},{3,2},{4,5},{5,4},{6,7},{7,6},{8,9},{9,8},{10,11... | collective-permute-start | bytes 393224 | tf_op jit(solution)/shard_map/ppermute | solution.py:34
  4.7 7.6 %collective-permute-start.3 = (bf16[128,256]{1,0:T(8,128)(2,1)S(1)}, bf16[128,256]{1,0:T(8,128)(2,1)S(1)}, u32[]{:S(2)}, u32[]{:S(2)}) collective-permute-start(bf16[128,256]{1,0:T(8,128)(2,1)S(1)} %get-tuple-element.87.refs_0_), channel_id=1, source_target_pairs={{0,3},{1,2},{2,1},{3,0},{4,7},{5,6},{6,5},{7,4},{8,11},{9,10},{10,... | collective-permute-start | bytes 196616 | tf_op jit(solution)/shard_map/ppermute | solution.py:34
  7.2 7.2 %collective-permute-start.2 = (bf16[128,256]{1,0:T(8,128)(2,1)S(1)}, bf16[128,256]{1,0:T(8,128)(2,1)S(1)}, u32[]{:S(2)}, u32[]{:S(2)}) collective-permute-start(bf16[128,256]{1,0:T(8,128)(2,1)S(1)} %get-tuple-element.87.refs_0_), channel_id=1, source_target_pairs={{0,2},{1,3},{2,0},{3,1},{4,6},{5,7},{6,4},{7,5},{8,10},{9,11},{10,... | collective-permute-start | bytes 196616 | tf_op jit(solution)/shard_map/ppermute | solution.py:34
  15.0 10.3 %collective-permute-start.6 = (bf16[4,128,256]{2,1,0:T(8,128)(2,1)S(1)}, bf16[4,128,256]{2,1,0:T(8,128)(2,1)S(1)}, u32[]{:S(2)}, u32[]{:S(2)}) collective-permute-start(bf16[4,128,256]{2,1,0:T(8,128)(2,1)S(1)} %line.2.refs_0_.refs_2_), channel_id=1, source_target_pairs={{0,24},{4,28},{8,16},{12,20},{16,8},{20,12},{24,0},{28,4},{1,25},{... | collective-permute-start | bytes 786440 | tf_op jit(solution)/shard_map/ppermute | solution.py:34
  17.5 13.6 %collective-permute-start.4 = (bf16[4,128,256]{2,1,0:T(8,128)(2,1)S(1)}, bf16[4,128,256]{2,1,0:T(8,128)(2,1)S(1)}, u32[]{:S(2)}, u32[]{:S(2)}) collective-permute-start(bf16[4,128,256]{2,1,0:T(8,128)(2,1)S(1)} %line.2.refs_0_.refs_2_), channel_id=1, source_target_pairs={{0,8},{4,12},{8,0},{12,4},{16,24},{20,28},{24,16},{28,20},{1,9},{5... | collective-permute-start | bytes 786440 | tf_op jit(solution)/shard_map/ppermute | solution.py:34
  18.1 13.0 %collective-permute-start.5 = (bf16[4,128,256]{2,1,0:T(8,128)(2,1)S(1)}, bf16[4,128,256]{2,1,0:T(8,128)(2,1)S(1)}, u32[]{:S(2)}, u32[]{:S(2)}) collective-permute-start(bf16[4,128,256]{2,1,0:T(8,128)(2,1)S(1)} %line.2.refs_0_.refs_2_), channel_id=1, source_target_pairs={{0,16},{4,20},{8,24},{12,28},{16,0},{20,4},{24,8},{28,12},{1,17},{... | collective-permute-start | bytes 786440 | tf_op jit(solution)/shard_map/ppermute | solution.py:34
  19.3 6.1 %collective-permute-start.11 = (bf16[128,256]{1,0:T(8,128)(2,1)S(1)}, bf16[128,256]{1,0:T(8,128)(2,1)S(1)}, u32[]{:S(2)}, u32[]{:S(2)}) collective-permute-start(bf16[128,256]{1,0:T(8,128)(2,1)S(1)} %get-tuple-element.55.refs_0_), channel_id=1, source_target_pairs={{0,3},{1,2},{2,1},{3,0},{4,7},{5,6},{6,5},{7,4},{8,11},{9,10},{10,... | collective-permute-start | bytes 196616 | tf_op jit(solution)/shard_map/ppermute | solution.py:34
  21.5 5.4 %collective-permute-start.10 = (bf16[128,256]{1,0:T(8,128)(2,1)S(1)}, bf16[128,256]{1,0:T(8,128)(2,1)S(1)}, u32[]{:S(2)}, u32[]{:S(2)}) collective-permute-start(bf16[128,256]{1,0:T(8,128)(2,1)S(1)} %get-tuple-element.55.refs_0_), channel_id=1, source_target_pairs={{0,2},{1,3},{2,0},{3,1},{4,6},{5,7},{6,4},{7,5},{8,10},{9,11},{10,... | collective-permute-start | bytes 196616 | tf_op jit(solution)/shard_map/ppermute | solution.py:34
  27.5 15.5 %collective-permute-start.12 = (bf16[4,128,256]{2,1,0:T(8,128)(2,1)S(1)}, bf16[4,128,256]{2,1,0:T(8,128)(2,1)S(1)}, u32[]{:S(2)}, u32[]{:S(2)}) collective-permute-start(bf16[4,128,256]{2,1,0:T(8,128)(2,1)S(1)} %line.3.refs_0_.refs_6_), channel_id=1, source_target_pairs={{0,8},{4,12},{8,0},{12,4},{16,24},{20,28},{24,16},{28,20},{1,9},{5... | collective-permute-start | bytes 786440 | tf_op jit(solution)/shard_map/ppermute | solution.py:34
  29.1 14.5 %collective-permute-start.13 = (bf16[4,128,256]{2,1,0:T(8,128)(2,1)S(1)}, bf16[4,128,256]{2,1,0:T(8,128)(2,1)S(1)}, u32[]{:S(2)}, u32[]{:S(2)}) collective-permute-start(bf16[4,128,256]{2,1,0:T(8,128)(2,1)S(1)} %line.3.refs_0_.refs_6_), channel_id=1, source_target_pairs={{0,16},{4,20},{8,24},{12,28},{16,0},{20,4},{24,8},{28,12},{1,17},{... | collective-permute-start | bytes 786440 | tf_op jit(solution)/shard_map/ppermute | solution.py:34
  30.6 12.9 %collective-permute-start.14 = (bf16[4,128,256]{2,1,0:T(8,128)(2,1)S(1)}, bf16[4,128,256]{2,1,0:T(8,128)(2,1)S(1)}, u32[]{:S(2)}, u32[]{:S(2)}) collective-permute-start(bf16[4,128,256]{2,1,0:T(8,128)(2,1)S(1)} %line.3.refs_0_.refs_6_), channel_id=1, source_target_pairs={{0,24},{4,28},{8,16},{12,20},{16,8},{20,12},{24,0},{28,4},{1,25},{... | collective-permute-start | bytes 786440 | tf_op jit(solution)/shard_map/ppermute | solution.py:34
  40.0 9.4 %collective-permute-start.17 = (bf16[4,128,256]{2,1,0:T(8,128)(2,1)S(1)}, bf16[4,128,256]{2,1,0:T(8,128)(2,1)S(1)}, u32[]{:S(2)}, u32[]{:S(2)}) collective-permute-start(bf16[4,128,256]{2,1,0:T(8,128)(2,1)S(1)} %get-tuple-element.62), channel_id=1, source_target_pairs={{0,8},{4,12},{8,0},{12,4},{16,24},{20,28},{24,16},{28,20},{1,9},{5... | collective-permute-start | bytes 786440 | tf_op jit(solution)/shard_map/ppermute | solution.py:34
  41.5 13.7 %collective-permute-start.18 = (bf16[4,128,256]{2,1,0:T(8,128)(2,1)S(1)}, bf16[4,128,256]{2,1,0:T(8,128)(2,1)S(1)}, u32[]{:S(2)}, u32[]{:S(2)}) collective-permute-start(bf16[4,128,256]{2,1,0:T(8,128)(2,1)S(1)} %get-tuple-element.63), channel_id=1, source_target_pairs={{0,16},{4,20},{8,24},{12,28},{16,0},{20,4},{24,8},{28,12},{1,17},{... | collective-permute-start | bytes 786440 | tf_op jit(solution)/shard_map/ppermute | solution.py:34
  43.1 12.2 %collective-permute-start.19 = (bf16[4,128,256]{2,1,0:T(8,128)(2,1)S(1)}, bf16[4,128,256]{2,1,0:T(8,128)(2,1)S(1)}, u32[]{:S(2)}, u32[]{:S(2)}) collective-permute-start(bf16[4,128,256]{2,1,0:T(8,128)(2,1)S(1)} %get-tuple-element.64), channel_id=1, source_target_pairs={{0,24},{4,28},{8,16},{12,20},{16,8},{20,12},{24,0},{28,4},{1,25},{... | collective-permute-start | bytes 786440 | tf_op jit(solution)/shard_map/ppermute | solution.py:34
  49.0 6.9 %collective-permute-start.20 = (bf16[256,256]{1,0:T(8,128)(2,1)S(1)}, bf16[256,256]{1,0:T(8,128)(2,1)S(1)}, u32[]{:S(2)}, u32[]{:S(2)}) collective-permute-start(bf16[256,256]{1,0:T(8,128)(2,1)S(1)} %attend.3.gk_ref.refs_1_), channel_id=1, source_target_pairs={{0,4},{4,0},{8,12},{12,8},{16,20},{20,16},{24,28},{28,24},{1,5},{5... | collective-permute-start | bytes 393224 | tf_op jit(solution)/shard_map/ppermute | solution.py:34
  57.2 10.2 %collective-permute-start.23 = (bf16[4,128,256]{2,1,0:T(8,128)(2,1)S(1)}, bf16[4,128,256]{2,1,0:T(8,128)(2,1)S(1)}, u32[]{:S(2)}, u32[]{:S(2)}) collective-permute-start(bf16[4,128,256]{2,1,0:T(8,128)(2,1)S(1)} %get-tuple-element.73), channel_id=1, source_target_pairs={{0,8},{4,12},{8,0},{12,4},{16,24},{20,28},{24,16},{28,20},{1,9},{5... | collective-permute-start | bytes 786440 | tf_op jit(solution)/shard_map/ppermute | solution.py:34
  58.5 12.9 %collective-permute-start.24 = (bf16[4,128,256]{2,1,0:T(8,128)(2,1)S(1)}, bf16[4,128,256]{2,1,0:T(8,128)(2,1)S(1)}, u32[]{:S(2)}, u32[]{:S(2)}) collective-permute-start(bf16[4,128,256]{2,1,0:T(8,128)(2,1)S(1)} %get-tuple-element.74), channel_id=1, source_target_pairs={{0,16},{4,20},{8,24},{12,28},{16,0},{20,4},{24,8},{28,12},{1,17},{... | collective-permute-start | bytes 786440 | tf_op jit(solution)/shard_map/ppermute | solution.py:34
  59.3 12.0 %collective-permute-start.25 = (bf16[4,128,256]{2,1,0:T(8,128)(2,1)S(1)}, bf16[4,128,256]{2,1,0:T(8,128)(2,1)S(1)}, u32[]{:S(2)}, u32[]{:S(2)}) collective-permute-start(bf16[4,128,256]{2,1,0:T(8,128)(2,1)S(1)} %get-tuple-element.75), channel_id=1, source_target_pairs={{0,24},{4,28},{8,16},{12,20},{16,8},{20,12},{24,0},{28,4},{1,25},{... | collective-permute-start | bytes 786440 | tf_op jit(solution)/shard_map/ppermute | solution.py:34
  60.7 5.7 %collective-permute-start.21 = (bf16[128,256]{1,0:T(8,128)(2,1)S(1)}, bf16[128,256]{1,0:T(8,128)(2,1)S(1)}, u32[]{:S(2)}, u32[]{:S(2)}) collective-permute-start(bf16[128,256]{1,0:T(8,128)(2,1)S(1)} %get-tuple-element.70), channel_id=1, source_target_pairs={{0,2},{1,3},{2,0},{3,1},{4,6},{5,7},{6,4},{7,5},{8,10},{9,11},{10,... | collective-permute-start | bytes 196616 | tf_op jit(solution)/shard_map/ppermute | solution.py:34
  61.2 6.1 %collective-permute-start.22 = (bf16[128,256]{1,0:T(8,128)(2,1)S(1)}, bf16[128,256]{1,0:T(8,128)(2,1)S(1)}, u32[]{:S(2)}, u32[]{:S(2)}) collective-permute-start(bf16[128,256]{1,0:T(8,128)(2,1)S(1)} %get-tuple-element.71), channel_id=1, source_target_pairs={{0,3},{1,2},{2,1},{3,0},{4,7},{5,6},{6,5},{7,4},{8,11},{9,10},{10,... | collective-permute-start | bytes 196616 | tf_op jit(solution)/shard_map/ppermute | solution.py:34
  72.1 9.4 %collective-permute-start.27 = (bf16[128,512]{1,0:T(8,128)(2,1)S(1)}, bf16[128,512]{1,0:T(8,128)(2,1)S(1)}, u32[]{:S(2)}, u32[]{:S(2)}) collective-permute-start(bf16[128,512]{1,0:T(8,128)(2,1)S(1)} %get-tuple-element.80), channel_id=1, source_target_pairs={{0,1},{1,0},{2,3},{3,2},{4,5},{5,4},{6,7},{7,6},{8,9},{9,8},{10,11... | collective-permute-start | bytes 393224 | tf_op jit(solution)/shard_map/ppermute | solution.py:34
  72.2 6.3 %collective-permute-start.28 = (bf16[128,256]{1,0:T(8,128)(2,1)S(1)}, bf16[128,256]{1,0:T(8,128)(2,1)S(1)}, u32[]{:S(2)}, u32[]{:S(2)}) collective-permute-start(bf16[128,256]{1,0:T(8,128)(2,1)S(1)} %get-tuple-element.82), channel_id=1, source_target_pairs={{0,2},{1,3},{2,0},{3,1},{4,6},{5,7},{6,4},{7,5},{8,10},{9,11},{10,... | collective-permute-start | bytes 196616 | tf_op jit(solution)/shard_map/ppermute | solution.py:34
  75.1 6.4 %collective-permute-start.29 = (bf16[128,256]{1,0:T(8,128)(2,1)S(1)}, bf16[128,256]{1,0:T(8,128)(2,1)S(1)}, u32[]{:S(2)}, u32[]{:S(2)}) collective-permute-start(bf16[128,256]{1,0:T(8,128)(2,1)S(1)} %get-tuple-element.83), channel_id=1, source_target_pairs={{0,3},{1,2},{2,1},{3,0},{4,7},{5,6},{6,5},{7,4},{8,11},{9,10},{10,... | collective-permute-start | bytes 196616 | tf_op jit(solution)/shard_map/ppermute | solution.py:34
  (10 other events, 23.7 us)

commit v3 on v2

--- a/solution.py
+++ b/solution.py
@@ -103,9 +103,9 @@
 
 
 def attend_kernel(pair, heads, group, pos_ref, cos_ref, sin_ref, *refs):
-    raws, sib_raws, (q, v, u, gk_ref) = refs[:heads], refs[heads : 2 * heads], refs[2 * heads :]
+    raws, sib_raws, (q, v, u), outs = refs[:heads], refs[heads : 2 * heads], refs[2 * heads : 2 * heads + 3], refs[-heads:]
     width = heads * HEAD_SIZE
-    count = gk_ref.shape[0]
+    count = outs[0].shape[0]
     block = count // 2
     biases = []
     for part in range(2):
@@ -118,7 +118,6 @@
     scale = HEAD_SIZE ** (-0.5)
     slope = scale * math.log2(math.e)
     for head in range(heads):
-        cols = slice(head * HEAD_SIZE, (head + 1) * HEAD_SIZE)
         mine = raws[head][...] + sib_raws[head][...]
         keys = (mine * cosine + pltpu.roll(mine, HEAD_SIZE // 2, 1) * sine).astype(jnp.bfloat16)
         vals = v[:, pair * width + head * HEAD_SIZE : pair * width + (head + 1) * HEAD_SIZE]
@@ -143,7 +142,7 @@
                 total += jnp.dot(dscores, qs, preferred_element_type=jnp.float32)
             totals.append(total)
         drot = jnp.concatenate([totals[0] + totals[1][:block], totals[1][block:]], axis=0)
-        gk_ref[:, cols] = (drot * cosine - pltpu.roll(drot, HEAD_SIZE // 2, 1) * sine).astype(jnp.bfloat16)
+        outs[head][...] = (drot * cosine - pltpu.roll(drot, HEAD_SIZE // 2, 1) * sine).astype(jnp.bfloat16)
 
 
 def attend(pair, group, pos, cosine, sine, raw, sib_raw, q, v, u):
@@ -151,18 +150,19 @@
     q, v, u = (pltpu.with_memory_space_constraint(x, pltpu.VMEM) for x in (q, v, u))
     return pl.pallas_call(
         functools.partial(attend_kernel, pair, heads, group),
-        out_shape=jax.ShapeDtypeStruct((count, heads * width), jnp.bfloat16),
+        out_shape=[jax.ShapeDtypeStruct((count, width), jnp.bfloat16)] * heads,
         in_specs=[VMEM] * (6 + 2 * heads),
-        out_specs=VMEM,
+        out_specs=[VMEM] * heads,
         compiler_params=PARAMS,
         cost_estimate=CHEAP,
         name="attend",
     )(pos, cosine, sine, *raw, *sib_raw, q, v, u)
 
 
-def terms_kernel(place_ref, own_ref, sib_ref, gk_ref, sib_gk_ref, *outs):
+def terms_kernel(heads, place_ref, own_ref, sib_ref, *refs):
+    outs = refs[2 * heads :]
     chip = place_ref[0] // 2
-    gk, sib_gk = gk_ref[...], sib_gk_ref[...]
+    gk, sib_gk = (jnp.concatenate([ref[...] for ref in refs[n : n + heads]], axis=1) for n in (0, heads))
 
     def term(m, dtype):
         total = jnp.dot(own_ref[chip ^ m], gk, preferred_element_type=jnp.float32)
@@ -175,19 +175,19 @@
 
 def terms(locs, place, own, sib, gk, sib_gk):
     chips, block, count = own.shape
-    width = gk.shape[1]
+    heads, width = len(gk), len(gk) * gk[0].shape[1]
     outs = [
         jax.ShapeDtypeStruct((locs, block // locs, width), jnp.bfloat16 if m else jnp.float32) for m in range(chips)
     ]
     return pl.pallas_call(
-        terms_kernel,
+        functools.partial(terms_kernel, heads),
         out_shape=outs,
-        in_specs=[SMEM] + [VMEM] * 4,
+        in_specs=[SMEM] + [VMEM] * (2 + 2 * heads),
         out_specs=[VMEM] * len(outs),
         compiler_params=PARAMS,
         cost_estimate=CHEAP,
         name="terms",
-    )(place, own, sib, gk, sib_gk)
+    )(place, own, sib, *gk, *sib_gk)
 
 
 def add_kernel(locs, count, place_ref, *refs):
@@ -220,8 +220,11 @@
     )(place, *parts, *earlier)
 
 
-def back_kernel(pairs, parts, place_ref, *refs):
-    grads, pieces, outs = [g[...] for g in refs[:pairs]], refs[pairs : len(refs) - parts], refs[len(refs) - parts :]
+def back_kernel(pairs, heads, parts, place_ref, *refs):
+    pieces, outs = refs[pairs * heads : len(refs) - parts], refs[len(refs) - parts :]
+    grads = [
+        jnp.concatenate([ref[...] for ref in refs[pair * heads : (pair + 1) * heads]], axis=1) for pair in range(pairs)
+    ]
     chips = len(pieces) // pairs
     for m in range(chips):
         total = None
@@ -236,16 +239,16 @@
 
 
 def back(place, gks, pieces, block, parts):
-    pairs, chips = len(pieces), len(pieces[0])
-    return pl.pallas_call(
-        functools.partial(back_kernel, pairs, parts),
-        out_shape=[jax.ShapeDtypeStruct((chips // parts, gks[0].shape[0], block), jnp.bfloat16)] * parts,
-        in_specs=[SMEM] + [VMEM] * (pairs + pairs * chips),
+    pairs, heads, chips = len(pieces), len(gks[0]), len(pieces[0])
+    return pl.pallas_call(
+        functools.partial(back_kernel, pairs, heads, parts),
+        out_shape=[jax.ShapeDtypeStruct((chips // parts, gks[0][0].shape[0], block), jnp.bfloat16)] * parts,
+        in_specs=[SMEM] + [VMEM] * (pairs * heads + pairs * chips),
         out_specs=[VMEM] * parts,
         compiler_params=PARAMS,
         cost_estimate=CHEAP,
         name="back",
-    )(place, *gks, *[piece for group in pieces for piece in group])
+    )(place, *[gk for group in gks for gk in group], *[piece for group in pieces for piece in group])
 
 
 def columns_of(array, chip, core, block):
@@ -368,18 +371,17 @@
     gks, sib_gks, sums, got = [], [], [], []
     raw, sib_raw = raw_of(0)
     for pair in range(PAIRS):
-        gk = attend(pair, group, pos, cosine, sine, raw, sib_raw, queries, values, upstream)
-        gks.append(gk)
-        sib_gks.append(swap(gk))
-        if pair:
-            gk = after(gk, sums[-1][0])
-        outs = list(terms(locs, place, own_turned, sib_turned, gk, sib_gks[-1]))
+        gks.append(list(attend(pair, group, pos, cosine, sine, raw, sib_raw, queries, values, upstream)))
+        sib_gks.append([swap(gk) for gk in gks[-1]])
+        outs = list(terms(locs, place, own_turned, sib_turned, gks[-1], sib_gks[-1]))
         if pair + 1 < PAIRS:
             raw, sib_raw = raw_of(pair + 1, outs[0])
-        parts = outs[:1] + [flip(outs[m], "node", 2 * m, nodes) for m in range(1, chips)]
+        sends = [after(out, *parts[1:]) if pair else out for out in outs]
+        parts = outs[:1] + [flip(sends[m], "node", 2 * m, nodes) for m in range(1, chips)]
         if pair + 1 == PAIRS:
             theirs, mine = (
-                back(place, [after(grads[0], outs[0])] + grads[1:], pieces, block, 1)[0] for grads in (sib_gks, gks)
+                back(place, [[after(group[0], outs[0])] + group[1:] for group in grads], pieces, block, 1)[0]
+                for grads in (sib_gks, gks)
             )
             parts[0] = after(parts[0], theirs, mine, *got[-1])
         sums.append(add(locs, place, parts, [part[1] for part in sums]))

time: 82.5 us -> 81 us (0.982)
  waiting for transfers between devices: 25.8 us -> 23.6 us
    ppermute x30 -> x32, waiting for transfers between devices: 25.8 us -> 23.6 us  [flip(): return lax.ppermute(x, axis, [(i, i ^ mask) for i in range(size)])]
    ppermute x30 -> x32, starting transfers between devices: 30.9 us -> 31.6 us  [flip(): return lax.ppermute(x, axis, [(i, i ^ mask) for i in range(size)])]
  transfers between devices with their start and end apart: 30 -> 32, of which waited for: 10 -> 13; matrix products, arithmetic and copies ran while one was open for 3% -> 3% of each run, Pallas kernels for 23% -> 25%
where the time goes in v3:
time: 81 us; the launch traced here: 80.8 us
  starting transfers between devices  31.6 us (39%)
  waiting for transfers between devices  23.6 us (29%)
  Pallas kernels  21.6 us (27%)
  other arithmetic  2.22 us (3%)
  between operations  0.93 us (1%)
  local copies, waits for them, and re-layouts  0.91 us (1%)
    ppermute x32, starting transfers between devices, flip(): return lax.ppermute(x, axis, [(i, i ^ mask) for i in range(size)])  31.6 us
    ppermute x32, waiting for transfers between devices, flip(): return lax.ppermute(x, axis, [(i, i ^ mask) for i in range(size)])  23.6 us
    pallas_call x2, Pallas kernels, attend(): pl.pallas_call(functools.partial(attend_kernel, pair, heads, group), out_...  5.79 us
    pallas_call x4, Pallas kernels, raw_terms(): pl.pallas_call(raw_kernel, out_shape=[jax.ShapeDtypeStruct((count, HEAD_S...  3.91 us
    pallas_call x2, Pallas kernels, back(): pl.pallas_call(functools.partial(back_kernel, pairs, heads, parts), out_s...  2.57 us
    pallas_call x2, Pallas kernels, terms(): pl.pallas_call(functools.partial(terms_kernel, heads), out_shape=outs, in...  2.49 us
    pallas_call x1, Pallas kernels, join(): pl.pallas_call(join_kernel, out_shape=jax.ShapeDtypeStruct((count, 2 * ch...  1.93 us
    pallas_call x1, Pallas kernels, cut(): pl.pallas_call(cut_kernel, out_shape=[jax.ShapeDtypeStruct((chips, count,...  1.83 us
  transfers between devices with their start and end apart: 32, of which 13 were waited for; matrix products, arithmetic and copies ran while one was open for 3% of the time, Pallas kernels for 25%

profile of v3, /device:TPU:0, one launch (start us, length us, event | category | flops | bytes accessed | tf_op | source)
XLA Modules:
  0.0 80.8 jit_solution(1180684113284245520)
XLA Ops:
  1.1 2.7 %collective-permute-start.1 = (bf16[128,512]{1,0:T(8,128)(2,1)}, bf16[128,512]{1,0:T(8,128)(2,1)S(1)}, u32[]{:S(2)}, u32[]{:S(2)}) collective-permute-start(bf16[128,512]{1,0:T(8,128)(2,1)} %param.10), channel_id=1, source_target_pairs={{0,1},{1,0},{2,3},{3,2},{4,5},{5,4},{6,7},{7,6},{8,9},{9,8},{10,11... | collective-permute-start | bytes 393224 | tf_op jit(solution)/shard_map/ppermute | solution.py:34
  4.7 2.5 %collective-permute-start.3 = (bf16[128,256]{1,0:T(8,128)(2,1)S(1)}, bf16[128,256]{1,0:T(8,128)(2,1)S(1)}, u32[]{:S(2)}, u32[]{:S(2)}) collective-permute-start(bf16[128,256]{1,0:T(8,128)(2,1)S(1)} %get-tuple-element.103.refs_0_), channel_id=1, source_target_pairs={{0,3},{1,2},{2,1},{3,0},{4,7},{5,6},{6,5},{7,4},{8,11},{9,10},{10,... | collective-permute-start | bytes 196616 | tf_op jit(solution)/shard_map/ppermute | solution.py:34
  7.5 4.8 %collective-permute-done.3.refs_3_ = bf16[128,256]{1,0:T(8,128)(2,1)S(1)} collective-permute-done((bf16[128,256]{1,0:T(8,128)(2,1)S(1)}, bf16[128,256]{1,0:T(8,128)(2,1)S(1)}, u32[]{:S(2)}, u32[]{:S(2)}) %collective-permute-start.3) | collective-permute-done | bytes 65568 | tf_op jit(solution)/shard_map/ppermute | solution.py:34
  12.3 2.2 %collective-permute-done.2.refs_2_ = bf16[128,256]{1,0:T(8,128)(2,1)S(1)} collective-permute-done((bf16[128,256]{1,0:T(8,128)(2,1)S(1)}, bf16[128,256]{1,0:T(8,128)(2,1)S(1)}, u32[]{:S(2)}, u32[]{:S(2)}) %collective-permute-start.2) | collective-permute-done | bytes 65568 | tf_op jit(solution)/shard_map/ppermute | solution.py:34
  15.0 2.5 %collective-permute-start.6 = (bf16[4,128,256]{2,1,0:T(8,128)(2,1)S(1)}, bf16[4,128,256]{2,1,0:T(8,128)(2,1)S(1)}, u32[]{:S(2)}, u32[]{:S(2)}) collective-permute-start(bf16[4,128,256]{2,1,0:T(8,128)(2,1)S(1)} %line.2.refs_0_.refs_4_), channel_id=1, source_target_pairs={{0,24},{4,28},{8,16},{12,20},{16,8},{20,12},{24,0},{28,4},{1,25},{... | collective-permute-start | bytes 786440 | tf_op jit(solution)/shard_map/ppermute | solution.py:34
  19.3 2.3 %collective-permute-start.12 = (bf16[128,256]{1,0:T(8,128)(2,1)S(1)}, bf16[128,256]{1,0:T(8,128)(2,1)S(1)}, u32[]{:S(2)}, u32[]{:S(2)}) collective-permute-start(bf16[128,256]{1,0:T(8,128)(2,1)S(1)} %get-tuple-element.65.refs_0_), channel_id=1, source_target_pairs={{0,3},{1,2},{2,1},{3,0},{4,7},{5,6},{6,5},{7,4},{8,11},{9,10},{10,... | collective-permute-start | bytes 196616 | tf_op jit(solution)/shard_map/ppermute | solution.py:34
  21.5 1.8 %cut.1 = (bf16[4,256,512]{2,1,0:T(8,128)(2,1)S(1)}, bf16[4,256,512]{2,1,0:T(8,128)(2,1)S(1)}) custom-call(s32[2]{0:T(128)S(1)} %pad_add_fusion.place_ref, bf16[256,4096]{1,0:T(8,128)(2,1)} %x_hbm.1, bf16[256,4096]{1,0:T(8,128)(2,1)S(1)} %collective-permute-done.sib_hbm), custom_call_target="tpu_custom_call" | custom-call | flops 1 | bytes 1 | tf_op jit(solution)/shard_map/cut/pallas_call | solution.py:276
  23.4 2.0 %collective-permute-done.12.refs_3_ = bf16[128,256]{1,0:T(8,128)(2,1)S(1)} collective-permute-done((bf16[128,256]{1,0:T(8,128)(2,1)S(1)}, bf16[128,256]{1,0:T(8,128)(2,1)S(1)}, u32[]{:S(2)}, u32[]{:S(2)}) %collective-permute-start.12) | collective-permute-done | bytes 65568 | tf_op jit(solution)/shard_map/ppermute | solution.py:34
  25.3 1.6 %collective-permute-done.11.refs_2_ = bf16[128,256]{1,0:T(8,128)(2,1)S(1)} collective-permute-done((bf16[128,256]{1,0:T(8,128)(2,1)S(1)}, bf16[128,256]{1,0:T(8,128)(2,1)S(1)}, u32[]{:S(2)}, u32[]{:S(2)}) %collective-permute-start.11) | collective-permute-done | bytes 65568 | tf_op jit(solution)/shard_map/ppermute | solution.py:34
  27.5 2.5 %collective-permute-start.15 = (bf16[4,128,256]{2,1,0:T(8,128)(2,1)S(1)}, bf16[4,128,256]{2,1,0:T(8,128)(2,1)S(1)}, u32[]{:S(2)}, u32[]{:S(2)}) collective-permute-start(bf16[4,128,256]{2,1,0:T(8,128)(2,1)S(1)} %line.3.refs_0_.refs_8_), channel_id=1, source_target_pairs={{0,24},{4,28},{8,16},{12,20},{16,8},{20,12},{24,0},{28,4},{1,25},{... | collective-permute-start | bytes 786440 | tf_op jit(solution)/shard_map/ppermute | solution.py:34
  34.4 2.9 %attend.2 = (bf16[256,128]{1,0:T(8,128)(2,1)S(1)}, bf16[256,128]{1,0:T(8,128)(2,1)S(1)}) custom-call(s32[1,256]{1,0:T(1,128)S(1)} %bitcast.3, f32[256,128]{1,0:T(8,128)S(1)} %get-tuple-element.107.cos_ref, f32[256,128]{1,0:T(8,128)S(1)} %get-tuple-element.108.sin_ref, f32[256,128]{1,0:T(8,128)S(1)} %get-tuple-element.54.refs_0_, ...), custom_call_target="tpu_custom_call" | custom-call | flops 1 | bytes 1 | tf_op jit(solution)/shard_map/attend/pallas_call | solution.py:151
  40.0 1.6 %collective-permute-start.20 = (bf16[4,128,256]{2,1,0:T(8,128)(2,1)S(1)}, bf16[4,128,256]{2,1,0:T(8,128)(2,1)S(1)}, u32[]{:S(2)}, u32[]{:S(2)}) collective-permute-start(bf16[4,128,256]{2,1,0:T(8,128)(2,1)S(1)} %get-tuple-element.79), channel_id=1, source_target_pairs={{0,8},{4,12},{8,0},{12,4},{16,24},{20,28},{24,16},{28,20},{1,9},{5... | collective-permute-start | bytes 786440 | tf_op jit(solution)/shard_map/ppermute | solution.py:34
  41.6 1.5 %collective-permute-start.21 = (bf16[4,128,256]{2,1,0:T(8,128)(2,1)S(1)}, bf16[4,128,256]{2,1,0:T(8,128)(2,1)S(1)}, u32[]{:S(2)}, u32[]{:S(2)}) collective-permute-start(bf16[4,128,256]{2,1,0:T(8,128)(2,1)S(1)} %get-tuple-element.80), channel_id=1, source_target_pairs={{0,16},{4,20},{8,24},{12,28},{16,0},{20,4},{24,8},{28,12},{1,17},{... | collective-permute-start | bytes 786440 | tf_op jit(solution)/shard_map/ppermute | solution.py:34
  46.2 2.9 %attend.3 = (bf16[256,128]{1,0:T(8,128)(2,1)S(1)}, bf16[256,128]{1,0:T(8,128)(2,1)S(1)}) custom-call(s32[1,256]{1,0:T(1,128)S(1)} %bitcast.4, f32[256,128]{1,0:T(8,128)S(1)} %get-tuple-element.107.cos_ref, f32[256,128]{1,0:T(8,128)S(1)} %get-tuple-element.108.sin_ref, f32[256,128]{1,0:T(8,128)S(1)} %get-tuple-element.67.refs_0_, ...), custom_call_target="tpu_custom_call" | custom-call | flops 1 | bytes 1 | tf_op jit(solution)/shard_map/attend/pallas_call | solution.py:151
  52.0 3.5 %collective-permute-done.21.refs_2_ = bf16[4,128,256]{2,1,0:T(8,128)(2,1)S(1)} collective-permute-done((bf16[4,128,256]{2,1,0:T(8,128)(2,1)S(1)}, bf16[4,128,256]{2,1,0:T(8,128)(2,1)S(1)}, u32[]{:S(2)}, u32[]{:S(2)}) %collective-permute-start.21) | collective-permute-done | bytes 262176 | tf_op jit(solution)/shard_map/ppermute | solution.py:34
  57.6 1.4 %collective-permute-start.27 = (bf16[4,128,256]{2,1,0:T(8,128)(2,1)S(1)}, bf16[4,128,256]{2,1,0:T(8,128)(2,1)S(1)}, u32[]{:S(2)}, u32[]{:S(2)}) collective-permute-start(bf16[4,128,256]{2,1,0:T(8,128)(2,1)S(1)} %get-tuple-element.90), channel_id=1, source_target_pairs={{0,24},{4,28},{8,16},{12,20},{16,8},{20,12},{24,0},{28,4},{1,25},{... | collective-permute-start | bytes 786440 | tf_op jit(solution)/shard_map/ppermute | solution.py:34
  60.2 1.9 %collective-permute-start.24 = (bf16[128,256]{1,0:T(8,128)(2,1)S(1)}, bf16[128,256]{1,0:T(8,128)(2,1)S(1)}, u32[]{:S(2)}, u32[]{:S(2)}) collective-permute-start(bf16[128,256]{1,0:T(8,128)(2,1)S(1)} %get-tuple-element.83), channel_id=1, source_target_pairs={{0,3},{1,2},{2,1},{3,0},{4,7},{5,6},{6,5},{7,4},{8,11},{9,10},{10,... | collective-permute-start | bytes 196616 | tf_op jit(solution)/shard_map/ppermute | solution.py:34
  62.1 1.3 %back.2.refs_0_ = bf16[4,256,512]{2,1,0:T(8,128)(2,1)S(1)} custom-call(s32[2]{0:T(128)S(1)} %pad_add_fusion.place_ref, bf16[256,128]{1,0:T(8,128)(2,1)S(1)} %get-tuple-element.75.refs_0_, bf16[256,128]{1,0:T(8,128)(2,1)S(1)} %get-tuple-element.62.refs_1_, bf16[256,128]{1,0:T(8,128)(2,1)S(1)} %get-tuple-element.76.refs_0_.refs_2_, ...), custom_call_target="tpu_custom_call" | custom-call | flops 1 | bytes 1 | tf_op jit(solution)/shard_map/back/pallas_call | solution.py:243
  63.4 1.3 %back.3 = bf16[4,256,512]{2,1,0:T(8,128)(2,1)S(1)} custom-call(s32[2]{0:T(128)S(1)} %pad_add_fusion.place_ref, bf16[256,128]{1,0:T(8,128)(2,1)S(1)} %collective-permute-done.9.refs_2_.refs_0_, bf16[256,128]{1,0:T(8,128)(2,1)S(1)} %collective-permute-done.10.refs_3_.refs_1_, bf16[256,128]{1,0:T(8,128)(2,1)S(1)} %collective-permute-done.18.refs_2_, ...), custom_call_target="tpu_custom_call" | custom-call | flops 1 | bytes 1 | tf_op jit(solution)/shard_map/back/pallas_call | solution.py:243
  66.4 3.4 %collective-permute-done.26.refs_2_ = bf16[4,128,256]{2,1,0:T(8,128)(2,1)S(1)} collective-permute-done((bf16[4,128,256]{2,1,0:T(8,128)(2,1)S(1)}, bf16[4,128,256]{2,1,0:T(8,128)(2,1)S(1)}, u32[]{:S(2)}, u32[]{:S(2)}) %collective-permute-start.26) | collective-permute-done | bytes 262176 | tf_op jit(solution)/shard_map/ppermute | solution.py:34
  70.7 2.9 %collective-permute-start.30 = (bf16[128,256]{1,0:T(8,128)(2,1)S(1)}, bf16[128,256]{1,0:T(8,128)(2,1)S(1)}, u32[]{:S(2)}, u32[]{:S(2)}) collective-permute-start(bf16[128,256]{1,0:T(8,128)(2,1)S(1)} %get-tuple-element.98), channel_id=1, source_target_pairs={{0,2},{1,3},{2,0},{3,1},{4,6},{5,7},{6,4},{7,5},{8,10},{9,11},{10,... | collective-permute-start | bytes 196616 | tf_op jit(solution)/shard_map/ppermute | solution.py:34
  73.6 1.5 %collective-permute-start.31 = (bf16[128,256]{1,0:T(8,128)(2,1)S(1)}, bf16[128,256]{1,0:T(8,128)(2,1)S(1)}, u32[]{:S(2)}, u32[]{:S(2)}) collective-permute-start(bf16[128,256]{1,0:T(8,128)(2,1)S(1)} %get-tuple-element.99), channel_id=1, source_target_pairs={{0,3},{1,2},{2,1},{3,0},{4,7},{5,6},{6,5},{7,4},{8,11},{9,10},{10,... | collective-permute-start | bytes 196616 | tf_op jit(solution)/shard_map/ppermute | solution.py:34
  75.1 1.9 %join.1 = bf16[256,4096]{1,0:T(8,128)(2,1)} custom-call(s32[2]{0:T(128)S(1)} %pad_add_fusion.place_ref, bf16[4,256,512]{2,1,0:T(8,128)(2,1)S(1)} %back.2.refs_0_, bf16[4,256,512]{2,1,0:T(8,128)(2,1)S(1)} %collective-permute-done.28.refs_1_), custom_call_target="tpu_custom_call" | custom-call | flops 1 | bytes 1 | tf_op jit(solution)/shard_map/join/pallas_call | solution.py:314
  77.0 3.0 %collective-permute-done.31 = bf16[128,256]{1,0:T(8,128)(2,1)S(1)} collective-permute-done((bf16[128,256]{1,0:T(8,128)(2,1)S(1)}, bf16[128,256]{1,0:T(8,128)(2,1)S(1)}, u32[]{:S(2)}, u32[]{:S(2)}) %collective-permute-start.31) | collective-permute-done | bytes 65568 | tf_op jit(solution)/shard_map/ppermute | solution.py:34
  (73 shorter events, 24.1 us)
Async XLA Ops:
  0.6 11.6 %collective-permute-start = (bf16[256,4096]{1,0:T(8,128)(2,1)}, bf16[256,4096]{1,0:T(8,128)(2,1)S(1)}, u32[]{:S(2)}, u32[]{:S(2)}) collective-permute-start(bf16[256,4096]{1,0:T(8,128)(2,1)} %x_hbm.1), channel_id=1, source_target_pairs={{0,4},{4,0},{8,12},{12,8},{16,20},{20,16},{24,28},{28,24},{1,5},{5... | collective-permute-start | bytes 6291464 | tf_op jit(solution)/shard_map/ppermute | solution.py:34
  1.1 13.3 %collective-permute-start.1 = (bf16[128,512]{1,0:T(8,128)(2,1)}, bf16[128,512]{1,0:T(8,128)(2,1)S(1)}, u32[]{:S(2)}, u32[]{:S(2)}) collective-permute-start(bf16[128,512]{1,0:T(8,128)(2,1)} %param.10), channel_id=1, source_target_pairs={{0,1},{1,0},{2,3},{3,2},{4,5},{5,4},{6,7},{7,6},{8,9},{9,8},{10,11... | collective-permute-start | bytes 393224 | tf_op jit(solution)/shard_map/ppermute | solution.py:34
  4.7 7.6 %collective-permute-start.3 = (bf16[128,256]{1,0:T(8,128)(2,1)S(1)}, bf16[128,256]{1,0:T(8,128)(2,1)S(1)}, u32[]{:S(2)}, u32[]{:S(2)}) collective-permute-start(bf16[128,256]{1,0:T(8,128)(2,1)S(1)} %get-tuple-element.103.refs_0_), channel_id=1, source_target_pairs={{0,3},{1,2},{2,1},{3,0},{4,7},{5,6},{6,5},{7,4},{8,11},{9,10},{10,... | collective-permute-start | bytes 196616 | tf_op jit(solution)/shard_map/ppermute | solution.py:34
  7.2 7.2 %collective-permute-start.2 = (bf16[128,256]{1,0:T(8,128)(2,1)S(1)}, bf16[128,256]{1,0:T(8,128)(2,1)S(1)}, u32[]{:S(2)}, u32[]{:S(2)}) collective-permute-start(bf16[128,256]{1,0:T(8,128)(2,1)S(1)} %get-tuple-element.103.refs_0_), channel_id=1, source_target_pairs={{0,2},{1,3},{2,0},{3,1},{4,6},{5,7},{6,4},{7,5},{8,10},{9,11},{10,... | collective-permute-start | bytes 196616 | tf_op jit(solution)/shard_map/ppermute | solution.py:34
  15.0 10.3 %collective-permute-start.6 = (bf16[4,128,256]{2,1,0:T(8,128)(2,1)S(1)}, bf16[4,128,256]{2,1,0:T(8,128)(2,1)S(1)}, u32[]{:S(2)}, u32[]{:S(2)}) collective-permute-start(bf16[4,128,256]{2,1,0:T(8,128)(2,1)S(1)} %line.2.refs_0_.refs_4_), channel_id=1, source_target_pairs={{0,24},{4,28},{8,16},{12,20},{16,8},{20,12},{24,0},{28,4},{1,25},{... | collective-permute-start | bytes 786440 | tf_op jit(solution)/shard_map/ppermute | solution.py:34
  17.5 13.6 %collective-permute-start.5 = (bf16[4,128,256]{2,1,0:T(8,128)(2,1)S(1)}, bf16[4,128,256]{2,1,0:T(8,128)(2,1)S(1)}, u32[]{:S(2)}, u32[]{:S(2)}) collective-permute-start(bf16[4,128,256]{2,1,0:T(8,128)(2,1)S(1)} %line.2.refs_0_.refs_4_), channel_id=1, source_target_pairs={{0,16},{4,20},{8,24},{12,28},{16,0},{20,4},{24,8},{28,12},{1,17},{... | collective-permute-start | bytes 786440 | tf_op jit(solution)/shard_map/ppermute | solution.py:34
  18.0 13.1 %collective-permute-start.4 = (bf16[4,128,256]{2,1,0:T(8,128)(2,1)S(1)}, bf16[4,128,256]{2,1,0:T(8,128)(2,1)S(1)}, u32[]{:S(2)}, u32[]{:S(2)}) collective-permute-start(bf16[4,128,256]{2,1,0:T(8,128)(2,1)S(1)} %line.2.refs_0_.refs_4_), channel_id=1, source_target_pairs={{0,8},{4,12},{8,0},{12,4},{16,24},{20,28},{24,16},{28,20},{1,9},{5... | collective-permute-start | bytes 786440 | tf_op jit(solution)/shard_map/ppermute | solution.py:34
  19.3 6.1 %collective-permute-start.12 = (bf16[128,256]{1,0:T(8,128)(2,1)S(1)}, bf16[128,256]{1,0:T(8,128)(2,1)S(1)}, u32[]{:S(2)}, u32[]{:S(2)}) collective-permute-start(bf16[128,256]{1,0:T(8,128)(2,1)S(1)} %get-tuple-element.65.refs_0_), channel_id=1, source_target_pairs={{0,3},{1,2},{2,1},{3,0},{4,7},{5,6},{6,5},{7,4},{8,11},{9,10},{10,... | collective-permute-start | bytes 196616 | tf_op jit(solution)/shard_map/ppermute | solution.py:34
  21.5 5.4 %collective-permute-start.11 = (bf16[128,256]{1,0:T(8,128)(2,1)S(1)}, bf16[128,256]{1,0:T(8,128)(2,1)S(1)}, u32[]{:S(2)}, u32[]{:S(2)}) collective-permute-start(bf16[128,256]{1,0:T(8,128)(2,1)S(1)} %get-tuple-element.65.refs_0_), channel_id=1, source_target_pairs={{0,2},{1,3},{2,0},{3,1},{4,6},{5,7},{6,4},{7,5},{8,10},{9,11},{10,... | collective-permute-start | bytes 196616 | tf_op jit(solution)/shard_map/ppermute | solution.py:34
  27.5 15.6 %collective-permute-start.15 = (bf16[4,128,256]{2,1,0:T(8,128)(2,1)S(1)}, bf16[4,128,256]{2,1,0:T(8,128)(2,1)S(1)}, u32[]{:S(2)}, u32[]{:S(2)}) collective-permute-start(bf16[4,128,256]{2,1,0:T(8,128)(2,1)S(1)} %line.3.refs_0_.refs_8_), channel_id=1, source_target_pairs={{0,24},{4,28},{8,16},{12,20},{16,8},{20,12},{24,0},{28,4},{1,25},{... | collective-permute-start | bytes 786440 | tf_op jit(solution)/shard_map/ppermute | solution.py:34
  30.0 13.6 %collective-permute-start.14 = (bf16[4,128,256]{2,1,0:T(8,128)(2,1)S(1)}, bf16[4,128,256]{2,1,0:T(8,128)(2,1)S(1)}, u32[]{:S(2)}, u32[]{:S(2)}) collective-permute-start(bf16[4,128,256]{2,1,0:T(8,128)(2,1)S(1)} %line.3.refs_0_.refs_8_), channel_id=1, source_target_pairs={{0,16},{4,20},{8,24},{12,28},{16,0},{20,4},{24,8},{28,12},{1,17},{... | collective-permute-start | bytes 786440 | tf_op jit(solution)/shard_map/ppermute | solution.py:34
  30.5 13.1 %collective-permute-start.13 = (bf16[4,128,256]{2,1,0:T(8,128)(2,1)S(1)}, bf16[4,128,256]{2,1,0:T(8,128)(2,1)S(1)}, u32[]{:S(2)}, u32[]{:S(2)}) collective-permute-start(bf16[4,128,256]{2,1,0:T(8,128)(2,1)S(1)} %line.3.refs_0_.refs_8_), channel_id=1, source_target_pairs={{0,8},{4,12},{8,0},{12,4},{16,24},{20,28},{24,16},{28,20},{1,9},{5... | collective-permute-start | bytes 786440 | tf_op jit(solution)/shard_map/ppermute | solution.py:34
  40.0 11.9 %collective-permute-start.20 = (bf16[4,128,256]{2,1,0:T(8,128)(2,1)S(1)}, bf16[4,128,256]{2,1,0:T(8,128)(2,1)S(1)}, u32[]{:S(2)}, u32[]{:S(2)}) collective-permute-start(bf16[4,128,256]{2,1,0:T(8,128)(2,1)S(1)} %get-tuple-element.79), channel_id=1, source_target_pairs={{0,8},{4,12},{8,0},{12,4},{16,24},{20,28},{24,16},{28,20},{1,9},{5... | collective-permute-start | bytes 786440 | tf_op jit(solution)/shard_map/ppermute | solution.py:34
  41.6 13.9 %collective-permute-start.21 = (bf16[4,128,256]{2,1,0:T(8,128)(2,1)S(1)}, bf16[4,128,256]{2,1,0:T(8,128)(2,1)S(1)}, u32[]{:S(2)}, u32[]{:S(2)}) collective-permute-start(bf16[4,128,256]{2,1,0:T(8,128)(2,1)S(1)} %get-tuple-element.80), channel_id=1, source_target_pairs={{0,16},{4,20},{8,24},{12,28},{16,0},{20,4},{24,8},{28,12},{1,17},{... | collective-permute-start | bytes 786440 | tf_op jit(solution)/shard_map/ppermute | solution.py:34
  43.1 12.4 %collective-permute-start.22 = (bf16[4,128,256]{2,1,0:T(8,128)(2,1)S(1)}, bf16[4,128,256]{2,1,0:T(8,128)(2,1)S(1)}, u32[]{:S(2)}, u32[]{:S(2)}) collective-permute-start(bf16[4,128,256]{2,1,0:T(8,128)(2,1)S(1)} %get-tuple-element.81), channel_id=1, source_target_pairs={{0,24},{4,28},{8,16},{12,20},{16,8},{20,12},{24,0},{28,4},{1,25},{... | collective-permute-start | bytes 786440 | tf_op jit(solution)/shard_map/ppermute | solution.py:34
  55.5 10.9 %collective-permute-start.25 = (bf16[4,128,256]{2,1,0:T(8,128)(2,1)S(1)}, bf16[4,128,256]{2,1,0:T(8,128)(2,1)S(1)}, u32[]{:S(2)}, u32[]{:S(2)}) collective-permute-start(bf16[4,128,256]{2,1,0:T(8,128)(2,1)S(1)} %get-tuple-element.86), channel_id=1, source_target_pairs={{0,8},{4,12},{8,0},{12,4},{16,24},{20,28},{24,16},{28,20},{1,9},{5... | collective-permute-start | bytes 786440 | tf_op jit(solution)/shard_map/ppermute | solution.py:34
  56.7 13.1 %collective-permute-start.26 = (bf16[4,128,256]{2,1,0:T(8,128)(2,1)S(1)}, bf16[4,128,256]{2,1,0:T(8,128)(2,1)S(1)}, u32[]{:S(2)}, u32[]{:S(2)}) collective-permute-start(bf16[4,128,256]{2,1,0:T(8,128)(2,1)S(1)} %get-tuple-element.88), channel_id=1, source_target_pairs={{0,16},{4,20},{8,24},{12,28},{16,0},{20,4},{24,8},{28,12},{1,17},{... | collective-permute-start | bytes 786440 | tf_op jit(solution)/shard_map/ppermute | solution.py:34
  57.6 12.3 %collective-permute-start.27 = (bf16[4,128,256]{2,1,0:T(8,128)(2,1)S(1)}, bf16[4,128,256]{2,1,0:T(8,128)(2,1)S(1)}, u32[]{:S(2)}, u32[]{:S(2)}) collective-permute-start(bf16[4,128,256]{2,1,0:T(8,128)(2,1)S(1)} %get-tuple-element.90), channel_id=1, source_target_pairs={{0,24},{4,28},{8,16},{12,20},{16,8},{20,12},{24,0},{28,4},{1,25},{... | collective-permute-start | bytes 786440 | tf_op jit(solution)/shard_map/ppermute | solution.py:34
  59.7 6.0 %collective-permute-start.23 = (bf16[128,256]{1,0:T(8,128)(2,1)S(1)}, bf16[128,256]{1,0:T(8,128)(2,1)S(1)}, u32[]{:S(2)}, u32[]{:S(2)}) collective-permute-start(bf16[128,256]{1,0:T(8,128)(2,1)S(1)} %get-tuple-element.82), channel_id=1, source_target_pairs={{0,2},{1,3},{2,0},{3,1},{4,6},{5,7},{6,4},{7,5},{8,10},{9,11},{10,... | collective-permute-start | bytes 196616 | tf_op jit(solution)/shard_map/ppermute | solution.py:34
  60.2 6.2 %collective-permute-start.24 = (bf16[128,256]{1,0:T(8,128)(2,1)S(1)}, bf16[128,256]{1,0:T(8,128)(2,1)S(1)}, u32[]{:S(2)}, u32[]{:S(2)}) collective-permute-start(bf16[128,256]{1,0:T(8,128)(2,1)S(1)} %get-tuple-element.83), channel_id=1, source_target_pairs={{0,3},{1,2},{2,1},{3,0},{4,7},{5,6},{6,5},{7,4},{8,11},{9,10},{10,... | collective-permute-start | bytes 196616 | tf_op jit(solution)/shard_map/ppermute | solution.py:34
  70.5 4.5 %collective-permute-start.28 = (bf16[4,256,512]{2,1,0:T(8,128)(2,1)S(1)}, bf16[4,256,512]{2,1,0:T(8,128)(2,1)S(1)}, u32[]{:S(2)}, u32[]{:S(2)}) collective-permute-start(bf16[4,256,512]{2,1,0:T(8,128)(2,1)S(1)} %back.3), channel_id=1, source_target_pairs={{0,4},{4,0},{8,12},{12,8},{16,20},{20,16},{24,28},{28,24},{1,5},{5... | collective-permute-start | bytes 3145736 | tf_op jit(solution)/shard_map/ppermute | solution.py:34
  70.6 9.4 %collective-permute-start.29 = (bf16[128,512]{1,0:T(8,128)(2,1)S(1)}, bf16[128,512]{1,0:T(8,128)(2,1)S(1)}, u32[]{:S(2)}, u32[]{:S(2)}) collective-permute-start(bf16[128,512]{1,0:T(8,128)(2,1)S(1)} %get-tuple-element.96), channel_id=1, source_target_pairs={{0,1},{1,0},{2,3},{3,2},{4,5},{5,4},{6,7},{7,6},{8,9},{9,8},{10,11... | collective-permute-start | bytes 393224 | tf_op jit(solution)/shard_map/ppermute | solution.py:34
  70.7 6.3 %collective-permute-start.30 = (bf16[128,256]{1,0:T(8,128)(2,1)S(1)}, bf16[128,256]{1,0:T(8,128)(2,1)S(1)}, u32[]{:S(2)}, u32[]{:S(2)}) collective-permute-start(bf16[128,256]{1,0:T(8,128)(2,1)S(1)} %get-tuple-element.98), channel_id=1, source_target_pairs={{0,2},{1,3},{2,0},{3,1},{4,6},{5,7},{6,4},{7,5},{8,10},{9,11},{10,... | collective-permute-start | bytes 196616 | tf_op jit(solution)/shard_map/ppermute | solution.py:34
  73.6 6.4 %collective-permute-start.31 = (bf16[128,256]{1,0:T(8,128)(2,1)S(1)}, bf16[128,256]{1,0:T(8,128)(2,1)S(1)}, u32[]{:S(2)}, u32[]{:S(2)}) collective-permute-start(bf16[128,256]{1,0:T(8,128)(2,1)S(1)} %get-tuple-element.99), channel_id=1, source_target_pairs={{0,3},{1,2},{2,1},{3,0},{4,7},{5,6},{6,5},{7,4},{8,11},{9,10},{10,... | collective-permute-start | bytes 196616 | tf_op jit(solution)/shard_map/ppermute | solution.py:34
  (12 other events, 23.0 us)

commit v4 on v3

--- a/solution.py
+++ b/solution.py
@@ -376,7 +376,7 @@
         outs = list(terms(locs, place, own_turned, sib_turned, gks[-1], sib_gks[-1]))
         if pair + 1 < PAIRS:
             raw, sib_raw = raw_of(pair + 1, outs[0])
-        sends = [after(out, *parts[1:]) if pair else out for out in outs]
+        sends = [after(out, *parts[1:]) if pair and m == chips - 1 else out for m, out in enumerate(outs)]
         parts = outs[:1] + [flip(sends[m], "node", 2 * m, nodes) for m in range(1, chips)]
         if pair + 1 == PAIRS:
             theirs, mine = (

time: 81 us -> 78.4 us (0.968)
  waiting for transfers between devices: 23.6 us -> 20 us
  starting transfers between devices: 31.6 us -> 32.7 us
    ppermute x32, waiting for transfers between devices: 23.6 us -> 20 us  [flip(): return lax.ppermute(x, axis, [(i, i ^ mask) for i in range(size)])]
    ppermute x32, starting transfers between devices: 31.6 us -> 32.7 us  [flip(): return lax.ppermute(x, axis, [(i, i ^ mask) for i in range(size)])]
  transfers between devices with their start and end apart: 32 -> 32, of which waited for: 13 -> 12; matrix products, arithmetic and copies ran while one was open for 3% -> 3% of each run, Pallas kernels for 25% -> 26%
where the time goes in v4:
time: 78.4 us; the launch traced here: 78.2 us
  starting transfers between devices  32.7 us (42%)
  Pallas kernels  21.6 us (28%)
  waiting for transfers between devices  20 us (26%)
  other arithmetic  2.22 us (3%)
  between operations  0.92 us (1%)
  local copies, waits for them, and re-layouts  0.91 us (1%)
    ppermute x32, starting transfers between devices, flip(): return lax.ppermute(x, axis, [(i, i ^ mask) for i in range(size)])  32.7 us
    ppermute x32, waiting for transfers between devices, flip(): return lax.ppermute(x, axis, [(i, i ^ mask) for i in range(size)])  20 us
    pallas_call x2, Pallas kernels, attend(): pl.pallas_call(functools.partial(attend_kernel, pair, heads, group), out_...  5.79 us
    pallas_call x4, Pallas kernels, raw_terms(): pl.pallas_call(raw_kernel, out_shape=[jax.ShapeDtypeStruct((count, HEAD_S...  3.91 us
    pallas_call x2, Pallas kernels, back(): pl.pallas_call(functools.partial(back_kernel, pairs, heads, parts), out_s...  2.57 us
    pallas_call x2, Pallas kernels, terms(): pl.pallas_call(functools.partial(terms_kernel, heads), out_shape=outs, in...  2.49 us
    pallas_call x1, Pallas kernels, join(): pl.pallas_call(join_kernel, out_shape=jax.ShapeDtypeStruct((count, 2 * ch...  1.93 us
    pallas_call x1, Pallas kernels, cut(): pl.pallas_call(cut_kernel, out_shape=[jax.ShapeDtypeStruct((chips, count,...  1.83 us
  transfers between devices with their start and end apart: 32, of which 12 were waited for; matrix products, arithmetic and copies ran while one was open for 3% of the time, Pallas kernels for 26%

profile of v4, /device:TPU:0, one launch (start us, length us, event | category | flops | bytes accessed | tf_op | source)
XLA Modules:
  0.0 78.2 jit_solution(3394027270791978491)
XLA Ops:
  1.1 2.7 %collective-permute-start.1 = (bf16[128,512]{1,0:T(8,128)(2,1)}, bf16[128,512]{1,0:T(8,128)(2,1)S(1)}, u32[]{:S(2)}, u32[]{:S(2)}) collective-permute-start(bf16[128,512]{1,0:T(8,128)(2,1)} %param.10), channel_id=1, source_target_pairs={{0,1},{1,0},{2,3},{3,2},{4,5},{5,4},{6,7},{7,6},{8,9},{9,8},{10,11... | collective-permute-start | bytes 393224 | tf_op jit(solution)/shard_map/ppermute | solution.py:34
  4.7 2.5 %collective-permute-start.3 = (bf16[128,256]{1,0:T(8,128)(2,1)S(1)}, bf16[128,256]{1,0:T(8,128)(2,1)S(1)}, u32[]{:S(2)}, u32[]{:S(2)}) collective-permute-start(bf16[128,256]{1,0:T(8,128)(2,1)S(1)} %get-tuple-element.99.refs_0_), channel_id=1, source_target_pairs={{0,3},{1,2},{2,1},{3,0},{4,7},{5,6},{6,5},{7,4},{8,11},{9,10},{10,... | collective-permute-start | bytes 196616 | tf_op jit(solution)/shard_map/ppermute | solution.py:34
  7.5 4.8 %collective-permute-done.3.refs_3_ = bf16[128,256]{1,0:T(8,128)(2,1)S(1)} collective-permute-done((bf16[128,256]{1,0:T(8,128)(2,1)S(1)}, bf16[128,256]{1,0:T(8,128)(2,1)S(1)}, u32[]{:S(2)}, u32[]{:S(2)}) %collective-permute-start.3) | collective-permute-done | bytes 65568 | tf_op jit(solution)/shard_map/ppermute | solution.py:34
  12.3 2.2 %collective-permute-done.2.refs_2_ = bf16[128,256]{1,0:T(8,128)(2,1)S(1)} collective-permute-done((bf16[128,256]{1,0:T(8,128)(2,1)S(1)}, bf16[128,256]{1,0:T(8,128)(2,1)S(1)}, u32[]{:S(2)}, u32[]{:S(2)}) %collective-permute-start.2) | collective-permute-done | bytes 65568 | tf_op jit(solution)/shard_map/ppermute | solution.py:34
  15.0 2.5 %collective-permute-start.6 = (bf16[4,128,256]{2,1,0:T(8,128)(2,1)S(1)}, bf16[4,128,256]{2,1,0:T(8,128)(2,1)S(1)}, u32[]{:S(2)}, u32[]{:S(2)}) collective-permute-start(bf16[4,128,256]{2,1,0:T(8,128)(2,1)S(1)} %line.2.refs_0_.refs_4_), channel_id=1, source_target_pairs={{0,24},{4,28},{8,16},{12,20},{16,8},{20,12},{24,0},{28,4},{1,25},{... | collective-permute-start | bytes 786440 | tf_op jit(solution)/shard_map/ppermute | solution.py:34
  19.3 2.3 %collective-permute-start.12 = (bf16[128,256]{1,0:T(8,128)(2,1)S(1)}, bf16[128,256]{1,0:T(8,128)(2,1)S(1)}, u32[]{:S(2)}, u32[]{:S(2)}) collective-permute-start(bf16[128,256]{1,0:T(8,128)(2,1)S(1)} %get-tuple-element.63.refs_0_), channel_id=1, source_target_pairs={{0,3},{1,2},{2,1},{3,0},{4,7},{5,6},{6,5},{7,4},{8,11},{9,10},{10,... | collective-permute-start | bytes 196616 | tf_op jit(solution)/shard_map/ppermute | solution.py:34
  21.5 1.8 %cut.1 = (bf16[4,256,512]{2,1,0:T(8,128)(2,1)S(1)}, bf16[4,256,512]{2,1,0:T(8,128)(2,1)S(1)}) custom-call(s32[2]{0:T(128)S(1)} %pad_add_fusion.place_ref, bf16[256,4096]{1,0:T(8,128)(2,1)} %x_hbm.1, bf16[256,4096]{1,0:T(8,128)(2,1)S(1)} %collective-permute-done.sib_hbm), custom_call_target="tpu_custom_call" | custom-call | flops 1 | bytes 1 | tf_op jit(solution)/shard_map/cut/pallas_call | solution.py:276
  23.4 2.0 %collective-permute-done.12.refs_3_ = bf16[128,256]{1,0:T(8,128)(2,1)S(1)} collective-permute-done((bf16[128,256]{1,0:T(8,128)(2,1)S(1)}, bf16[128,256]{1,0:T(8,128)(2,1)S(1)}, u32[]{:S(2)}, u32[]{:S(2)}) %collective-permute-start.12) | collective-permute-done | bytes 65568 | tf_op jit(solution)/shard_map/ppermute | solution.py:34
  25.3 1.6 %collective-permute-done.11.refs_2_ = bf16[128,256]{1,0:T(8,128)(2,1)S(1)} collective-permute-done((bf16[128,256]{1,0:T(8,128)(2,1)S(1)}, bf16[128,256]{1,0:T(8,128)(2,1)S(1)}, u32[]{:S(2)}, u32[]{:S(2)}) %collective-permute-start.11) | collective-permute-done | bytes 65568 | tf_op jit(solution)/shard_map/ppermute | solution.py:34
  27.5 2.5 %collective-permute-start.15 = (bf16[4,128,256]{2,1,0:T(8,128)(2,1)S(1)}, bf16[4,128,256]{2,1,0:T(8,128)(2,1)S(1)}, u32[]{:S(2)}, u32[]{:S(2)}) collective-permute-start(bf16[4,128,256]{2,1,0:T(8,128)(2,1)S(1)} %line.3.refs_0_.refs_8_), channel_id=1, source_target_pairs={{0,24},{4,28},{8,16},{12,20},{16,8},{20,12},{24,0},{28,4},{1,25},{... | collective-permute-start | bytes 786440 | tf_op jit(solution)/shard_map/ppermute | solution.py:34
  34.4 2.9 %attend.2 = (bf16[256,128]{1,0:T(8,128)(2,1)S(1)}, bf16[256,128]{1,0:T(8,128)(2,1)S(1)}) custom-call(s32[1,256]{1,0:T(1,128)S(1)} %bitcast.3, f32[256,128]{1,0:T(8,128)S(1)} %get-tuple-element.103.cos_ref, f32[256,128]{1,0:T(8,128)S(1)} %get-tuple-element.104.sin_ref, f32[256,128]{1,0:T(8,128)S(1)} %get-tuple-element.52.refs_0_, ...), custom_call_target="tpu_custom_call" | custom-call | flops 1 | bytes 1 | tf_op jit(solution)/shard_map/attend/pallas_call | solution.py:151
  40.0 1.6 %collective-permute-start.20 = (bf16[4,128,256]{2,1,0:T(8,128)(2,1)S(1)}, bf16[4,128,256]{2,1,0:T(8,128)(2,1)S(1)}, u32[]{:S(2)}, u32[]{:S(2)}) collective-permute-start(bf16[4,128,256]{2,1,0:T(8,128)(2,1)S(1)} %get-tuple-element.77), channel_id=1, source_target_pairs={{0,8},{4,12},{8,0},{12,4},{16,24},{20,28},{24,16},{28,20},{1,9},{5... | collective-permute-start | bytes 786440 | tf_op jit(solution)/shard_map/ppermute | solution.py:34
  41.6 1.5 %collective-permute-start.21 = (bf16[4,128,256]{2,1,0:T(8,128)(2,1)S(1)}, bf16[4,128,256]{2,1,0:T(8,128)(2,1)S(1)}, u32[]{:S(2)}, u32[]{:S(2)}) collective-permute-start(bf16[4,128,256]{2,1,0:T(8,128)(2,1)S(1)} %get-tuple-element.78), channel_id=1, source_target_pairs={{0,16},{4,20},{8,24},{12,28},{16,0},{20,4},{24,8},{28,12},{1,17},{... | collective-permute-start | bytes 786440 | tf_op jit(solution)/shard_map/ppermute | solution.py:34
  46.2 2.9 %attend.3 = (bf16[256,128]{1,0:T(8,128)(2,1)S(1)}, bf16[256,128]{1,0:T(8,128)(2,1)S(1)}) custom-call(s32[1,256]{1,0:T(1,128)S(1)} %bitcast.4, f32[256,128]{1,0:T(8,128)S(1)} %get-tuple-element.103.cos_ref, f32[256,128]{1,0:T(8,128)S(1)} %get-tuple-element.104.sin_ref, f32[256,128]{1,0:T(8,128)S(1)} %get-tuple-element.65.refs_0_, ...), custom_call_target="tpu_custom_call" | custom-call | flops 1 | bytes 1 | tf_op jit(solution)/shard_map/attend/pallas_call | solution.py:151
  52.0 1.6 %collective-permute-start.25 = (bf16[4,128,256]{2,1,0:T(8,128)(2,1)S(1)}, bf16[4,128,256]{2,1,0:T(8,128)(2,1)S(1)}, u32[]{:S(2)}, u32[]{:S(2)}) collective-permute-start(bf16[4,128,256]{2,1,0:T(8,128)(2,1)S(1)} %get-tuple-element.83), channel_id=1, source_target_pairs={{0,8},{4,12},{8,0},{12,4},{16,24},{20,28},{24,16},{28,20},{1,9},{5... | collective-permute-start | bytes 786440 | tf_op jit(solution)/shard_map/ppermute | solution.py:34
  53.6 1.5 %collective-permute-start.26 = (bf16[4,128,256]{2,1,0:T(8,128)(2,1)S(1)}, bf16[4,128,256]{2,1,0:T(8,128)(2,1)S(1)}, u32[]{:S(2)}, u32[]{:S(2)}) collective-permute-start(bf16[4,128,256]{2,1,0:T(8,128)(2,1)S(1)} %get-tuple-element.84), channel_id=1, source_target_pairs={{0,16},{4,20},{8,24},{12,28},{16,0},{20,4},{24,8},{28,12},{1,17},{... | collective-permute-start | bytes 786440 | tf_op jit(solution)/shard_map/ppermute | solution.py:34
  55.5 1.5 %collective-permute-start.27 = (bf16[4,128,256]{2,1,0:T(8,128)(2,1)S(1)}, bf16[4,128,256]{2,1,0:T(8,128)(2,1)S(1)}, u32[]{:S(2)}, u32[]{:S(2)}) collective-permute-start(bf16[4,128,256]{2,1,0:T(8,128)(2,1)S(1)} %get-tuple-element.86), channel_id=1, source_target_pairs={{0,24},{4,28},{8,16},{12,20},{16,8},{20,12},{24,0},{28,4},{1,25},{... | collective-permute-start | bytes 786440 | tf_op jit(solution)/shard_map/ppermute | solution.py:34
  58.2 1.9 %collective-permute-start.24 = (bf16[128,256]{1,0:T(8,128)(2,1)S(1)}, bf16[128,256]{1,0:T(8,128)(2,1)S(1)}, u32[]{:S(2)}, u32[]{:S(2)}) collective-permute-start(bf16[128,256]{1,0:T(8,128)(2,1)S(1)} %get-tuple-element.81), channel_id=1, source_target_pairs={{0,3},{1,2},{2,1},{3,0},{4,7},{5,6},{6,5},{7,4},{8,11},{9,10},{10,... | collective-permute-start | bytes 196616 | tf_op jit(solution)/shard_map/ppermute | solution.py:34
  62.7 2.1 %collective-permute-done.23 = bf16[128,256]{1,0:T(8,128)(2,1)S(1)} collective-permute-done((bf16[128,256]{1,0:T(8,128)(2,1)S(1)}, bf16[128,256]{1,0:T(8,128)(2,1)S(1)}, u32[]{:S(2)}, u32[]{:S(2)}) %collective-permute-start.23) | collective-permute-done | bytes 65568 | tf_op jit(solution)/shard_map/ppermute | solution.py:34
  64.9 2.4 %collective-permute-done.26.refs_2_ = bf16[4,128,256]{2,1,0:T(8,128)(2,1)S(1)} collective-permute-done((bf16[4,128,256]{2,1,0:T(8,128)(2,1)S(1)}, bf16[4,128,256]{2,1,0:T(8,128)(2,1)S(1)}, u32[]{:S(2)}, u32[]{:S(2)}) %collective-permute-start.26) | collective-permute-done | bytes 262176 | tf_op jit(solution)/shard_map/ppermute | solution.py:34
  68.1 2.9 %collective-permute-start.30 = (bf16[128,256]{1,0:T(8,128)(2,1)S(1)}, bf16[128,256]{1,0:T(8,128)(2,1)S(1)}, u32[]{:S(2)}, u32[]{:S(2)}) collective-permute-start(bf16[128,256]{1,0:T(8,128)(2,1)S(1)} %get-tuple-element.94), channel_id=1, source_target_pairs={{0,2},{1,3},{2,0},{3,1},{4,6},{5,7},{6,4},{7,5},{8,10},{9,11},{10,... | collective-permute-start | bytes 196616 | tf_op jit(solution)/shard_map/ppermute | solution.py:34
  71.0 1.5 %collective-permute-start.31 = (bf16[128,256]{1,0:T(8,128)(2,1)S(1)}, bf16[128,256]{1,0:T(8,128)(2,1)S(1)}, u32[]{:S(2)}, u32[]{:S(2)}) collective-permute-start(bf16[128,256]{1,0:T(8,128)(2,1)S(1)} %get-tuple-element.95), channel_id=1, source_target_pairs={{0,3},{1,2},{2,1},{3,0},{4,7},{5,6},{6,5},{7,4},{8,11},{9,10},{10,... | collective-permute-start | bytes 196616 | tf_op jit(solution)/shard_map/ppermute | solution.py:34
  72.5 1.9 %join.1 = bf16[256,4096]{1,0:T(8,128)(2,1)} custom-call(s32[2]{0:T(128)S(1)} %pad_add_fusion.place_ref, bf16[4,256,512]{2,1,0:T(8,128)(2,1)S(1)} %back.2.refs_0_, bf16[4,256,512]{2,1,0:T(8,128)(2,1)S(1)} %collective-permute-done.28.refs_1_), custom_call_target="tpu_custom_call" | custom-call | flops 1 | bytes 1 | tf_op jit(solution)/shard_map/join/pallas_call | solution.py:314
  74.5 3.0 %collective-permute-done.31 = bf16[128,256]{1,0:T(8,128)(2,1)S(1)} collective-permute-done((bf16[128,256]{1,0:T(8,128)(2,1)S(1)}, bf16[128,256]{1,0:T(8,128)(2,1)S(1)}, u32[]{:S(2)}, u32[]{:S(2)}) %collective-permute-start.31) | collective-permute-done | bytes 65568 | tf_op jit(solution)/shard_map/ppermute | solution.py:34
  (73 shorter events, 23.3 us)
Async XLA Ops:
  0.6 11.6 %collective-permute-start = (bf16[256,4096]{1,0:T(8,128)(2,1)}, bf16[256,4096]{1,0:T(8,128)(2,1)S(1)}, u32[]{:S(2)}, u32[]{:S(2)}) collective-permute-start(bf16[256,4096]{1,0:T(8,128)(2,1)} %x_hbm.1), channel_id=1, source_target_pairs={{0,4},{4,0},{8,12},{12,8},{16,20},{20,16},{24,28},{28,24},{1,5},{5... | collective-permute-start | bytes 6291464 | tf_op jit(solution)/shard_map/ppermute | solution.py:34
  1.1 13.3 %collective-permute-start.1 = (bf16[128,512]{1,0:T(8,128)(2,1)}, bf16[128,512]{1,0:T(8,128)(2,1)S(1)}, u32[]{:S(2)}, u32[]{:S(2)}) collective-permute-start(bf16[128,512]{1,0:T(8,128)(2,1)} %param.10), channel_id=1, source_target_pairs={{0,1},{1,0},{2,3},{3,2},{4,5},{5,4},{6,7},{7,6},{8,9},{9,8},{10,11... | collective-permute-start | bytes 393224 | tf_op jit(solution)/shard_map/ppermute | solution.py:34
  4.7 7.6 %collective-permute-start.3 = (bf16[128,256]{1,0:T(8,128)(2,1)S(1)}, bf16[128,256]{1,0:T(8,128)(2,1)S(1)}, u32[]{:S(2)}, u32[]{:S(2)}) collective-permute-start(bf16[128,256]{1,0:T(8,128)(2,1)S(1)} %get-tuple-element.99.refs_0_), channel_id=1, source_target_pairs={{0,3},{1,2},{2,1},{3,0},{4,7},{5,6},{6,5},{7,4},{8,11},{9,10},{10,... | collective-permute-start | bytes 196616 | tf_op jit(solution)/shard_map/ppermute | solution.py:34
  7.2 7.2 %collective-permute-start.2 = (bf16[128,256]{1,0:T(8,128)(2,1)S(1)}, bf16[128,256]{1,0:T(8,128)(2,1)S(1)}, u32[]{:S(2)}, u32[]{:S(2)}) collective-permute-start(bf16[128,256]{1,0:T(8,128)(2,1)S(1)} %get-tuple-element.99.refs_0_), channel_id=1, source_target_pairs={{0,2},{1,3},{2,0},{3,1},{4,6},{5,7},{6,4},{7,5},{8,10},{9,11},{10,... | collective-permute-start | bytes 196616 | tf_op jit(solution)/shard_map/ppermute | solution.py:34
  15.0 10.3 %collective-permute-start.6 = (bf16[4,128,256]{2,1,0:T(8,128)(2,1)S(1)}, bf16[4,128,256]{2,1,0:T(8,128)(2,1)S(1)}, u32[]{:S(2)}, u32[]{:S(2)}) collective-permute-start(bf16[4,128,256]{2,1,0:T(8,128)(2,1)S(1)} %line.2.refs_0_.refs_4_), channel_id=1, source_target_pairs={{0,24},{4,28},{8,16},{12,20},{16,8},{20,12},{24,0},{28,4},{1,25},{... | collective-permute-start | bytes 786440 | tf_op jit(solution)/shard_map/ppermute | solution.py:34
  17.5 13.6 %collective-permute-start.5 = (bf16[4,128,256]{2,1,0:T(8,128)(2,1)S(1)}, bf16[4,128,256]{2,1,0:T(8,128)(2,1)S(1)}, u32[]{:S(2)}, u32[]{:S(2)}) collective-permute-start(bf16[4,128,256]{2,1,0:T(8,128)(2,1)S(1)} %line.2.refs_0_.refs_4_), channel_id=1, source_target_pairs={{0,16},{4,20},{8,24},{12,28},{16,0},{20,4},{24,8},{28,12},{1,17},{... | collective-permute-start | bytes 786440 | tf_op jit(solution)/shard_map/ppermute | solution.py:34
  18.0 13.1 %collective-permute-start.4 = (bf16[4,128,256]{2,1,0:T(8,128)(2,1)S(1)}, bf16[4,128,256]{2,1,0:T(8,128)(2,1)S(1)}, u32[]{:S(2)}, u32[]{:S(2)}) collective-permute-start(bf16[4,128,256]{2,1,0:T(8,128)(2,1)S(1)} %line.2.refs_0_.refs_4_), channel_id=1, source_target_pairs={{0,8},{4,12},{8,0},{12,4},{16,24},{20,28},{24,16},{28,20},{1,9},{5... | collective-permute-start | bytes 786440 | tf_op jit(solution)/shard_map/ppermute | solution.py:34
  19.3 6.1 %collective-permute-start.12 = (bf16[128,256]{1,0:T(8,128)(2,1)S(1)}, bf16[128,256]{1,0:T(8,128)(2,1)S(1)}, u32[]{:S(2)}, u32[]{:S(2)}) collective-permute-start(bf16[128,256]{1,0:T(8,128)(2,1)S(1)} %get-tuple-element.63.refs_0_), channel_id=1, source_target_pairs={{0,3},{1,2},{2,1},{3,0},{4,7},{5,6},{6,5},{7,4},{8,11},{9,10},{10,... | collective-permute-start | bytes 196616 | tf_op jit(solution)/shard_map/ppermute | solution.py:34
  21.5 5.4 %collective-permute-start.11 = (bf16[128,256]{1,0:T(8,128)(2,1)S(1)}, bf16[128,256]{1,0:T(8,128)(2,1)S(1)}, u32[]{:S(2)}, u32[]{:S(2)}) collective-permute-start(bf16[128,256]{1,0:T(8,128)(2,1)S(1)} %get-tuple-element.63.refs_0_), channel_id=1, source_target_pairs={{0,2},{1,3},{2,0},{3,1},{4,6},{5,7},{6,4},{7,5},{8,10},{9,11},{10,... | collective-permute-start | bytes 196616 | tf_op jit(solution)/shard_map/ppermute | solution.py:34
  27.5 15.6 %collective-permute-start.15 = (bf16[4,128,256]{2,1,0:T(8,128)(2,1)S(1)}, bf16[4,128,256]{2,1,0:T(8,128)(2,1)S(1)}, u32[]{:S(2)}, u32[]{:S(2)}) collective-permute-start(bf16[4,128,256]{2,1,0:T(8,128)(2,1)S(1)} %line.3.refs_0_.refs_8_), channel_id=1, source_target_pairs={{0,24},{4,28},{8,16},{12,20},{16,8},{20,12},{24,0},{28,4},{1,25},{... | collective-permute-start | bytes 786440 | tf_op jit(solution)/shard_map/ppermute | solution.py:34
  30.0 13.6 %collective-permute-start.14 = (bf16[4,128,256]{2,1,0:T(8,128)(2,1)S(1)}, bf16[4,128,256]{2,1,0:T(8,128)(2,1)S(1)}, u32[]{:S(2)}, u32[]{:S(2)}) collective-permute-start(bf16[4,128,256]{2,1,0:T(8,128)(2,1)S(1)} %line.3.refs_0_.refs_8_), channel_id=1, source_target_pairs={{0,16},{4,20},{8,24},{12,28},{16,0},{20,4},{24,8},{28,12},{1,17},{... | collective-permute-start | bytes 786440 | tf_op jit(solution)/shard_map/ppermute | solution.py:34
  30.5 13.1 %collective-permute-start.13 = (bf16[4,128,256]{2,1,0:T(8,128)(2,1)S(1)}, bf16[4,128,256]{2,1,0:T(8,128)(2,1)S(1)}, u32[]{:S(2)}, u32[]{:S(2)}) collective-permute-start(bf16[4,128,256]{2,1,0:T(8,128)(2,1)S(1)} %line.3.refs_0_.refs_8_), channel_id=1, source_target_pairs={{0,8},{4,12},{8,0},{12,4},{16,24},{20,28},{24,16},{28,20},{1,9},{5... | collective-permute-start | bytes 786440 | tf_op jit(solution)/shard_map/ppermute | solution.py:34
  40.0 15.0 %collective-permute-start.20 = (bf16[4,128,256]{2,1,0:T(8,128)(2,1)S(1)}, bf16[4,128,256]{2,1,0:T(8,128)(2,1)S(1)}, u32[]{:S(2)}, u32[]{:S(2)}) collective-permute-start(bf16[4,128,256]{2,1,0:T(8,128)(2,1)S(1)} %get-tuple-element.77), channel_id=1, source_target_pairs={{0,8},{4,12},{8,0},{12,4},{16,24},{20,28},{24,16},{28,20},{1,9},{5... | collective-permute-start | bytes 786440 | tf_op jit(solution)/shard_map/ppermute | solution.py:34
  41.6 13.9 %collective-permute-start.21 = (bf16[4,128,256]{2,1,0:T(8,128)(2,1)S(1)}, bf16[4,128,256]{2,1,0:T(8,128)(2,1)S(1)}, u32[]{:S(2)}, u32[]{:S(2)}) collective-permute-start(bf16[4,128,256]{2,1,0:T(8,128)(2,1)S(1)} %get-tuple-element.78), channel_id=1, source_target_pairs={{0,16},{4,20},{8,24},{12,28},{16,0},{20,4},{24,8},{28,12},{1,17},{... | collective-permute-start | bytes 786440 | tf_op jit(solution)/shard_map/ppermute | solution.py:34
  43.1 12.4 %collective-permute-start.22 = (bf16[4,128,256]{2,1,0:T(8,128)(2,1)S(1)}, bf16[4,128,256]{2,1,0:T(8,128)(2,1)S(1)}, u32[]{:S(2)}, u32[]{:S(2)}) collective-permute-start(bf16[4,128,256]{2,1,0:T(8,128)(2,1)S(1)} %get-tuple-element.79), channel_id=1, source_target_pairs={{0,24},{4,28},{8,16},{12,20},{16,8},{20,12},{24,0},{28,4},{1,25},{... | collective-permute-start | bytes 786440 | tf_op jit(solution)/shard_map/ppermute | solution.py:34
  52.0 12.9 %collective-permute-start.25 = (bf16[4,128,256]{2,1,0:T(8,128)(2,1)S(1)}, bf16[4,128,256]{2,1,0:T(8,128)(2,1)S(1)}, u32[]{:S(2)}, u32[]{:S(2)}) collective-permute-start(bf16[4,128,256]{2,1,0:T(8,128)(2,1)S(1)} %get-tuple-element.83), channel_id=1, source_target_pairs={{0,8},{4,12},{8,0},{12,4},{16,24},{20,28},{24,16},{28,20},{1,9},{5... | collective-permute-start | bytes 786440 | tf_op jit(solution)/shard_map/ppermute | solution.py:34
  53.6 13.7 %collective-permute-start.26 = (bf16[4,128,256]{2,1,0:T(8,128)(2,1)S(1)}, bf16[4,128,256]{2,1,0:T(8,128)(2,1)S(1)}, u32[]{:S(2)}, u32[]{:S(2)}) collective-permute-start(bf16[4,128,256]{2,1,0:T(8,128)(2,1)S(1)} %get-tuple-element.84), channel_id=1, source_target_pairs={{0,16},{4,20},{8,24},{12,28},{16,0},{20,4},{24,8},{28,12},{1,17},{... | collective-permute-start | bytes 786440 | tf_op jit(solution)/shard_map/ppermute | solution.py:34
  55.5 11.8 %collective-permute-start.27 = (bf16[4,128,256]{2,1,0:T(8,128)(2,1)S(1)}, bf16[4,128,256]{2,1,0:T(8,128)(2,1)S(1)}, u32[]{:S(2)}, u32[]{:S(2)}) collective-permute-start(bf16[4,128,256]{2,1,0:T(8,128)(2,1)S(1)} %get-tuple-element.86), channel_id=1, source_target_pairs={{0,24},{4,28},{8,16},{12,20},{16,8},{20,12},{24,0},{28,4},{1,25},{... | collective-permute-start | bytes 786440 | tf_op jit(solution)/shard_map/ppermute | solution.py:34
  57.7 7.2 %collective-permute-start.23 = (bf16[128,256]{1,0:T(8,128)(2,1)S(1)}, bf16[128,256]{1,0:T(8,128)(2,1)S(1)}, u32[]{:S(2)}, u32[]{:S(2)}) collective-permute-start(bf16[128,256]{1,0:T(8,128)(2,1)S(1)} %get-tuple-element.80), channel_id=1, source_target_pairs={{0,2},{1,3},{2,0},{3,1},{4,6},{5,7},{6,4},{7,5},{8,10},{9,11},{10,... | collective-permute-start | bytes 196616 | tf_op jit(solution)/shard_map/ppermute | solution.py:34
  58.2 6.6 %collective-permute-start.24 = (bf16[128,256]{1,0:T(8,128)(2,1)S(1)}, bf16[128,256]{1,0:T(8,128)(2,1)S(1)}, u32[]{:S(2)}, u32[]{:S(2)}) collective-permute-start(bf16[128,256]{1,0:T(8,128)(2,1)S(1)} %get-tuple-element.81), channel_id=1, source_target_pairs={{0,3},{1,2},{2,1},{3,0},{4,7},{5,6},{6,5},{7,4},{8,11},{9,10},{10,... | collective-permute-start | bytes 196616 | tf_op jit(solution)/shard_map/ppermute | solution.py:34
  68.0 4.5 %collective-permute-start.28 = (bf16[4,256,512]{2,1,0:T(8,128)(2,1)S(1)}, bf16[4,256,512]{2,1,0:T(8,128)(2,1)S(1)}, u32[]{:S(2)}, u32[]{:S(2)}) collective-permute-start(bf16[4,256,512]{2,1,0:T(8,128)(2,1)S(1)} %back.3), channel_id=1, source_target_pairs={{0,4},{4,0},{8,12},{12,8},{16,20},{20,16},{24,28},{28,24},{1,5},{5... | collective-permute-start | bytes 3145736 | tf_op jit(solution)/shard_map/ppermute | solution.py:34
  68.0 9.4 %collective-permute-start.29 = (bf16[128,512]{1,0:T(8,128)(2,1)S(1)}, bf16[128,512]{1,0:T(8,128)(2,1)S(1)}, u32[]{:S(2)}, u32[]{:S(2)}) collective-permute-start(bf16[128,512]{1,0:T(8,128)(2,1)S(1)} %get-tuple-element.92), channel_id=1, source_target_pairs={{0,1},{1,0},{2,3},{3,2},{4,5},{5,4},{6,7},{7,6},{8,9},{9,8},{10,11... | collective-permute-start | bytes 393224 | tf_op jit(solution)/shard_map/ppermute | solution.py:34
  68.1 6.3 %collective-permute-start.30 = (bf16[128,256]{1,0:T(8,128)(2,1)S(1)}, bf16[128,256]{1,0:T(8,128)(2,1)S(1)}, u32[]{:S(2)}, u32[]{:S(2)}) collective-permute-start(bf16[128,256]{1,0:T(8,128)(2,1)S(1)} %get-tuple-element.94), channel_id=1, source_target_pairs={{0,2},{1,3},{2,0},{3,1},{4,6},{5,7},{6,4},{7,5},{8,10},{9,11},{10,... | collective-permute-start | bytes 196616 | tf_op jit(solution)/shard_map/ppermute | solution.py:34
  71.0 6.4 %collective-permute-start.31 = (bf16[128,256]{1,0:T(8,128)(2,1)S(1)}, bf16[128,256]{1,0:T(8,128)(2,1)S(1)}, u32[]{:S(2)}, u32[]{:S(2)}) collective-permute-start(bf16[128,256]{1,0:T(8,128)(2,1)S(1)} %get-tuple-element.95), channel_id=1, source_target_pairs={{0,3},{1,2},{2,1},{3,0},{4,7},{5,6},{6,5},{7,4},{8,11},{9,10},{10,... | collective-permute-start | bytes 196616 | tf_op jit(solution)/shard_map/ppermute | solution.py:34
  (12 other events, 23.0 us)

commit v5 on v4

--- a/solution.py
+++ b/solution.py
@@ -347,6 +347,8 @@
         return flip(x, "node", 1, nodes)
 
     sib_tokens = swap(tokens)
+    cosine, sine = angle_tables(positions)
+    pos = positions.reshape(1, count)
     lines, pieces = [], []
     beside = flip(key_weight, "local", 1, locs)
     for pair in range(PAIRS):
@@ -354,15 +356,13 @@
         if pair:
             own = after(own, lines[-1])
         shards = [own, beside] + [flip(own, "local", k, locs) for k in range(2, locs)]
-        shards[-1] = after(shards[-1], *((own_x, pieces[-1][-1]) if pair else (sib_tokens,)))
+        shards[-1] = after(shards[-1], *((own_x, pieces[-1][-1]) if pair else (sib_tokens, cosine, sine)))
         lines.append(put_in_line(pair, width, place, shards))
-        pieces.append([lines[-1]] + [flip(lines[-1], "node", 2 * m, nodes) for m in range(1, chips)])
+        sends = [after(lines[-1], *pieces[-1][1:3]) if pair and m == chips - 1 else lines[-1] for m in range(chips)]
+        pieces.append([lines[-1]] + [flip(sends[m], "node", 2 * m, nodes) for m in range(1, chips)])
         if not pair:
             own_x, sib_x = cut(place, tokens, after(sib_tokens, lines[0]), chips, block, core)
     own_turned, sib_turned = turn(own_x, sib_x)
-
-    cosine, sine = angle_tables(positions)
-    pos = positions.reshape(1, count)
 
     def raw_of(pair, *others):
         sib, own = (after(x, *others) if others else x for x in (sib_x, own_x))

time: 78.4 us -> 79 us (level)
  starting transfers between devices: 32.7 us -> 37.2 us
  waiting for transfers between devices: 20 us -> 16 us
    ppermute x32, starting transfers between devices: 32.7 us -> 37.2 us  [flip(): return lax.ppermute(x, axis, [(i, i ^ mask) for i in range(size)])]
    ppermute x32, waiting for transfers between devices: 20 us -> 16 us  [flip(): return lax.ppermute(x, axis, [(i, i ^ mask) for i in range(size)])]
  transfers between devices with their start and end apart: 32 -> 32, of which waited for: 12 -> 14; matrix products, arithmetic and copies ran while one was open for 3% -> 3% of each run, Pallas kernels for 26% -> 26%
where the time goes in v5:
time: 79 us; the launch traced here: 78.7 us
  starting transfers between devices  37.2 us (47%)
  Pallas kernels  21.6 us (27%)
  waiting for transfers between devices  16 us (20%)
  other arithmetic  2.23 us (3%)
  between operations  0.92 us (1%)
  local copies, waits for them, and re-layouts  0.9 us (1%)
    ppermute x32, starting transfers between devices, flip(): return lax.ppermute(x, axis, [(i, i ^ mask) for i in range(size)])  37.2 us
    ppermute x32, waiting for transfers between devices, flip(): return lax.ppermute(x, axis, [(i, i ^ mask) for i in range(size)])  16 us
    pallas_call x2, Pallas kernels, attend(): pl.pallas_call(functools.partial(attend_kernel, pair, heads, group), out_...  5.8 us
    pallas_call x4, Pallas kernels, raw_terms(): pl.pallas_call(raw_kernel, out_shape=[jax.ShapeDtypeStruct((count, HEAD_S...  3.9 us
    pallas_call x2, Pallas kernels, back(): pl.pallas_call(functools.partial(back_kernel, pairs, heads, parts), out_s...  2.57 us
    pallas_call x2, Pallas kernels, terms(): pl.pallas_call(functools.partial(terms_kernel, heads), out_shape=outs, in...  2.49 us
    pallas_call x1, Pallas kernels, join(): pl.pallas_call(join_kernel, out_shape=jax.ShapeDtypeStruct((count, 2 * ch...  1.93 us
    pallas_call x1, Pallas kernels, cut(): pl.pallas_call(cut_kernel, out_shape=[jax.ShapeDtypeStruct((chips, count,...  1.82 us
  transfers between devices with their start and end apart: 32, of which 14 were waited for; matrix products, arithmetic and copies ran while one was open for 3% of the time, Pallas kernels for 26%

profile of v5, /device:TPU:0, one launch (start us, length us, event | category | flops | bytes accessed | tf_op | source)
XLA Modules:
  0.0 78.7 jit_solution(18035968149212270525)
XLA Ops:
  2.0 4.7 %collective-permute-start.3 = (bf16[128,256]{1,0:T(8,128)(2,1)S(1)}, bf16[128,256]{1,0:T(8,128)(2,1)S(1)}, u32[]{:S(2)}, u32[]{:S(2)}) collective-permute-start(bf16[128,256]{1,0:T(8,128)(2,1)S(1)} %get-tuple-element.101.refs_0_), channel_id=1, source_target_pairs={{0,3},{1,2},{2,1},{3,0},{4,7},{5,6},{6,5},{7,4},{8,11},{9,10},{10,... | collective-permute-start | bytes 196616 | tf_op jit(solution)/shard_map/ppermute | solution.py:34
  9.6 3.3 %collective-permute-done.2.refs_2_ = bf16[128,256]{1,0:T(8,128)(2,1)S(1)} collective-permute-done((bf16[128,256]{1,0:T(8,128)(2,1)S(1)}, bf16[128,256]{1,0:T(8,128)(2,1)S(1)}, u32[]{:S(2)}, u32[]{:S(2)}) %collective-permute-start.2) | collective-permute-done | bytes 65568 | tf_op jit(solution)/shard_map/ppermute | solution.py:34
  14.5 2.5 %collective-permute-start.6 = (bf16[4,128,256]{2,1,0:T(8,128)(2,1)S(1)}, bf16[4,128,256]{2,1,0:T(8,128)(2,1)S(1)}, u32[]{:S(2)}, u32[]{:S(2)}) collective-permute-start(bf16[4,128,256]{2,1,0:T(8,128)(2,1)S(1)} %line.2.refs_0_.refs_4_), channel_id=1, source_target_pairs={{0,24},{4,28},{8,16},{12,20},{16,8},{20,12},{24,0},{28,4},{1,25},{... | collective-permute-start | bytes 786440 | tf_op jit(solution)/shard_map/ppermute | solution.py:34
  18.1 2.8 %collective-permute-start.12 = (bf16[128,256]{1,0:T(8,128)(2,1)S(1)}, bf16[128,256]{1,0:T(8,128)(2,1)S(1)}, u32[]{:S(2)}, u32[]{:S(2)}) collective-permute-start(bf16[128,256]{1,0:T(8,128)(2,1)S(1)} %get-tuple-element.64.refs_0_), channel_id=1, source_target_pairs={{0,3},{1,2},{2,1},{3,0},{4,7},{5,6},{6,5},{7,4},{8,11},{9,10},{10,... | collective-permute-start | bytes 196616 | tf_op jit(solution)/shard_map/ppermute | solution.py:34
  21.0 1.8 %cut.1 = (bf16[4,256,512]{2,1,0:T(8,128)(2,1)S(1)}, bf16[4,256,512]{2,1,0:T(8,128)(2,1)S(1)}) custom-call(s32[2]{0:T(128)S(1)} %pad_add_fusion.place_ref, bf16[256,4096]{1,0:T(8,128)(2,1)} %x_hbm.1, bf16[256,4096]{1,0:T(8,128)(2,1)S(1)} %collective-permute-done.sib_hbm), custom_call_target="tpu_custom_call" | custom-call | flops 1 | bytes 1 | tf_op jit(solution)/shard_map/cut/pallas_call | solution.py:276
  22.9 1.4 %collective-permute-done.12.refs_3_ = bf16[128,256]{1,0:T(8,128)(2,1)S(1)} collective-permute-done((bf16[128,256]{1,0:T(8,128)(2,1)S(1)}, bf16[128,256]{1,0:T(8,128)(2,1)S(1)}, u32[]{:S(2)}, u32[]{:S(2)}) %collective-permute-start.12) | collective-permute-done | bytes 65568 | tf_op jit(solution)/shard_map/ppermute | solution.py:34
  24.8 1.3 %collective-permute-done.11.refs_2_ = bf16[128,256]{1,0:T(8,128)(2,1)S(1)} collective-permute-done((bf16[128,256]{1,0:T(8,128)(2,1)S(1)}, bf16[128,256]{1,0:T(8,128)(2,1)S(1)}, u32[]{:S(2)}, u32[]{:S(2)}) %collective-permute-start.11) | collective-permute-done | bytes 65568 | tf_op jit(solution)/shard_map/ppermute | solution.py:34
  26.7 1.6 %collective-permute-start.14 = (bf16[4,128,256]{2,1,0:T(8,128)(2,1)S(1)}, bf16[4,128,256]{2,1,0:T(8,128)(2,1)S(1)}, u32[]{:S(2)}, u32[]{:S(2)}) collective-permute-start(bf16[4,128,256]{2,1,0:T(8,128)(2,1)S(1)} %line.3.refs_0_.refs_8_), channel_id=1, source_target_pairs={{0,16},{4,20},{8,24},{12,28},{16,0},{20,4},{24,8},{28,12},{1,17},{... | collective-permute-start | bytes 786440 | tf_op jit(solution)/shard_map/ppermute | solution.py:34
  28.3 1.5 %collective-permute-start.13 = (bf16[4,128,256]{2,1,0:T(8,128)(2,1)S(1)}, bf16[4,128,256]{2,1,0:T(8,128)(2,1)S(1)}, u32[]{:S(2)}, u32[]{:S(2)}) collective-permute-start(bf16[4,128,256]{2,1,0:T(8,128)(2,1)S(1)} %line.3.refs_0_.refs_8_), channel_id=1, source_target_pairs={{0,8},{4,12},{8,0},{12,4},{16,24},{20,28},{24,16},{28,20},{1,9},{5... | collective-permute-start | bytes 786440 | tf_op jit(solution)/shard_map/ppermute | solution.py:34
  33.1 2.9 %attend.2 = (bf16[256,128]{1,0:T(8,128)(2,1)S(1)}, bf16[256,128]{1,0:T(8,128)(2,1)S(1)}) custom-call(s32[1,256]{1,0:T(1,128)S(1)} %bitcast.3, f32[256,128]{1,0:T(8,128)S(1)} %get-tuple-element.105.cos_ref, f32[256,128]{1,0:T(8,128)S(1)} %get-tuple-element.106.sin_ref, f32[256,128]{1,0:T(8,128)S(1)} %get-tuple-element.53.refs_0_, ...), custom_call_target="tpu_custom_call" | custom-call | flops 1 | bytes 1 | tf_op jit(solution)/shard_map/attend/pallas_call | solution.py:151
  38.7 1.4 %collective-permute-start.20 = (bf16[4,128,256]{2,1,0:T(8,128)(2,1)S(1)}, bf16[4,128,256]{2,1,0:T(8,128)(2,1)S(1)}, u32[]{:S(2)}, u32[]{:S(2)}) collective-permute-start(bf16[4,128,256]{2,1,0:T(8,128)(2,1)S(1)} %get-tuple-element.79), channel_id=1, source_target_pairs={{0,8},{4,12},{8,0},{12,4},{16,24},{20,28},{24,16},{28,20},{1,9},{5... | collective-permute-start | bytes 786440 | tf_op jit(solution)/shard_map/ppermute | solution.py:34
  40.1 1.5 %collective-permute-start.21 = (bf16[4,128,256]{2,1,0:T(8,128)(2,1)S(1)}, bf16[4,128,256]{2,1,0:T(8,128)(2,1)S(1)}, u32[]{:S(2)}, u32[]{:S(2)}) collective-permute-start(bf16[4,128,256]{2,1,0:T(8,128)(2,1)S(1)} %get-tuple-element.80), channel_id=1, source_target_pairs={{0,16},{4,20},{8,24},{12,28},{16,0},{20,4},{24,8},{28,12},{1,17},{... | collective-permute-start | bytes 786440 | tf_op jit(solution)/shard_map/ppermute | solution.py:34
  44.9 2.9 %attend.3 = (bf16[256,128]{1,0:T(8,128)(2,1)S(1)}, bf16[256,128]{1,0:T(8,128)(2,1)S(1)}) custom-call(s32[1,256]{1,0:T(1,128)S(1)} %bitcast.4, f32[256,128]{1,0:T(8,128)S(1)} %get-tuple-element.105.cos_ref, f32[256,128]{1,0:T(8,128)S(1)} %get-tuple-element.106.sin_ref, f32[256,128]{1,0:T(8,128)S(1)} %get-tuple-element.67.refs_0_, ...), custom_call_target="tpu_custom_call" | custom-call | flops 1 | bytes 1 | tf_op jit(solution)/shard_map/attend/pallas_call | solution.py:151
  49.4 1.2 %terms.3 = (f32[4,128,256]{2,1,0:T(8,128)S(1)}, bf16[4,128,256]{2,1,0:T(8,128)(2,1)S(1)}, bf16[4,128,256]{2,1,0:T(8,128)(2,1)S(1)}, bf16[4,128,256]{2,1,0:T(8,128)(2,1)S(1)}) custom-call(s32[2]{0:T(128)S(1)} %pad_add_fusion.place_ref, bf16[4,512,256]{2,1,0:T(8,128)(2,1)S(1)} %get-tuple-element.59.own_ref, ...), custom_call_target="tpu_custom_call" | custom-call | flops 1 | bytes 1 | tf_op jit(solution)/shard_map/terms/pallas_call | solution.py:182
  50.7 1.4 %collective-permute-start.25 = (bf16[4,128,256]{2,1,0:T(8,128)(2,1)S(1)}, bf16[4,128,256]{2,1,0:T(8,128)(2,1)S(1)}, u32[]{:S(2)}, u32[]{:S(2)}) collective-permute-start(bf16[4,128,256]{2,1,0:T(8,128)(2,1)S(1)} %get-tuple-element.85), channel_id=1, source_target_pairs={{0,8},{4,12},{8,0},{12,4},{16,24},{20,28},{24,16},{28,20},{1,9},{5... | collective-permute-start | bytes 786440 | tf_op jit(solution)/shard_map/ppermute | solution.py:34
  52.0 1.5 %collective-permute-start.26 = (bf16[4,128,256]{2,1,0:T(8,128)(2,1)S(1)}, bf16[4,128,256]{2,1,0:T(8,128)(2,1)S(1)}, u32[]{:S(2)}, u32[]{:S(2)}) collective-permute-start(bf16[4,128,256]{2,1,0:T(8,128)(2,1)S(1)} %get-tuple-element.86), channel_id=1, source_target_pairs={{0,16},{4,20},{8,24},{12,28},{16,0},{20,4},{24,8},{28,12},{1,17},{... | collective-permute-start | bytes 786440 | tf_op jit(solution)/shard_map/ppermute | solution.py:34
  54.0 1.5 %collective-permute-start.27 = (bf16[4,128,256]{2,1,0:T(8,128)(2,1)S(1)}, bf16[4,128,256]{2,1,0:T(8,128)(2,1)S(1)}, u32[]{:S(2)}, u32[]{:S(2)}) collective-permute-start(bf16[4,128,256]{2,1,0:T(8,128)(2,1)S(1)} %get-tuple-element.88), channel_id=1, source_target_pairs={{0,24},{4,28},{8,16},{12,20},{16,8},{20,12},{24,0},{28,4},{1,25},{... | collective-permute-start | bytes 786440 | tf_op jit(solution)/shard_map/ppermute | solution.py:34
  56.1 2.4 %collective-permute-start.23 = (bf16[128,256]{1,0:T(8,128)(2,1)S(1)}, bf16[128,256]{1,0:T(8,128)(2,1)S(1)}, u32[]{:S(2)}, u32[]{:S(2)}) collective-permute-start(bf16[128,256]{1,0:T(8,128)(2,1)S(1)} %get-tuple-element.82), channel_id=1, source_target_pairs={{0,2},{1,3},{2,0},{3,1},{4,6},{5,7},{6,4},{7,5},{8,10},{9,11},{10,... | collective-permute-start | bytes 196616 | tf_op jit(solution)/shard_map/ppermute | solution.py:34
  58.5 3.1 %collective-permute-start.24 = (bf16[128,256]{1,0:T(8,128)(2,1)S(1)}, bf16[128,256]{1,0:T(8,128)(2,1)S(1)}, u32[]{:S(2)}, u32[]{:S(2)}) collective-permute-start(bf16[128,256]{1,0:T(8,128)(2,1)S(1)} %get-tuple-element.83), channel_id=1, source_target_pairs={{0,3},{1,2},{2,1},{3,0},{4,7},{5,6},{6,5},{7,4},{8,11},{9,10},{10,... | collective-permute-start | bytes 196616 | tf_op jit(solution)/shard_map/ppermute | solution.py:34
  61.6 1.3 %back.2.refs_0_ = bf16[4,256,512]{2,1,0:T(8,128)(2,1)S(1)} custom-call(s32[2]{0:T(128)S(1)} %pad_add_fusion.place_ref, bf16[256,128]{1,0:T(8,128)(2,1)S(1)} %get-tuple-element.75.refs_0_, bf16[256,128]{1,0:T(8,128)(2,1)S(1)} %get-tuple-element.61.refs_1_, bf16[256,128]{1,0:T(8,128)(2,1)S(1)} %get-tuple-element.76.refs_0_.refs_2_, ...), custom_call_target="tpu_custom_call" | custom-call | flops 1 | bytes 1 | tf_op jit(solution)/shard_map/back/pallas_call | solution.py:243
  62.9 1.3 %back.3 = bf16[4,256,512]{2,1,0:T(8,128)(2,1)S(1)} custom-call(s32[2]{0:T(128)S(1)} %pad_add_fusion.place_ref, bf16[256,128]{1,0:T(8,128)(2,1)S(1)} %collective-permute-done.9.refs_2_.refs_0_, bf16[256,128]{1,0:T(8,128)(2,1)S(1)} %collective-permute-done.10.refs_3_.refs_1_, bf16[256,128]{1,0:T(8,128)(2,1)S(1)} %collective-permute-done.18.refs_2_, ...), custom_call_target="tpu_custom_call" | custom-call | flops 1 | bytes 1 | tf_op jit(solution)/shard_map/back/pallas_call | solution.py:243
  66.5 2.9 %collective-permute-start.29 = (bf16[128,512]{1,0:T(8,128)(2,1)S(1)}, bf16[128,512]{1,0:T(8,128)(2,1)S(1)}, u32[]{:S(2)}, u32[]{:S(2)}) collective-permute-start(bf16[128,512]{1,0:T(8,128)(2,1)S(1)} %get-tuple-element.94), channel_id=1, source_target_pairs={{0,1},{1,0},{2,3},{3,2},{4,5},{5,4},{6,7},{7,6},{8,9},{9,8},{10,11... | collective-permute-start | bytes 393224 | tf_op jit(solution)/shard_map/ppermute | solution.py:34
  71.8 1.9 %join.1 = bf16[256,4096]{1,0:T(8,128)(2,1)} custom-call(s32[2]{0:T(128)S(1)} %pad_add_fusion.place_ref, bf16[4,256,512]{2,1,0:T(8,128)(2,1)S(1)} %back.2.refs_0_, bf16[4,256,512]{2,1,0:T(8,128)(2,1)S(1)} %collective-permute-done.28.refs_1_), custom_call_target="tpu_custom_call" | custom-call | flops 1 | bytes 1 | tf_op jit(solution)/shard_map/join/pallas_call | solution.py:314
  73.7 4.2 %collective-permute-done.30 = bf16[128,256]{1,0:T(8,128)(2,1)S(1)} collective-permute-done((bf16[128,256]{1,0:T(8,128)(2,1)S(1)}, bf16[128,256]{1,0:T(8,128)(2,1)S(1)}, u32[]{:S(2)}, u32[]{:S(2)}) %collective-permute-start.30) | collective-permute-done | bytes 65568 | tf_op jit(solution)/shard_map/ppermute | solution.py:34
  (73 shorter events, 25.7 us)
Async XLA Ops:
  0.6 9.0 %collective-permute-start = (bf16[256,4096]{1,0:T(8,128)(2,1)}, bf16[256,4096]{1,0:T(8,128)(2,1)S(1)}, u32[]{:S(2)}, u32[]{:S(2)}) collective-permute-start(bf16[256,4096]{1,0:T(8,128)(2,1)} %x_hbm.1), channel_id=1, source_target_pairs={{0,4},{4,0},{8,12},{12,8},{16,20},{20,16},{24,28},{28,24},{1,5},{5... | collective-permute-start | bytes 6291464 | tf_op jit(solution)/shard_map/ppermute | solution.py:34
  2.0 7.6 %collective-permute-start.3 = (bf16[128,256]{1,0:T(8,128)(2,1)S(1)}, bf16[128,256]{1,0:T(8,128)(2,1)S(1)}, u32[]{:S(2)}, u32[]{:S(2)}) collective-permute-start(bf16[128,256]{1,0:T(8,128)(2,1)S(1)} %get-tuple-element.101.refs_0_), channel_id=1, source_target_pairs={{0,3},{1,2},{2,1},{3,0},{4,7},{5,6},{6,5},{7,4},{8,11},{9,10},{10,... | collective-permute-start | bytes 196616 | tf_op jit(solution)/shard_map/ppermute | solution.py:34
  6.7 6.2 %collective-permute-start.2 = (bf16[128,256]{1,0:T(8,128)(2,1)S(1)}, bf16[128,256]{1,0:T(8,128)(2,1)S(1)}, u32[]{:S(2)}, u32[]{:S(2)}) collective-permute-start(bf16[128,256]{1,0:T(8,128)(2,1)S(1)} %get-tuple-element.101.refs_0_), channel_id=1, source_target_pairs={{0,2},{1,3},{2,0},{3,1},{4,6},{5,7},{6,4},{7,5},{8,10},{9,11},{10,... | collective-permute-start | bytes 196616 | tf_op jit(solution)/shard_map/ppermute | solution.py:34
  6.7 7.2 %collective-permute-start.1 = (bf16[128,512]{1,0:T(8,128)(2,1)}, bf16[128,512]{1,0:T(8,128)(2,1)S(1)}, u32[]{:S(2)}, u32[]{:S(2)}) collective-permute-start(bf16[128,512]{1,0:T(8,128)(2,1)} %param.10), channel_id=1, source_target_pairs={{0,1},{1,0},{2,3},{3,2},{4,5},{5,4},{6,7},{7,6},{8,9},{9,8},{10,11... | collective-permute-start | bytes 393224 | tf_op jit(solution)/shard_map/ppermute | solution.py:34
  14.5 10.3 %collective-permute-start.6 = (bf16[4,128,256]{2,1,0:T(8,128)(2,1)S(1)}, bf16[4,128,256]{2,1,0:T(8,128)(2,1)S(1)}, u32[]{:S(2)}, u32[]{:S(2)}) collective-permute-start(bf16[4,128,256]{2,1,0:T(8,128)(2,1)S(1)} %line.2.refs_0_.refs_4_), channel_id=1, source_target_pairs={{0,24},{4,28},{8,16},{12,20},{16,8},{20,12},{24,0},{28,4},{1,25},{... | collective-permute-start | bytes 786440 | tf_op jit(solution)/shard_map/ppermute | solution.py:34
  17.0 12.7 %collective-permute-start.5 = (bf16[4,128,256]{2,1,0:T(8,128)(2,1)S(1)}, bf16[4,128,256]{2,1,0:T(8,128)(2,1)S(1)}, u32[]{:S(2)}, u32[]{:S(2)}) collective-permute-start(bf16[4,128,256]{2,1,0:T(8,128)(2,1)S(1)} %line.2.refs_0_.refs_4_), channel_id=1, source_target_pairs={{0,16},{4,20},{8,24},{12,28},{16,0},{20,4},{24,8},{28,12},{1,17},{... | collective-permute-start | bytes 786440 | tf_op jit(solution)/shard_map/ppermute | solution.py:34
  17.5 12.2 %collective-permute-start.4 = (bf16[4,128,256]{2,1,0:T(8,128)(2,1)S(1)}, bf16[4,128,256]{2,1,0:T(8,128)(2,1)S(1)}, u32[]{:S(2)}, u32[]{:S(2)}) collective-permute-start(bf16[4,128,256]{2,1,0:T(8,128)(2,1)S(1)} %line.2.refs_0_.refs_4_), channel_id=1, source_target_pairs={{0,8},{4,12},{8,0},{12,4},{16,24},{20,28},{24,16},{28,20},{1,9},{5... | collective-permute-start | bytes 786440 | tf_op jit(solution)/shard_map/ppermute | solution.py:34
  18.1 6.2 %collective-permute-start.12 = (bf16[128,256]{1,0:T(8,128)(2,1)S(1)}, bf16[128,256]{1,0:T(8,128)(2,1)S(1)}, u32[]{:S(2)}, u32[]{:S(2)}) collective-permute-start(bf16[128,256]{1,0:T(8,128)(2,1)S(1)} %get-tuple-element.64.refs_0_), channel_id=1, source_target_pairs={{0,3},{1,2},{2,1},{3,0},{4,7},{5,6},{6,5},{7,4},{8,11},{9,10},{10,... | collective-permute-start | bytes 196616 | tf_op jit(solution)/shard_map/ppermute | solution.py:34
  20.8 5.3 %collective-permute-start.11 = (bf16[128,256]{1,0:T(8,128)(2,1)S(1)}, bf16[128,256]{1,0:T(8,128)(2,1)S(1)}, u32[]{:S(2)}, u32[]{:S(2)}) collective-permute-start(bf16[128,256]{1,0:T(8,128)(2,1)S(1)} %get-tuple-element.64.refs_0_), channel_id=1, source_target_pairs={{0,2},{1,3},{2,0},{3,1},{4,6},{5,7},{6,4},{7,5},{8,10},{9,11},{10,... | collective-permute-start | bytes 196616 | tf_op jit(solution)/shard_map/ppermute | solution.py:34
  26.7 14.9 %collective-permute-start.14 = (bf16[4,128,256]{2,1,0:T(8,128)(2,1)S(1)}, bf16[4,128,256]{2,1,0:T(8,128)(2,1)S(1)}, u32[]{:S(2)}, u32[]{:S(2)}) collective-permute-start(bf16[4,128,256]{2,1,0:T(8,128)(2,1)S(1)} %line.3.refs_0_.refs_8_), channel_id=1, source_target_pairs={{0,16},{4,20},{8,24},{12,28},{16,0},{20,4},{24,8},{28,12},{1,17},{... | collective-permute-start | bytes 786440 | tf_op jit(solution)/shard_map/ppermute | solution.py:34
  28.3 14.0 %collective-permute-start.13 = (bf16[4,128,256]{2,1,0:T(8,128)(2,1)S(1)}, bf16[4,128,256]{2,1,0:T(8,128)(2,1)S(1)}, u32[]{:S(2)}, u32[]{:S(2)}) collective-permute-start(bf16[4,128,256]{2,1,0:T(8,128)(2,1)S(1)} %line.3.refs_0_.refs_8_), channel_id=1, source_target_pairs={{0,8},{4,12},{8,0},{12,4},{16,24},{20,28},{24,16},{28,20},{1,9},{5... | collective-permute-start | bytes 786440 | tf_op jit(solution)/shard_map/ppermute | solution.py:34
  31.3 10.9 %collective-permute-start.15 = (bf16[4,128,256]{2,1,0:T(8,128)(2,1)S(1)}, bf16[4,128,256]{2,1,0:T(8,128)(2,1)S(1)}, u32[]{:S(2)}, u32[]{:S(2)}) collective-permute-start(bf16[4,128,256]{2,1,0:T(8,128)(2,1)S(1)} %line.3.refs_0_.refs_8_), channel_id=1, source_target_pairs={{0,24},{4,28},{8,16},{12,20},{16,8},{20,12},{24,0},{28,4},{1,25},{... | collective-permute-start | bytes 786440 | tf_op jit(solution)/shard_map/ppermute | solution.py:34
  38.7 14.8 %collective-permute-start.20 = (bf16[4,128,256]{2,1,0:T(8,128)(2,1)S(1)}, bf16[4,128,256]{2,1,0:T(8,128)(2,1)S(1)}, u32[]{:S(2)}, u32[]{:S(2)}) collective-permute-start(bf16[4,128,256]{2,1,0:T(8,128)(2,1)S(1)} %get-tuple-element.79), channel_id=1, source_target_pairs={{0,8},{4,12},{8,0},{12,4},{16,24},{20,28},{24,16},{28,20},{1,9},{5... | collective-permute-start | bytes 786440 | tf_op jit(solution)/shard_map/ppermute | solution.py:34
  40.1 13.9 %collective-permute-start.21 = (bf16[4,128,256]{2,1,0:T(8,128)(2,1)S(1)}, bf16[4,128,256]{2,1,0:T(8,128)(2,1)S(1)}, u32[]{:S(2)}, u32[]{:S(2)}) collective-permute-start(bf16[4,128,256]{2,1,0:T(8,128)(2,1)S(1)} %get-tuple-element.80), channel_id=1, source_target_pairs={{0,16},{4,20},{8,24},{12,28},{16,0},{20,4},{24,8},{28,12},{1,17},{... | collective-permute-start | bytes 786440 | tf_op jit(solution)/shard_map/ppermute | solution.py:34
  41.6 12.4 %collective-permute-start.22 = (bf16[4,128,256]{2,1,0:T(8,128)(2,1)S(1)}, bf16[4,128,256]{2,1,0:T(8,128)(2,1)S(1)}, u32[]{:S(2)}, u32[]{:S(2)}) collective-permute-start(bf16[4,128,256]{2,1,0:T(8,128)(2,1)S(1)} %get-tuple-element.81), channel_id=1, source_target_pairs={{0,24},{4,28},{8,16},{12,20},{16,8},{20,12},{24,0},{28,4},{1,25},{... | collective-permute-start | bytes 786440 | tf_op jit(solution)/shard_map/ppermute | solution.py:34
  50.7 14.0 %collective-permute-start.25 = (bf16[4,128,256]{2,1,0:T(8,128)(2,1)S(1)}, bf16[4,128,256]{2,1,0:T(8,128)(2,1)S(1)}, u32[]{:S(2)}, u32[]{:S(2)}) collective-permute-start(bf16[4,128,256]{2,1,0:T(8,128)(2,1)S(1)} %get-tuple-element.85), channel_id=1, source_target_pairs={{0,8},{4,12},{8,0},{12,4},{16,24},{20,28},{24,16},{28,20},{1,9},{5... | collective-permute-start | bytes 786440 | tf_op jit(solution)/shard_map/ppermute | solution.py:34
  52.0 13.7 %collective-permute-start.26 = (bf16[4,128,256]{2,1,0:T(8,128)(2,1)S(1)}, bf16[4,128,256]{2,1,0:T(8,128)(2,1)S(1)}, u32[]{:S(2)}, u32[]{:S(2)}) collective-permute-start(bf16[4,128,256]{2,1,0:T(8,128)(2,1)S(1)} %get-tuple-element.86), channel_id=1, source_target_pairs={{0,16},{4,20},{8,24},{12,28},{16,0},{20,4},{24,8},{28,12},{1,17},{... | collective-permute-start | bytes 786440 | tf_op jit(solution)/shard_map/ppermute | solution.py:34
  54.0 11.8 %collective-permute-start.27 = (bf16[4,128,256]{2,1,0:T(8,128)(2,1)S(1)}, bf16[4,128,256]{2,1,0:T(8,128)(2,1)S(1)}, u32[]{:S(2)}, u32[]{:S(2)}) collective-permute-start(bf16[4,128,256]{2,1,0:T(8,128)(2,1)S(1)} %get-tuple-element.88), channel_id=1, source_target_pairs={{0,24},{4,28},{8,16},{12,20},{16,8},{20,12},{24,0},{28,4},{1,25},{... | collective-permute-start | bytes 786440 | tf_op jit(solution)/shard_map/ppermute | solution.py:34
  56.1 8.1 %collective-permute-start.23 = (bf16[128,256]{1,0:T(8,128)(2,1)S(1)}, bf16[128,256]{1,0:T(8,128)(2,1)S(1)}, u32[]{:S(2)}, u32[]{:S(2)}) collective-permute-start(bf16[128,256]{1,0:T(8,128)(2,1)S(1)} %get-tuple-element.82), channel_id=1, source_target_pairs={{0,2},{1,3},{2,0},{3,1},{4,6},{5,7},{6,4},{7,5},{8,10},{9,11},{10,... | collective-permute-start | bytes 196616 | tf_op jit(solution)/shard_map/ppermute | solution.py:34
  58.5 6.1 %collective-permute-start.24 = (bf16[128,256]{1,0:T(8,128)(2,1)S(1)}, bf16[128,256]{1,0:T(8,128)(2,1)S(1)}, u32[]{:S(2)}, u32[]{:S(2)}) collective-permute-start(bf16[128,256]{1,0:T(8,128)(2,1)S(1)} %get-tuple-element.83), channel_id=1, source_target_pairs={{0,3},{1,2},{2,1},{3,0},{4,7},{5,6},{6,5},{7,4},{8,11},{9,10},{10,... | collective-permute-start | bytes 196616 | tf_op jit(solution)/shard_map/ppermute | solution.py:34
  66.4 5.4 %collective-permute-start.28 = (bf16[4,256,512]{2,1,0:T(8,128)(2,1)S(1)}, bf16[4,256,512]{2,1,0:T(8,128)(2,1)S(1)}, u32[]{:S(2)}, u32[]{:S(2)}) collective-permute-start(bf16[4,256,512]{2,1,0:T(8,128)(2,1)S(1)} %back.3), channel_id=1, source_target_pairs={{0,4},{4,0},{8,12},{12,8},{16,20},{20,16},{24,28},{28,24},{1,5},{5... | collective-permute-start | bytes 3145736 | tf_op jit(solution)/shard_map/ppermute | solution.py:34
  66.5 11.4 %collective-permute-start.29 = (bf16[128,512]{1,0:T(8,128)(2,1)S(1)}, bf16[128,512]{1,0:T(8,128)(2,1)S(1)}, u32[]{:S(2)}, u32[]{:S(2)}) collective-permute-start(bf16[128,512]{1,0:T(8,128)(2,1)S(1)} %get-tuple-element.94), channel_id=1, source_target_pairs={{0,1},{1,0},{2,3},{3,2},{4,5},{5,4},{6,7},{7,6},{8,9},{9,8},{10,11... | collective-permute-start | bytes 393224 | tf_op jit(solution)/shard_map/ppermute | solution.py:34
  69.4 8.6 %collective-permute-start.30 = (bf16[128,256]{1,0:T(8,128)(2,1)S(1)}, bf16[128,256]{1,0:T(8,128)(2,1)S(1)}, u32[]{:S(2)}, u32[]{:S(2)}) collective-permute-start(bf16[128,256]{1,0:T(8,128)(2,1)S(1)} %get-tuple-element.96), channel_id=1, source_target_pairs={{0,2},{1,3},{2,0},{3,1},{4,6},{5,7},{6,4},{7,5},{8,10},{9,11},{10,... | collective-permute-start | bytes 196616 | tf_op jit(solution)/shard_map/ppermute | solution.py:34
  70.6 7.4 %collective-permute-start.31 = (bf16[128,256]{1,0:T(8,128)(2,1)S(1)}, bf16[128,256]{1,0:T(8,128)(2,1)S(1)}, u32[]{:S(2)}, u32[]{:S(2)}) collective-permute-start(bf16[128,256]{1,0:T(8,128)(2,1)S(1)} %get-tuple-element.97), channel_id=1, source_target_pairs={{0,3},{1,2},{2,1},{3,0},{4,7},{5,6},{6,5},{7,4},{8,11},{9,10},{10,... | collective-permute-start | bytes 196616 | tf_op jit(solution)/shard_map/ppermute | solution.py:34
  (12 other events, 29.6 us)

commit v6 on v5

--- a/solution.py
+++ b/solution.py
@@ -376,7 +376,7 @@
         outs = list(terms(locs, place, own_turned, sib_turned, gks[-1], sib_gks[-1]))
         if pair + 1 < PAIRS:
             raw, sib_raw = raw_of(pair + 1, outs[0])
-        sends = [after(out, *parts[1:]) if pair and m == chips - 1 else out for m, out in enumerate(outs)]
+        sends = [after(out, *parts[1:]) if pair and m == 1 else out for m, out in enumerate(outs)]
         parts = outs[:1] + [flip(sends[m], "node", 2 * m, nodes) for m in range(1, chips)]
         if pair + 1 == PAIRS:
             theirs, mine = (

time: 79 us -> 79.3 us (level)
  waiting for transfers between devices: 16 us -> 17.2 us
  starting transfers between devices: 37.2 us -> 36.3 us
    ppermute x32, waiting for transfers between devices: 16 us -> 17.2 us  [flip(): return lax.ppermute(x, axis, [(i, i ^ mask) for i in range(size)])]
    ppermute x32, starting transfers between devices: 37.2 us -> 36.3 us  [flip(): return lax.ppermute(x, axis, [(i, i ^ mask) for i in range(size)])]
  transfers between devices with their start and end apart: 32 -> 32, of which waited for: 14 -> 15; matrix products, arithmetic and copies ran while one was open for 3% -> 3% of each run, Pallas kernels for 26% -> 26%
where the time goes in v6:
time: 79.3 us; the launch traced here: 79.1 us
  starting transfers between devices  36.3 us (46%)
  Pallas kernels  21.6 us (27%)
  waiting for transfers between devices  17.2 us (22%)
  other arithmetic  2.23 us (3%)
  between operations  0.91 us (1%)
  local copies, waits for them, and re-layouts  0.9 us (1%)
    ppermute x32, starting transfers between devices, flip(): return lax.ppermute(x, axis, [(i, i ^ mask) for i in range(size)])  36.3 us
    ppermute x32, waiting for transfers between devices, flip(): return lax.ppermute(x, axis, [(i, i ^ mask) for i in range(size)])  17.2 us
    pallas_call x2, Pallas kernels, attend(): pl.pallas_call(functools.partial(attend_kernel, pair, heads, group), out_...  5.8 us
    pallas_call x4, Pallas kernels, raw_terms(): pl.pallas_call(raw_kernel, out_shape=[jax.ShapeDtypeStruct((count, HEAD_S...  3.9 us
    pallas_call x2, Pallas kernels, back(): pl.pallas_call(functools.partial(back_kernel, pairs, heads, parts), out_s...  2.57 us
    pallas_call x2, Pallas kernels, terms(): pl.pallas_call(functools.partial(terms_kernel, heads), out_shape=outs, in...  2.49 us
    pallas_call x1, Pallas kernels, join(): pl.pallas_call(join_kernel, out_shape=jax.ShapeDtypeStruct((count, 2 * ch...  1.93 us
    pallas_call x1, Pallas kernels, cut(): pl.pallas_call(cut_kernel, out_shape=[jax.ShapeDtypeStruct((chips, count,...  1.82 us
  transfers between devices with their start and end apart: 32, of which 15 were waited for; matrix products, arithmetic and copies ran while one was open for 3% of the time, Pallas kernels for 26%

profile of v6, /device:TPU:0, one launch (start us, length us, event | category | flops | bytes accessed | tf_op | source)
XLA Modules:
  0.0 79.1 jit_solution(793957517141732697)
XLA Ops:
  2.0 4.7 %collective-permute-start.3 = (bf16[128,256]{1,0:T(8,128)(2,1)S(1)}, bf16[128,256]{1,0:T(8,128)(2,1)S(1)}, u32[]{:S(2)}, u32[]{:S(2)}) collective-permute-start(bf16[128,256]{1,0:T(8,128)(2,1)S(1)} %get-tuple-element.101.refs_0_), channel_id=1, source_target_pairs={{0,3},{1,2},{2,1},{3,0},{4,7},{5,6},{6,5},{7,4},{8,11},{9,10},{10,... | collective-permute-start | bytes 196616 | tf_op jit(solution)/shard_map/ppermute | solution.py:34
  9.6 3.3 %collective-permute-done.2.refs_2_ = bf16[128,256]{1,0:T(8,128)(2,1)S(1)} collective-permute-done((bf16[128,256]{1,0:T(8,128)(2,1)S(1)}, bf16[128,256]{1,0:T(8,128)(2,1)S(1)}, u32[]{:S(2)}, u32[]{:S(2)}) %collective-permute-start.2) | collective-permute-done | bytes 65568 | tf_op jit(solution)/shard_map/ppermute | solution.py:34
  14.5 2.5 %collective-permute-start.6 = (bf16[4,128,256]{2,1,0:T(8,128)(2,1)S(1)}, bf16[4,128,256]{2,1,0:T(8,128)(2,1)S(1)}, u32[]{:S(2)}, u32[]{:S(2)}) collective-permute-start(bf16[4,128,256]{2,1,0:T(8,128)(2,1)S(1)} %line.2.refs_0_.refs_4_), channel_id=1, source_target_pairs={{0,24},{4,28},{8,16},{12,20},{16,8},{20,12},{24,0},{28,4},{1,25},{... | collective-permute-start | bytes 786440 | tf_op jit(solution)/shard_map/ppermute | solution.py:34
  18.1 2.8 %collective-permute-start.12 = (bf16[128,256]{1,0:T(8,128)(2,1)S(1)}, bf16[128,256]{1,0:T(8,128)(2,1)S(1)}, u32[]{:S(2)}, u32[]{:S(2)}) collective-permute-start(bf16[128,256]{1,0:T(8,128)(2,1)S(1)} %get-tuple-element.64.refs_0_), channel_id=1, source_target_pairs={{0,3},{1,2},{2,1},{3,0},{4,7},{5,6},{6,5},{7,4},{8,11},{9,10},{10,... | collective-permute-start | bytes 196616 | tf_op jit(solution)/shard_map/ppermute | solution.py:34
  21.0 1.8 %cut.1 = (bf16[4,256,512]{2,1,0:T(8,128)(2,1)S(1)}, bf16[4,256,512]{2,1,0:T(8,128)(2,1)S(1)}) custom-call(s32[2]{0:T(128)S(1)} %pad_add_fusion.place_ref, bf16[256,4096]{1,0:T(8,128)(2,1)} %x_hbm.1, bf16[256,4096]{1,0:T(8,128)(2,1)S(1)} %collective-permute-done.sib_hbm), custom_call_target="tpu_custom_call" | custom-call | flops 1 | bytes 1 | tf_op jit(solution)/shard_map/cut/pallas_call | solution.py:276
  22.9 1.4 %collective-permute-done.12.refs_3_ = bf16[128,256]{1,0:T(8,128)(2,1)S(1)} collective-permute-done((bf16[128,256]{1,0:T(8,128)(2,1)S(1)}, bf16[128,256]{1,0:T(8,128)(2,1)S(1)}, u32[]{:S(2)}, u32[]{:S(2)}) %collective-permute-start.12) | collective-permute-done | bytes 65568 | tf_op jit(solution)/shard_map/ppermute | solution.py:34
  24.8 1.3 %collective-permute-done.11.refs_2_ = bf16[128,256]{1,0:T(8,128)(2,1)S(1)} collective-permute-done((bf16[128,256]{1,0:T(8,128)(2,1)S(1)}, bf16[128,256]{1,0:T(8,128)(2,1)S(1)}, u32[]{:S(2)}, u32[]{:S(2)}) %collective-permute-start.11) | collective-permute-done | bytes 65568 | tf_op jit(solution)/shard_map/ppermute | solution.py:34
  26.7 1.6 %collective-permute-start.14 = (bf16[4,128,256]{2,1,0:T(8,128)(2,1)S(1)}, bf16[4,128,256]{2,1,0:T(8,128)(2,1)S(1)}, u32[]{:S(2)}, u32[]{:S(2)}) collective-permute-start(bf16[4,128,256]{2,1,0:T(8,128)(2,1)S(1)} %line.3.refs_0_.refs_8_), channel_id=1, source_target_pairs={{0,16},{4,20},{8,24},{12,28},{16,0},{20,4},{24,8},{28,12},{1,17},{... | collective-permute-start | bytes 786440 | tf_op jit(solution)/shard_map/ppermute | solution.py:34
  28.3 1.5 %collective-permute-start.13 = (bf16[4,128,256]{2,1,0:T(8,128)(2,1)S(1)}, bf16[4,128,256]{2,1,0:T(8,128)(2,1)S(1)}, u32[]{:S(2)}, u32[]{:S(2)}) collective-permute-start(bf16[4,128,256]{2,1,0:T(8,128)(2,1)S(1)} %line.3.refs_0_.refs_8_), channel_id=1, source_target_pairs={{0,8},{4,12},{8,0},{12,4},{16,24},{20,28},{24,16},{28,20},{1,9},{5... | collective-permute-start | bytes 786440 | tf_op jit(solution)/shard_map/ppermute | solution.py:34
  33.1 2.9 %attend.2 = (bf16[256,128]{1,0:T(8,128)(2,1)S(1)}, bf16[256,128]{1,0:T(8,128)(2,1)S(1)}) custom-call(s32[1,256]{1,0:T(1,128)S(1)} %bitcast.3, f32[256,128]{1,0:T(8,128)S(1)} %get-tuple-element.105.cos_ref, f32[256,128]{1,0:T(8,128)S(1)} %get-tuple-element.106.sin_ref, f32[256,128]{1,0:T(8,128)S(1)} %get-tuple-element.53.refs_0_, ...), custom_call_target="tpu_custom_call" | custom-call | flops 1 | bytes 1 | tf_op jit(solution)/shard_map/attend/pallas_call | solution.py:151
  38.7 1.4 %collective-permute-start.20 = (bf16[4,128,256]{2,1,0:T(8,128)(2,1)S(1)}, bf16[4,128,256]{2,1,0:T(8,128)(2,1)S(1)}, u32[]{:S(2)}, u32[]{:S(2)}) collective-permute-start(bf16[4,128,256]{2,1,0:T(8,128)(2,1)S(1)} %get-tuple-element.79), channel_id=1, source_target_pairs={{0,8},{4,12},{8,0},{12,4},{16,24},{20,28},{24,16},{28,20},{1,9},{5... | collective-permute-start | bytes 786440 | tf_op jit(solution)/shard_map/ppermute | solution.py:34
  40.1 1.5 %collective-permute-start.21 = (bf16[4,128,256]{2,1,0:T(8,128)(2,1)S(1)}, bf16[4,128,256]{2,1,0:T(8,128)(2,1)S(1)}, u32[]{:S(2)}, u32[]{:S(2)}) collective-permute-start(bf16[4,128,256]{2,1,0:T(8,128)(2,1)S(1)} %get-tuple-element.80), channel_id=1, source_target_pairs={{0,16},{4,20},{8,24},{12,28},{16,0},{20,4},{24,8},{28,12},{1,17},{... | collective-permute-start | bytes 786440 | tf_op jit(solution)/shard_map/ppermute | solution.py:34
  44.9 2.9 %attend.3 = (bf16[256,128]{1,0:T(8,128)(2,1)S(1)}, bf16[256,128]{1,0:T(8,128)(2,1)S(1)}) custom-call(s32[1,256]{1,0:T(1,128)S(1)} %bitcast.4, f32[256,128]{1,0:T(8,128)S(1)} %get-tuple-element.105.cos_ref, f32[256,128]{1,0:T(8,128)S(1)} %get-tuple-element.106.sin_ref, f32[256,128]{1,0:T(8,128)S(1)} %get-tuple-element.67.refs_0_, ...), custom_call_target="tpu_custom_call" | custom-call | flops 1 | bytes 1 | tf_op jit(solution)/shard_map/attend/pallas_call | solution.py:151
  49.4 1.2 %terms.3 = (f32[4,128,256]{2,1,0:T(8,128)S(1)}, bf16[4,128,256]{2,1,0:T(8,128)(2,1)S(1)}, bf16[4,128,256]{2,1,0:T(8,128)(2,1)S(1)}, bf16[4,128,256]{2,1,0:T(8,128)(2,1)S(1)}) custom-call(s32[2]{0:T(128)S(1)} %pad_add_fusion.place_ref, bf16[4,512,256]{2,1,0:T(8,128)(2,1)S(1)} %get-tuple-element.59.own_ref, ...), custom_call_target="tpu_custom_call" | custom-call | flops 1 | bytes 1 | tf_op jit(solution)/shard_map/terms/pallas_call | solution.py:182
  50.7 1.4 %collective-permute-start.26 = (bf16[4,128,256]{2,1,0:T(8,128)(2,1)S(1)}, bf16[4,128,256]{2,1,0:T(8,128)(2,1)S(1)}, u32[]{:S(2)}, u32[]{:S(2)}) collective-permute-start(bf16[4,128,256]{2,1,0:T(8,128)(2,1)S(1)} %get-tuple-element.87), channel_id=1, source_target_pairs={{0,16},{4,20},{8,24},{12,28},{16,0},{20,4},{24,8},{28,12},{1,17},{... | collective-permute-start | bytes 786440 | tf_op jit(solution)/shard_map/ppermute | solution.py:34
  52.0 1.4 %collective-permute-start.27 = (bf16[4,128,256]{2,1,0:T(8,128)(2,1)S(1)}, bf16[4,128,256]{2,1,0:T(8,128)(2,1)S(1)}, u32[]{:S(2)}, u32[]{:S(2)}) collective-permute-start(bf16[4,128,256]{2,1,0:T(8,128)(2,1)S(1)} %get-tuple-element.88), channel_id=1, source_target_pairs={{0,24},{4,28},{8,16},{12,20},{16,8},{20,12},{24,0},{28,4},{1,25},{... | collective-permute-start | bytes 786440 | tf_op jit(solution)/shard_map/ppermute | solution.py:34
  55.9 2.4 %collective-permute-start.23 = (bf16[128,256]{1,0:T(8,128)(2,1)S(1)}, bf16[128,256]{1,0:T(8,128)(2,1)S(1)}, u32[]{:S(2)}, u32[]{:S(2)}) collective-permute-start(bf16[128,256]{1,0:T(8,128)(2,1)S(1)} %get-tuple-element.82), channel_id=1, source_target_pairs={{0,2},{1,3},{2,0},{3,1},{4,6},{5,7},{6,4},{7,5},{8,10},{9,11},{10,... | collective-permute-start | bytes 196616 | tf_op jit(solution)/shard_map/ppermute | solution.py:34
  58.3 2.5 %collective-permute-start.24 = (bf16[128,256]{1,0:T(8,128)(2,1)S(1)}, bf16[128,256]{1,0:T(8,128)(2,1)S(1)}, u32[]{:S(2)}, u32[]{:S(2)}) collective-permute-start(bf16[128,256]{1,0:T(8,128)(2,1)S(1)} %get-tuple-element.83), channel_id=1, source_target_pairs={{0,3},{1,2},{2,1},{3,0},{4,7},{5,6},{6,5},{7,4},{8,11},{9,10},{10,... | collective-permute-start | bytes 196616 | tf_op jit(solution)/shard_map/ppermute | solution.py:34
  60.8 1.3 %back.2.refs_0_ = bf16[4,256,512]{2,1,0:T(8,128)(2,1)S(1)} custom-call(s32[2]{0:T(128)S(1)} %pad_add_fusion.place_ref, bf16[256,128]{1,0:T(8,128)(2,1)S(1)} %get-tuple-element.75.refs_0_, bf16[256,128]{1,0:T(8,128)(2,1)S(1)} %get-tuple-element.61.refs_1_, bf16[256,128]{1,0:T(8,128)(2,1)S(1)} %get-tuple-element.76.refs_0_.refs_2_, ...), custom_call_target="tpu_custom_call" | custom-call | flops 1 | bytes 1 | tf_op jit(solution)/shard_map/back/pallas_call | solution.py:243
  62.1 1.3 %back.3 = bf16[4,256,512]{2,1,0:T(8,128)(2,1)S(1)} custom-call(s32[2]{0:T(128)S(1)} %pad_add_fusion.place_ref, bf16[256,128]{1,0:T(8,128)(2,1)S(1)} %collective-permute-done.9.refs_2_.refs_0_, bf16[256,128]{1,0:T(8,128)(2,1)S(1)} %collective-permute-done.10.refs_3_.refs_1_, bf16[256,128]{1,0:T(8,128)(2,1)S(1)} %collective-permute-done.18.refs_2_, ...), custom_call_target="tpu_custom_call" | custom-call | flops 1 | bytes 1 | tf_op jit(solution)/shard_map/back/pallas_call | solution.py:243
  66.7 3.0 %collective-permute-start.29 = (bf16[128,512]{1,0:T(8,128)(2,1)S(1)}, bf16[128,512]{1,0:T(8,128)(2,1)S(1)}, u32[]{:S(2)}, u32[]{:S(2)}) collective-permute-start(bf16[128,512]{1,0:T(8,128)(2,1)S(1)} %get-tuple-element.94), channel_id=1, source_target_pairs={{0,1},{1,0},{2,3},{3,2},{4,5},{5,4},{6,7},{7,6},{8,9},{9,8},{10,11... | collective-permute-start | bytes 393224 | tf_op jit(solution)/shard_map/ppermute | solution.py:34
  69.7 1.6 %collective-permute-start.30 = (bf16[128,256]{1,0:T(8,128)(2,1)S(1)}, bf16[128,256]{1,0:T(8,128)(2,1)S(1)}, u32[]{:S(2)}, u32[]{:S(2)}) collective-permute-start(bf16[128,256]{1,0:T(8,128)(2,1)S(1)} %get-tuple-element.96), channel_id=1, source_target_pairs={{0,2},{1,3},{2,0},{3,1},{4,6},{5,7},{6,4},{7,5},{8,10},{9,11},{10,... | collective-permute-start | bytes 196616 | tf_op jit(solution)/shard_map/ppermute | solution.py:34
  72.1 1.9 %join.1 = bf16[256,4096]{1,0:T(8,128)(2,1)} custom-call(s32[2]{0:T(128)S(1)} %pad_add_fusion.place_ref, bf16[4,256,512]{2,1,0:T(8,128)(2,1)S(1)} %back.2.refs_0_, bf16[4,256,512]{2,1,0:T(8,128)(2,1)S(1)} %collective-permute-done.28.refs_1_), custom_call_target="tpu_custom_call" | custom-call | flops 1 | bytes 1 | tf_op jit(solution)/shard_map/join/pallas_call | solution.py:314
  74.1 4.2 %collective-permute-done.30 = bf16[128,256]{1,0:T(8,128)(2,1)S(1)} collective-permute-done((bf16[128,256]{1,0:T(8,128)(2,1)S(1)}, bf16[128,256]{1,0:T(8,128)(2,1)S(1)}, u32[]{:S(2)}, u32[]{:S(2)}) %collective-permute-start.30) | collective-permute-done | bytes 65568 | tf_op jit(solution)/shard_map/ppermute | solution.py:34
  (73 shorter events, 26.4 us)
Async XLA Ops:
  0.6 9.0 %collective-permute-start = (bf16[256,4096]{1,0:T(8,128)(2,1)}, bf16[256,4096]{1,0:T(8,128)(2,1)S(1)}, u32[]{:S(2)}, u32[]{:S(2)}) collective-permute-start(bf16[256,4096]{1,0:T(8,128)(2,1)} %x_hbm.1), channel_id=1, source_target_pairs={{0,4},{4,0},{8,12},{12,8},{16,20},{20,16},{24,28},{28,24},{1,5},{5... | collective-permute-start | bytes 6291464 | tf_op jit(solution)/shard_map/ppermute | solution.py:34
  2.0 7.6 %collective-permute-start.3 = (bf16[128,256]{1,0:T(8,128)(2,1)S(1)}, bf16[128,256]{1,0:T(8,128)(2,1)S(1)}, u32[]{:S(2)}, u32[]{:S(2)}) collective-permute-start(bf16[128,256]{1,0:T(8,128)(2,1)S(1)} %get-tuple-element.101.refs_0_), channel_id=1, source_target_pairs={{0,3},{1,2},{2,1},{3,0},{4,7},{5,6},{6,5},{7,4},{8,11},{9,10},{10,... | collective-permute-start | bytes 196616 | tf_op jit(solution)/shard_map/ppermute | solution.py:34
  6.7 6.2 %collective-permute-start.2 = (bf16[128,256]{1,0:T(8,128)(2,1)S(1)}, bf16[128,256]{1,0:T(8,128)(2,1)S(1)}, u32[]{:S(2)}, u32[]{:S(2)}) collective-permute-start(bf16[128,256]{1,0:T(8,128)(2,1)S(1)} %get-tuple-element.101.refs_0_), channel_id=1, source_target_pairs={{0,2},{1,3},{2,0},{3,1},{4,6},{5,7},{6,4},{7,5},{8,10},{9,11},{10,... | collective-permute-start | bytes 196616 | tf_op jit(solution)/shard_map/ppermute | solution.py:34
  6.7 7.2 %collective-permute-start.1 = (bf16[128,512]{1,0:T(8,128)(2,1)}, bf16[128,512]{1,0:T(8,128)(2,1)S(1)}, u32[]{:S(2)}, u32[]{:S(2)}) collective-permute-start(bf16[128,512]{1,0:T(8,128)(2,1)} %param.10), channel_id=1, source_target_pairs={{0,1},{1,0},{2,3},{3,2},{4,5},{5,4},{6,7},{7,6},{8,9},{9,8},{10,11... | collective-permute-start | bytes 393224 | tf_op jit(solution)/shard_map/ppermute | solution.py:34
  14.5 10.3 %collective-permute-start.6 = (bf16[4,128,256]{2,1,0:T(8,128)(2,1)S(1)}, bf16[4,128,256]{2,1,0:T(8,128)(2,1)S(1)}, u32[]{:S(2)}, u32[]{:S(2)}) collective-permute-start(bf16[4,128,256]{2,1,0:T(8,128)(2,1)S(1)} %line.2.refs_0_.refs_4_), channel_id=1, source_target_pairs={{0,24},{4,28},{8,16},{12,20},{16,8},{20,12},{24,0},{28,4},{1,25},{... | collective-permute-start | bytes 786440 | tf_op jit(solution)/shard_map/ppermute | solution.py:34
  17.0 12.7 %collective-permute-start.5 = (bf16[4,128,256]{2,1,0:T(8,128)(2,1)S(1)}, bf16[4,128,256]{2,1,0:T(8,128)(2,1)S(1)}, u32[]{:S(2)}, u32[]{:S(2)}) collective-permute-start(bf16[4,128,256]{2,1,0:T(8,128)(2,1)S(1)} %line.2.refs_0_.refs_4_), channel_id=1, source_target_pairs={{0,16},{4,20},{8,24},{12,28},{16,0},{20,4},{24,8},{28,12},{1,17},{... | collective-permute-start | bytes 786440 | tf_op jit(solution)/shard_map/ppermute | solution.py:34
  17.5 12.2 %collective-permute-start.4 = (bf16[4,128,256]{2,1,0:T(8,128)(2,1)S(1)}, bf16[4,128,256]{2,1,0:T(8,128)(2,1)S(1)}, u32[]{:S(2)}, u32[]{:S(2)}) collective-permute-start(bf16[4,128,256]{2,1,0:T(8,128)(2,1)S(1)} %line.2.refs_0_.refs_4_), channel_id=1, source_target_pairs={{0,8},{4,12},{8,0},{12,4},{16,24},{20,28},{24,16},{28,20},{1,9},{5... | collective-permute-start | bytes 786440 | tf_op jit(solution)/shard_map/ppermute | solution.py:34
  18.1 6.2 %collective-permute-start.12 = (bf16[128,256]{1,0:T(8,128)(2,1)S(1)}, bf16[128,256]{1,0:T(8,128)(2,1)S(1)}, u32[]{:S(2)}, u32[]{:S(2)}) collective-permute-start(bf16[128,256]{1,0:T(8,128)(2,1)S(1)} %get-tuple-element.64.refs_0_), channel_id=1, source_target_pairs={{0,3},{1,2},{2,1},{3,0},{4,7},{5,6},{6,5},{7,4},{8,11},{9,10},{10,... | collective-permute-start | bytes 196616 | tf_op jit(solution)/shard_map/ppermute | solution.py:34
  20.8 5.3 %collective-permute-start.11 = (bf16[128,256]{1,0:T(8,128)(2,1)S(1)}, bf16[128,256]{1,0:T(8,128)(2,1)S(1)}, u32[]{:S(2)}, u32[]{:S(2)}) collective-permute-start(bf16[128,256]{1,0:T(8,128)(2,1)S(1)} %get-tuple-element.64.refs_0_), channel_id=1, source_target_pairs={{0,2},{1,3},{2,0},{3,1},{4,6},{5,7},{6,4},{7,5},{8,10},{9,11},{10,... | collective-permute-start | bytes 196616 | tf_op jit(solution)/shard_map/ppermute | solution.py:34
  26.7 14.9 %collective-permute-start.14 = (bf16[4,128,256]{2,1,0:T(8,128)(2,1)S(1)}, bf16[4,128,256]{2,1,0:T(8,128)(2,1)S(1)}, u32[]{:S(2)}, u32[]{:S(2)}) collective-permute-start(bf16[4,128,256]{2,1,0:T(8,128)(2,1)S(1)} %line.3.refs_0_.refs_8_), channel_id=1, source_target_pairs={{0,16},{4,20},{8,24},{12,28},{16,0},{20,4},{24,8},{28,12},{1,17},{... | collective-permute-start | bytes 786440 | tf_op jit(solution)/shard_map/ppermute | solution.py:34
  28.3 14.0 %collective-permute-start.13 = (bf16[4,128,256]{2,1,0:T(8,128)(2,1)S(1)}, bf16[4,128,256]{2,1,0:T(8,128)(2,1)S(1)}, u32[]{:S(2)}, u32[]{:S(2)}) collective-permute-start(bf16[4,128,256]{2,1,0:T(8,128)(2,1)S(1)} %line.3.refs_0_.refs_8_), channel_id=1, source_target_pairs={{0,8},{4,12},{8,0},{12,4},{16,24},{20,28},{24,16},{28,20},{1,9},{5... | collective-permute-start | bytes 786440 | tf_op jit(solution)/shard_map/ppermute | solution.py:34
  31.3 10.9 %collective-permute-start.15 = (bf16[4,128,256]{2,1,0:T(8,128)(2,1)S(1)}, bf16[4,128,256]{2,1,0:T(8,128)(2,1)S(1)}, u32[]{:S(2)}, u32[]{:S(2)}) collective-permute-start(bf16[4,128,256]{2,1,0:T(8,128)(2,1)S(1)} %line.3.refs_0_.refs_8_), channel_id=1, source_target_pairs={{0,24},{4,28},{8,16},{12,20},{16,8},{20,12},{24,0},{28,4},{1,25},{... | collective-permute-start | bytes 786440 | tf_op jit(solution)/shard_map/ppermute | solution.py:34
  38.7 14.8 %collective-permute-start.20 = (bf16[4,128,256]{2,1,0:T(8,128)(2,1)S(1)}, bf16[4,128,256]{2,1,0:T(8,128)(2,1)S(1)}, u32[]{:S(2)}, u32[]{:S(2)}) collective-permute-start(bf16[4,128,256]{2,1,0:T(8,128)(2,1)S(1)} %get-tuple-element.79), channel_id=1, source_target_pairs={{0,8},{4,12},{8,0},{12,4},{16,24},{20,28},{24,16},{28,20},{1,9},{5... | collective-permute-start | bytes 786440 | tf_op jit(solution)/shard_map/ppermute | solution.py:34
  40.1 14.0 %collective-permute-start.21 = (bf16[4,128,256]{2,1,0:T(8,128)(2,1)S(1)}, bf16[4,128,256]{2,1,0:T(8,128)(2,1)S(1)}, u32[]{:S(2)}, u32[]{:S(2)}) collective-permute-start(bf16[4,128,256]{2,1,0:T(8,128)(2,1)S(1)} %get-tuple-element.80), channel_id=1, source_target_pairs={{0,16},{4,20},{8,24},{12,28},{16,0},{20,4},{24,8},{28,12},{1,17},{... | collective-permute-start | bytes 786440 | tf_op jit(solution)/shard_map/ppermute | solution.py:34
  41.6 12.5 %collective-permute-start.22 = (bf16[4,128,256]{2,1,0:T(8,128)(2,1)S(1)}, bf16[4,128,256]{2,1,0:T(8,128)(2,1)S(1)}, u32[]{:S(2)}, u32[]{:S(2)}) collective-permute-start(bf16[4,128,256]{2,1,0:T(8,128)(2,1)S(1)} %get-tuple-element.81), channel_id=1, source_target_pairs={{0,24},{4,28},{8,16},{12,20},{16,8},{20,12},{24,0},{28,4},{1,25},{... | collective-permute-start | bytes 786440 | tf_op jit(solution)/shard_map/ppermute | solution.py:34
  50.7 14.5 %collective-permute-start.26 = (bf16[4,128,256]{2,1,0:T(8,128)(2,1)S(1)}, bf16[4,128,256]{2,1,0:T(8,128)(2,1)S(1)}, u32[]{:S(2)}, u32[]{:S(2)}) collective-permute-start(bf16[4,128,256]{2,1,0:T(8,128)(2,1)S(1)} %get-tuple-element.87), channel_id=1, source_target_pairs={{0,16},{4,20},{8,24},{12,28},{16,0},{20,4},{24,8},{28,12},{1,17},{... | collective-permute-start | bytes 786440 | tf_op jit(solution)/shard_map/ppermute | solution.py:34
  52.0 13.2 %collective-permute-start.27 = (bf16[4,128,256]{2,1,0:T(8,128)(2,1)S(1)}, bf16[4,128,256]{2,1,0:T(8,128)(2,1)S(1)}, u32[]{:S(2)}, u32[]{:S(2)}) collective-permute-start(bf16[4,128,256]{2,1,0:T(8,128)(2,1)S(1)} %get-tuple-element.88), channel_id=1, source_target_pairs={{0,24},{4,28},{8,16},{12,20},{16,8},{20,12},{24,0},{28,4},{1,25},{... | collective-permute-start | bytes 786440 | tf_op jit(solution)/shard_map/ppermute | solution.py:34
  54.1 11.9 %collective-permute-start.25 = (bf16[4,128,256]{2,1,0:T(8,128)(2,1)S(1)}, bf16[4,128,256]{2,1,0:T(8,128)(2,1)S(1)}, u32[]{:S(2)}, u32[]{:S(2)}) collective-permute-start(bf16[4,128,256]{2,1,0:T(8,128)(2,1)S(1)} %get-tuple-element.86), channel_id=1, source_target_pairs={{0,8},{4,12},{8,0},{12,4},{16,24},{20,28},{24,16},{28,20},{1,9},{5... | collective-permute-start | bytes 786440 | tf_op jit(solution)/shard_map/ppermute | solution.py:34
  55.9 8.6 %collective-permute-start.23 = (bf16[128,256]{1,0:T(8,128)(2,1)S(1)}, bf16[128,256]{1,0:T(8,128)(2,1)S(1)}, u32[]{:S(2)}, u32[]{:S(2)}) collective-permute-start(bf16[128,256]{1,0:T(8,128)(2,1)S(1)} %get-tuple-element.82), channel_id=1, source_target_pairs={{0,2},{1,3},{2,0},{3,1},{4,6},{5,7},{6,4},{7,5},{8,10},{9,11},{10,... | collective-permute-start | bytes 196616 | tf_op jit(solution)/shard_map/ppermute | solution.py:34
  58.3 6.2 %collective-permute-start.24 = (bf16[128,256]{1,0:T(8,128)(2,1)S(1)}, bf16[128,256]{1,0:T(8,128)(2,1)S(1)}, u32[]{:S(2)}, u32[]{:S(2)}) collective-permute-start(bf16[128,256]{1,0:T(8,128)(2,1)S(1)} %get-tuple-element.83), channel_id=1, source_target_pairs={{0,3},{1,2},{2,1},{3,0},{4,7},{5,6},{6,5},{7,4},{8,11},{9,10},{10,... | collective-permute-start | bytes 196616 | tf_op jit(solution)/shard_map/ppermute | solution.py:34
  66.6 5.5 %collective-permute-start.28 = (bf16[4,256,512]{2,1,0:T(8,128)(2,1)S(1)}, bf16[4,256,512]{2,1,0:T(8,128)(2,1)S(1)}, u32[]{:S(2)}, u32[]{:S(2)}) collective-permute-start(bf16[4,256,512]{2,1,0:T(8,128)(2,1)S(1)} %back.3), channel_id=1, source_target_pairs={{0,4},{4,0},{8,12},{12,8},{16,20},{20,16},{24,28},{28,24},{1,5},{5... | collective-permute-start | bytes 3145736 | tf_op jit(solution)/shard_map/ppermute | solution.py:34
  66.7 11.5 %collective-permute-start.29 = (bf16[128,512]{1,0:T(8,128)(2,1)S(1)}, bf16[128,512]{1,0:T(8,128)(2,1)S(1)}, u32[]{:S(2)}, u32[]{:S(2)}) collective-permute-start(bf16[128,512]{1,0:T(8,128)(2,1)S(1)} %get-tuple-element.94), channel_id=1, source_target_pairs={{0,1},{1,0},{2,3},{3,2},{4,5},{5,4},{6,7},{7,6},{8,9},{9,8},{10,11... | collective-permute-start | bytes 393224 | tf_op jit(solution)/shard_map/ppermute | solution.py:34
  69.7 8.6 %collective-permute-start.30 = (bf16[128,256]{1,0:T(8,128)(2,1)S(1)}, bf16[128,256]{1,0:T(8,128)(2,1)S(1)}, u32[]{:S(2)}, u32[]{:S(2)}) collective-permute-start(bf16[128,256]{1,0:T(8,128)(2,1)S(1)} %get-tuple-element.96), channel_id=1, source_target_pairs={{0,2},{1,3},{2,0},{3,1},{4,6},{5,7},{6,4},{7,5},{8,10},{9,11},{10,... | collective-permute-start | bytes 196616 | tf_op jit(solution)/shard_map/ppermute | solution.py:34
  71.3 7.0 %collective-permute-start.31 = (bf16[128,256]{1,0:T(8,128)(2,1)S(1)}, bf16[128,256]{1,0:T(8,128)(2,1)S(1)}, u32[]{:S(2)}, u32[]{:S(2)}) collective-permute-start(bf16[128,256]{1,0:T(8,128)(2,1)S(1)} %get-tuple-element.97), channel_id=1, source_target_pairs={{0,3},{1,2},{2,1},{3,0},{4,7},{5,6},{6,5},{7,4},{8,11},{9,10},{10,... | collective-permute-start | bytes 196616 | tf_op jit(solution)/shard_map/ppermute | solution.py:34
  (12 other events, 29.6 us)

commit v7 on v4

--- a/solution.py
+++ b/solution.py
@@ -10,7 +10,7 @@
 
 HEAD_SIZE = 128
 PAIRS = 2
-BATCH = 4
+BATCH = 8
 HBM = pl.BlockSpec(memory_space=pltpu.HBM)
 VMEM = pl.BlockSpec(memory_space=pltpu.VMEM)
 SMEM = pl.BlockSpec(memory_space=pltpu.SMEM)

time: 78.4 us -> 77.9 us (level)
  transfers between devices with their start and end apart: 32 -> 32, of which waited for: 12 -> 12; matrix products, arithmetic and copies ran while one was open for 3% -> 3% of each run, Pallas kernels for 26% -> 25%
where the time goes in v7:
time: 77.9 us; the launch traced here: 77.7 us
  starting transfers between devices  32.7 us (42%)
  Pallas kernels  21 us (27%)
  waiting for transfers between devices  20 us (26%)
  other arithmetic  2.22 us (3%)
  between operations  0.92 us (1%)
  local copies, waits for them, and re-layouts  0.91 us (1%)
    ppermute x32, starting transfers between devices, flip(): return lax.ppermute(x, axis, [(i, i ^ mask) for i in range(size)])  32.7 us
    ppermute x32, waiting for transfers between devices, flip(): return lax.ppermute(x, axis, [(i, i ^ mask) for i in range(size)])  20 us
    pallas_call x2, Pallas kernels, attend(): pl.pallas_call(functools.partial(attend_kernel, pair, heads, group), out_...  5.23 us
    pallas_call x4, Pallas kernels, raw_terms(): pl.pallas_call(raw_kernel, out_shape=[jax.ShapeDtypeStruct((count, HEAD_S...  3.91 us
    pallas_call x2, Pallas kernels, back(): pl.pallas_call(functools.partial(back_kernel, pairs, heads, parts), out_s...  2.57 us
    pallas_call x2, Pallas kernels, terms(): pl.pallas_call(functools.partial(terms_kernel, heads), out_shape=outs, in...  2.49 us
    pallas_call x1, Pallas kernels, join(): pl.pallas_call(join_kernel, out_shape=jax.ShapeDtypeStruct((count, 2 * ch...  1.93 us
    pallas_call x1, Pallas kernels, cut(): pl.pallas_call(cut_kernel, out_shape=[jax.ShapeDtypeStruct((chips, count,...  1.83 us
  transfers between devices with their start and end apart: 32, of which 12 were waited for; matrix products, arithmetic and copies ran while one was open for 3% of the time, Pallas kernels for 25%

profile of v7, /device:TPU:0, one launch (start us, length us, event | category | flops | bytes accessed | tf_op | source)
XLA Modules:
  0.0 77.7 jit_solution(3962402089586047358)
XLA Ops:
  1.1 2.7 %collective-permute-start.1 = (bf16[128,512]{1,0:T(8,128)(2,1)}, bf16[128,512]{1,0:T(8,128)(2,1)S(1)}, u32[]{:S(2)}, u32[]{:S(2)}) collective-permute-start(bf16[128,512]{1,0:T(8,128)(2,1)} %param.10), channel_id=1, source_target_pairs={{0,1},{1,0},{2,3},{3,2},{4,5},{5,4},{6,7},{7,6},{8,9},{9,8},{10,11... | collective-permute-start | bytes 393224 | tf_op jit(solution)/shard_map/ppermute | solution.py:34
  4.7 2.5 %collective-permute-start.3 = (bf16[128,256]{1,0:T(8,128)(2,1)S(1)}, bf16[128,256]{1,0:T(8,128)(2,1)S(1)}, u32[]{:S(2)}, u32[]{:S(2)}) collective-permute-start(bf16[128,256]{1,0:T(8,128)(2,1)S(1)} %get-tuple-element.99.refs_0_), channel_id=1, source_target_pairs={{0,3},{1,2},{2,1},{3,0},{4,7},{5,6},{6,5},{7,4},{8,11},{9,10},{10,... | collective-permute-start | bytes 196616 | tf_op jit(solution)/shard_map/ppermute | solution.py:34
  7.5 4.8 %collective-permute-done.3.refs_3_ = bf16[128,256]{1,0:T(8,128)(2,1)S(1)} collective-permute-done((bf16[128,256]{1,0:T(8,128)(2,1)S(1)}, bf16[128,256]{1,0:T(8,128)(2,1)S(1)}, u32[]{:S(2)}, u32[]{:S(2)}) %collective-permute-start.3) | collective-permute-done | bytes 65568 | tf_op jit(solution)/shard_map/ppermute | solution.py:34
  12.3 2.2 %collective-permute-done.2.refs_2_ = bf16[128,256]{1,0:T(8,128)(2,1)S(1)} collective-permute-done((bf16[128,256]{1,0:T(8,128)(2,1)S(1)}, bf16[128,256]{1,0:T(8,128)(2,1)S(1)}, u32[]{:S(2)}, u32[]{:S(2)}) %collective-permute-start.2) | collective-permute-done | bytes 65568 | tf_op jit(solution)/shard_map/ppermute | solution.py:34
  15.0 2.5 %collective-permute-start.6 = (bf16[4,128,256]{2,1,0:T(8,128)(2,1)S(1)}, bf16[4,128,256]{2,1,0:T(8,128)(2,1)S(1)}, u32[]{:S(2)}, u32[]{:S(2)}) collective-permute-start(bf16[4,128,256]{2,1,0:T(8,128)(2,1)S(1)} %line.2.refs_0_.refs_4_), channel_id=1, source_target_pairs={{0,24},{4,28},{8,16},{12,20},{16,8},{20,12},{24,0},{28,4},{1,25},{... | collective-permute-start | bytes 786440 | tf_op jit(solution)/shard_map/ppermute | solution.py:34
  19.3 2.3 %collective-permute-start.12 = (bf16[128,256]{1,0:T(8,128)(2,1)S(1)}, bf16[128,256]{1,0:T(8,128)(2,1)S(1)}, u32[]{:S(2)}, u32[]{:S(2)}) collective-permute-start(bf16[128,256]{1,0:T(8,128)(2,1)S(1)} %get-tuple-element.63.refs_0_), channel_id=1, source_target_pairs={{0,3},{1,2},{2,1},{3,0},{4,7},{5,6},{6,5},{7,4},{8,11},{9,10},{10,... | collective-permute-start | bytes 196616 | tf_op jit(solution)/shard_map/ppermute | solution.py:34
  21.5 1.8 %cut.1 = (bf16[4,256,512]{2,1,0:T(8,128)(2,1)S(1)}, bf16[4,256,512]{2,1,0:T(8,128)(2,1)S(1)}) custom-call(s32[2]{0:T(128)S(1)} %pad_add_fusion.place_ref, bf16[256,4096]{1,0:T(8,128)(2,1)} %x_hbm.1, bf16[256,4096]{1,0:T(8,128)(2,1)S(1)} %collective-permute-done.sib_hbm), custom_call_target="tpu_custom_call" | custom-call | flops 1 | bytes 1 | tf_op jit(solution)/shard_map/cut/pallas_call | solution.py:276
  23.4 2.0 %collective-permute-done.12.refs_3_ = bf16[128,256]{1,0:T(8,128)(2,1)S(1)} collective-permute-done((bf16[128,256]{1,0:T(8,128)(2,1)S(1)}, bf16[128,256]{1,0:T(8,128)(2,1)S(1)}, u32[]{:S(2)}, u32[]{:S(2)}) %collective-permute-start.12) | collective-permute-done | bytes 65568 | tf_op jit(solution)/shard_map/ppermute | solution.py:34
  25.3 1.6 %collective-permute-done.11.refs_2_ = bf16[128,256]{1,0:T(8,128)(2,1)S(1)} collective-permute-done((bf16[128,256]{1,0:T(8,128)(2,1)S(1)}, bf16[128,256]{1,0:T(8,128)(2,1)S(1)}, u32[]{:S(2)}, u32[]{:S(2)}) %collective-permute-start.11) | collective-permute-done | bytes 65568 | tf_op jit(solution)/shard_map/ppermute | solution.py:34
  27.5 2.5 %collective-permute-start.15 = (bf16[4,128,256]{2,1,0:T(8,128)(2,1)S(1)}, bf16[4,128,256]{2,1,0:T(8,128)(2,1)S(1)}, u32[]{:S(2)}, u32[]{:S(2)}) collective-permute-start(bf16[4,128,256]{2,1,0:T(8,128)(2,1)S(1)} %line.3.refs_0_.refs_8_), channel_id=1, source_target_pairs={{0,24},{4,28},{8,16},{12,20},{16,8},{20,12},{24,0},{28,4},{1,25},{... | collective-permute-start | bytes 786440 | tf_op jit(solution)/shard_map/ppermute | solution.py:34
  34.4 2.6 %attend.2 = (bf16[256,128]{1,0:T(8,128)(2,1)S(1)}, bf16[256,128]{1,0:T(8,128)(2,1)S(1)}) custom-call(s32[1,256]{1,0:T(1,128)S(1)} %bitcast.3, f32[256,128]{1,0:T(8,128)S(1)} %get-tuple-element.103.cos_ref, f32[256,128]{1,0:T(8,128)S(1)} %get-tuple-element.104.sin_ref, f32[256,128]{1,0:T(8,128)S(1)} %get-tuple-element.52.refs_0_, ...), custom_call_target="tpu_custom_call" | custom-call | flops 1 | bytes 1 | tf_op jit(solution)/shard_map/attend/pallas_call | solution.py:151
  39.8 1.6 %collective-permute-start.20 = (bf16[4,128,256]{2,1,0:T(8,128)(2,1)S(1)}, bf16[4,128,256]{2,1,0:T(8,128)(2,1)S(1)}, u32[]{:S(2)}, u32[]{:S(2)}) collective-permute-start(bf16[4,128,256]{2,1,0:T(8,128)(2,1)S(1)} %get-tuple-element.77), channel_id=1, source_target_pairs={{0,8},{4,12},{8,0},{12,4},{16,24},{20,28},{24,16},{28,20},{1,9},{5... | collective-permute-start | bytes 786440 | tf_op jit(solution)/shard_map/ppermute | solution.py:34
  41.3 1.5 %collective-permute-start.21 = (bf16[4,128,256]{2,1,0:T(8,128)(2,1)S(1)}, bf16[4,128,256]{2,1,0:T(8,128)(2,1)S(1)}, u32[]{:S(2)}, u32[]{:S(2)}) collective-permute-start(bf16[4,128,256]{2,1,0:T(8,128)(2,1)S(1)} %get-tuple-element.78), channel_id=1, source_target_pairs={{0,16},{4,20},{8,24},{12,28},{16,0},{20,4},{24,8},{28,12},{1,17},{... | collective-permute-start | bytes 786440 | tf_op jit(solution)/shard_map/ppermute | solution.py:34
  45.9 2.6 %attend.3 = (bf16[256,128]{1,0:T(8,128)(2,1)S(1)}, bf16[256,128]{1,0:T(8,128)(2,1)S(1)}) custom-call(s32[1,256]{1,0:T(1,128)S(1)} %bitcast.4, f32[256,128]{1,0:T(8,128)S(1)} %get-tuple-element.103.cos_ref, f32[256,128]{1,0:T(8,128)S(1)} %get-tuple-element.104.sin_ref, f32[256,128]{1,0:T(8,128)S(1)} %get-tuple-element.65.refs_0_, ...), custom_call_target="tpu_custom_call" | custom-call | flops 1 | bytes 1 | tf_op jit(solution)/shard_map/attend/pallas_call | solution.py:151
  51.4 1.6 %collective-permute-start.25 = (bf16[4,128,256]{2,1,0:T(8,128)(2,1)S(1)}, bf16[4,128,256]{2,1,0:T(8,128)(2,1)S(1)}, u32[]{:S(2)}, u32[]{:S(2)}) collective-permute-start(bf16[4,128,256]{2,1,0:T(8,128)(2,1)S(1)} %get-tuple-element.83), channel_id=1, source_target_pairs={{0,8},{4,12},{8,0},{12,4},{16,24},{20,28},{24,16},{28,20},{1,9},{5... | collective-permute-start | bytes 786440 | tf_op jit(solution)/shard_map/ppermute | solution.py:34
  53.0 1.5 %collective-permute-start.26 = (bf16[4,128,256]{2,1,0:T(8,128)(2,1)S(1)}, bf16[4,128,256]{2,1,0:T(8,128)(2,1)S(1)}, u32[]{:S(2)}, u32[]{:S(2)}) collective-permute-start(bf16[4,128,256]{2,1,0:T(8,128)(2,1)S(1)} %get-tuple-element.84), channel_id=1, source_target_pairs={{0,16},{4,20},{8,24},{12,28},{16,0},{20,4},{24,8},{28,12},{1,17},{... | collective-permute-start | bytes 786440 | tf_op jit(solution)/shard_map/ppermute | solution.py:34
  55.2 1.5 %collective-permute-start.27 = (bf16[4,128,256]{2,1,0:T(8,128)(2,1)S(1)}, bf16[4,128,256]{2,1,0:T(8,128)(2,1)S(1)}, u32[]{:S(2)}, u32[]{:S(2)}) collective-permute-start(bf16[4,128,256]{2,1,0:T(8,128)(2,1)S(1)} %get-tuple-element.86), channel_id=1, source_target_pairs={{0,24},{4,28},{8,16},{12,20},{16,8},{20,12},{24,0},{28,4},{1,25},{... | collective-permute-start | bytes 786440 | tf_op jit(solution)/shard_map/ppermute | solution.py:34
  58.0 1.9 %collective-permute-start.24 = (bf16[128,256]{1,0:T(8,128)(2,1)S(1)}, bf16[128,256]{1,0:T(8,128)(2,1)S(1)}, u32[]{:S(2)}, u32[]{:S(2)}) collective-permute-start(bf16[128,256]{1,0:T(8,128)(2,1)S(1)} %get-tuple-element.81), channel_id=1, source_target_pairs={{0,3},{1,2},{2,1},{3,0},{4,7},{5,6},{6,5},{7,4},{8,11},{9,10},{10,... | collective-permute-start | bytes 196616 | tf_op jit(solution)/shard_map/ppermute | solution.py:34
  62.4 2.1 %collective-permute-done.23 = bf16[128,256]{1,0:T(8,128)(2,1)S(1)} collective-permute-done((bf16[128,256]{1,0:T(8,128)(2,1)S(1)}, bf16[128,256]{1,0:T(8,128)(2,1)S(1)}, u32[]{:S(2)}, u32[]{:S(2)}) %collective-permute-start.23) | collective-permute-done | bytes 65568 | tf_op jit(solution)/shard_map/ppermute | solution.py:34
  64.6 2.1 %collective-permute-done.26.refs_2_ = bf16[4,128,256]{2,1,0:T(8,128)(2,1)S(1)} collective-permute-done((bf16[4,128,256]{2,1,0:T(8,128)(2,1)S(1)}, bf16[4,128,256]{2,1,0:T(8,128)(2,1)S(1)}, u32[]{:S(2)}, u32[]{:S(2)}) %collective-permute-start.26) | collective-permute-done | bytes 262176 | tf_op jit(solution)/shard_map/ppermute | solution.py:34
  67.6 2.9 %collective-permute-start.30 = (bf16[128,256]{1,0:T(8,128)(2,1)S(1)}, bf16[128,256]{1,0:T(8,128)(2,1)S(1)}, u32[]{:S(2)}, u32[]{:S(2)}) collective-permute-start(bf16[128,256]{1,0:T(8,128)(2,1)S(1)} %get-tuple-element.94), channel_id=1, source_target_pairs={{0,2},{1,3},{2,0},{3,1},{4,6},{5,7},{6,4},{7,5},{8,10},{9,11},{10,... | collective-permute-start | bytes 196616 | tf_op jit(solution)/shard_map/ppermute | solution.py:34
  70.4 1.5 %collective-permute-start.31 = (bf16[128,256]{1,0:T(8,128)(2,1)S(1)}, bf16[128,256]{1,0:T(8,128)(2,1)S(1)}, u32[]{:S(2)}, u32[]{:S(2)}) collective-permute-start(bf16[128,256]{1,0:T(8,128)(2,1)S(1)} %get-tuple-element.95), channel_id=1, source_target_pairs={{0,3},{1,2},{2,1},{3,0},{4,7},{5,6},{6,5},{7,4},{8,11},{9,10},{10,... | collective-permute-start | bytes 196616 | tf_op jit(solution)/shard_map/ppermute | solution.py:34
  71.9 1.9 %join.1 = bf16[256,4096]{1,0:T(8,128)(2,1)} custom-call(s32[2]{0:T(128)S(1)} %pad_add_fusion.place_ref, bf16[4,256,512]{2,1,0:T(8,128)(2,1)S(1)} %back.2.refs_0_, bf16[4,256,512]{2,1,0:T(8,128)(2,1)S(1)} %collective-permute-done.28.refs_1_), custom_call_target="tpu_custom_call" | custom-call | flops 1 | bytes 1 | tf_op jit(solution)/shard_map/join/pallas_call | solution.py:314
  73.9 3.0 %collective-permute-done.31 = bf16[128,256]{1,0:T(8,128)(2,1)S(1)} collective-permute-done((bf16[128,256]{1,0:T(8,128)(2,1)S(1)}, bf16[128,256]{1,0:T(8,128)(2,1)S(1)}, u32[]{:S(2)}, u32[]{:S(2)}) %collective-permute-start.31) | collective-permute-done | bytes 65568 | tf_op jit(solution)/shard_map/ppermute | solution.py:34
  (73 shorter events, 23.6 us)
Async XLA Ops:
  0.6 11.6 %collective-permute-start = (bf16[256,4096]{1,0:T(8,128)(2,1)}, bf16[256,4096]{1,0:T(8,128)(2,1)S(1)}, u32[]{:S(2)}, u32[]{:S(2)}) collective-permute-start(bf16[256,4096]{1,0:T(8,128)(2,1)} %x_hbm.1), channel_id=1, source_target_pairs={{0,4},{4,0},{8,12},{12,8},{16,20},{20,16},{24,28},{28,24},{1,5},{5... | collective-permute-start | bytes 6291464 | tf_op jit(solution)/shard_map/ppermute | solution.py:34
  1.1 13.3 %collective-permute-start.1 = (bf16[128,512]{1,0:T(8,128)(2,1)}, bf16[128,512]{1,0:T(8,128)(2,1)S(1)}, u32[]{:S(2)}, u32[]{:S(2)}) collective-permute-start(bf16[128,512]{1,0:T(8,128)(2,1)} %param.10), channel_id=1, source_target_pairs={{0,1},{1,0},{2,3},{3,2},{4,5},{5,4},{6,7},{7,6},{8,9},{9,8},{10,11... | collective-permute-start | bytes 393224 | tf_op jit(solution)/shard_map/ppermute | solution.py:34
  4.7 7.6 %collective-permute-start.3 = (bf16[128,256]{1,0:T(8,128)(2,1)S(1)}, bf16[128,256]{1,0:T(8,128)(2,1)S(1)}, u32[]{:S(2)}, u32[]{:S(2)}) collective-permute-start(bf16[128,256]{1,0:T(8,128)(2,1)S(1)} %get-tuple-element.99.refs_0_), channel_id=1, source_target_pairs={{0,3},{1,2},{2,1},{3,0},{4,7},{5,6},{6,5},{7,4},{8,11},{9,10},{10,... | collective-permute-start | bytes 196616 | tf_op jit(solution)/shard_map/ppermute | solution.py:34
  7.2 7.2 %collective-permute-start.2 = (bf16[128,256]{1,0:T(8,128)(2,1)S(1)}, bf16[128,256]{1,0:T(8,128)(2,1)S(1)}, u32[]{:S(2)}, u32[]{:S(2)}) collective-permute-start(bf16[128,256]{1,0:T(8,128)(2,1)S(1)} %get-tuple-element.99.refs_0_), channel_id=1, source_target_pairs={{0,2},{1,3},{2,0},{3,1},{4,6},{5,7},{6,4},{7,5},{8,10},{9,11},{10,... | collective-permute-start | bytes 196616 | tf_op jit(solution)/shard_map/ppermute | solution.py:34
  15.0 10.3 %collective-permute-start.6 = (bf16[4,128,256]{2,1,0:T(8,128)(2,1)S(1)}, bf16[4,128,256]{2,1,0:T(8,128)(2,1)S(1)}, u32[]{:S(2)}, u32[]{:S(2)}) collective-permute-start(bf16[4,128,256]{2,1,0:T(8,128)(2,1)S(1)} %line.2.refs_0_.refs_4_), channel_id=1, source_target_pairs={{0,24},{4,28},{8,16},{12,20},{16,8},{20,12},{24,0},{28,4},{1,25},{... | collective-permute-start | bytes 786440 | tf_op jit(solution)/shard_map/ppermute | solution.py:34
  17.5 13.6 %collective-permute-start.5 = (bf16[4,128,256]{2,1,0:T(8,128)(2,1)S(1)}, bf16[4,128,256]{2,1,0:T(8,128)(2,1)S(1)}, u32[]{:S(2)}, u32[]{:S(2)}) collective-permute-start(bf16[4,128,256]{2,1,0:T(8,128)(2,1)S(1)} %line.2.refs_0_.refs_4_), channel_id=1, source_target_pairs={{0,16},{4,20},{8,24},{12,28},{16,0},{20,4},{24,8},{28,12},{1,17},{... | collective-permute-start | bytes 786440 | tf_op jit(solution)/shard_map/ppermute | solution.py:34
  18.0 13.1 %collective-permute-start.4 = (bf16[4,128,256]{2,1,0:T(8,128)(2,1)S(1)}, bf16[4,128,256]{2,1,0:T(8,128)(2,1)S(1)}, u32[]{:S(2)}, u32[]{:S(2)}) collective-permute-start(bf16[4,128,256]{2,1,0:T(8,128)(2,1)S(1)} %line.2.refs_0_.refs_4_), channel_id=1, source_target_pairs={{0,8},{4,12},{8,0},{12,4},{16,24},{20,28},{24,16},{28,20},{1,9},{5... | collective-permute-start | bytes 786440 | tf_op jit(solution)/shard_map/ppermute | solution.py:34
  19.3 6.1 %collective-permute-start.12 = (bf16[128,256]{1,0:T(8,128)(2,1)S(1)}, bf16[128,256]{1,0:T(8,128)(2,1)S(1)}, u32[]{:S(2)}, u32[]{:S(2)}) collective-permute-start(bf16[128,256]{1,0:T(8,128)(2,1)S(1)} %get-tuple-element.63.refs_0_), channel_id=1, source_target_pairs={{0,3},{1,2},{2,1},{3,0},{4,7},{5,6},{6,5},{7,4},{8,11},{9,10},{10,... | collective-permute-start | bytes 196616 | tf_op jit(solution)/shard_map/ppermute | solution.py:34
  21.5 5.4 %collective-permute-start.11 = (bf16[128,256]{1,0:T(8,128)(2,1)S(1)}, bf16[128,256]{1,0:T(8,128)(2,1)S(1)}, u32[]{:S(2)}, u32[]{:S(2)}) collective-permute-start(bf16[128,256]{1,0:T(8,128)(2,1)S(1)} %get-tuple-element.63.refs_0_), channel_id=1, source_target_pairs={{0,2},{1,3},{2,0},{3,1},{4,6},{5,7},{6,4},{7,5},{8,10},{9,11},{10,... | collective-permute-start | bytes 196616 | tf_op jit(solution)/shard_map/ppermute | solution.py:34
  27.5 15.3 %collective-permute-start.15 = (bf16[4,128,256]{2,1,0:T(8,128)(2,1)S(1)}, bf16[4,128,256]{2,1,0:T(8,128)(2,1)S(1)}, u32[]{:S(2)}, u32[]{:S(2)}) collective-permute-start(bf16[4,128,256]{2,1,0:T(8,128)(2,1)S(1)} %line.3.refs_0_.refs_8_), channel_id=1, source_target_pairs={{0,24},{4,28},{8,16},{12,20},{16,8},{20,12},{24,0},{28,4},{1,25},{... | collective-permute-start | bytes 786440 | tf_op jit(solution)/shard_map/ppermute | solution.py:34
  30.0 13.3 %collective-permute-start.14 = (bf16[4,128,256]{2,1,0:T(8,128)(2,1)S(1)}, bf16[4,128,256]{2,1,0:T(8,128)(2,1)S(1)}, u32[]{:S(2)}, u32[]{:S(2)}) collective-permute-start(bf16[4,128,256]{2,1,0:T(8,128)(2,1)S(1)} %line.3.refs_0_.refs_8_), channel_id=1, source_target_pairs={{0,16},{4,20},{8,24},{12,28},{16,0},{20,4},{24,8},{28,12},{1,17},{... | collective-permute-start | bytes 786440 | tf_op jit(solution)/shard_map/ppermute | solution.py:34
  30.5 12.8 %collective-permute-start.13 = (bf16[4,128,256]{2,1,0:T(8,128)(2,1)S(1)}, bf16[4,128,256]{2,1,0:T(8,128)(2,1)S(1)}, u32[]{:S(2)}, u32[]{:S(2)}) collective-permute-start(bf16[4,128,256]{2,1,0:T(8,128)(2,1)S(1)} %line.3.refs_0_.refs_8_), channel_id=1, source_target_pairs={{0,8},{4,12},{8,0},{12,4},{16,24},{20,28},{24,16},{28,20},{1,9},{5... | collective-permute-start | bytes 786440 | tf_op jit(solution)/shard_map/ppermute | solution.py:34
  39.8 14.8 %collective-permute-start.20 = (bf16[4,128,256]{2,1,0:T(8,128)(2,1)S(1)}, bf16[4,128,256]{2,1,0:T(8,128)(2,1)S(1)}, u32[]{:S(2)}, u32[]{:S(2)}) collective-permute-start(bf16[4,128,256]{2,1,0:T(8,128)(2,1)S(1)} %get-tuple-element.77), channel_id=1, source_target_pairs={{0,8},{4,12},{8,0},{12,4},{16,24},{20,28},{24,16},{28,20},{1,9},{5... | collective-permute-start | bytes 786440 | tf_op jit(solution)/shard_map/ppermute | solution.py:34
  41.3 13.9 %collective-permute-start.21 = (bf16[4,128,256]{2,1,0:T(8,128)(2,1)S(1)}, bf16[4,128,256]{2,1,0:T(8,128)(2,1)S(1)}, u32[]{:S(2)}, u32[]{:S(2)}) collective-permute-start(bf16[4,128,256]{2,1,0:T(8,128)(2,1)S(1)} %get-tuple-element.78), channel_id=1, source_target_pairs={{0,16},{4,20},{8,24},{12,28},{16,0},{20,4},{24,8},{28,12},{1,17},{... | collective-permute-start | bytes 786440 | tf_op jit(solution)/shard_map/ppermute | solution.py:34
  42.8 12.4 %collective-permute-start.22 = (bf16[4,128,256]{2,1,0:T(8,128)(2,1)S(1)}, bf16[4,128,256]{2,1,0:T(8,128)(2,1)S(1)}, u32[]{:S(2)}, u32[]{:S(2)}) collective-permute-start(bf16[4,128,256]{2,1,0:T(8,128)(2,1)S(1)} %get-tuple-element.79), channel_id=1, source_target_pairs={{0,24},{4,28},{8,16},{12,20},{16,8},{20,12},{24,0},{28,4},{1,25},{... | collective-permute-start | bytes 786440 | tf_op jit(solution)/shard_map/ppermute | solution.py:34
  51.4 13.2 %collective-permute-start.25 = (bf16[4,128,256]{2,1,0:T(8,128)(2,1)S(1)}, bf16[4,128,256]{2,1,0:T(8,128)(2,1)S(1)}, u32[]{:S(2)}, u32[]{:S(2)}) collective-permute-start(bf16[4,128,256]{2,1,0:T(8,128)(2,1)S(1)} %get-tuple-element.83), channel_id=1, source_target_pairs={{0,8},{4,12},{8,0},{12,4},{16,24},{20,28},{24,16},{28,20},{1,9},{5... | collective-permute-start | bytes 786440 | tf_op jit(solution)/shard_map/ppermute | solution.py:34
  53.0 13.7 %collective-permute-start.26 = (bf16[4,128,256]{2,1,0:T(8,128)(2,1)S(1)}, bf16[4,128,256]{2,1,0:T(8,128)(2,1)S(1)}, u32[]{:S(2)}, u32[]{:S(2)}) collective-permute-start(bf16[4,128,256]{2,1,0:T(8,128)(2,1)S(1)} %get-tuple-element.84), channel_id=1, source_target_pairs={{0,16},{4,20},{8,24},{12,28},{16,0},{20,4},{24,8},{28,12},{1,17},{... | collective-permute-start | bytes 786440 | tf_op jit(solution)/shard_map/ppermute | solution.py:34
  55.2 11.5 %collective-permute-start.27 = (bf16[4,128,256]{2,1,0:T(8,128)(2,1)S(1)}, bf16[4,128,256]{2,1,0:T(8,128)(2,1)S(1)}, u32[]{:S(2)}, u32[]{:S(2)}) collective-permute-start(bf16[4,128,256]{2,1,0:T(8,128)(2,1)S(1)} %get-tuple-element.86), channel_id=1, source_target_pairs={{0,24},{4,28},{8,16},{12,20},{16,8},{20,12},{24,0},{28,4},{1,25},{... | collective-permute-start | bytes 786440 | tf_op jit(solution)/shard_map/ppermute | solution.py:34
  57.4 7.2 %collective-permute-start.23 = (bf16[128,256]{1,0:T(8,128)(2,1)S(1)}, bf16[128,256]{1,0:T(8,128)(2,1)S(1)}, u32[]{:S(2)}, u32[]{:S(2)}) collective-permute-start(bf16[128,256]{1,0:T(8,128)(2,1)S(1)} %get-tuple-element.80), channel_id=1, source_target_pairs={{0,2},{1,3},{2,0},{3,1},{4,6},{5,7},{6,4},{7,5},{8,10},{9,11},{10,... | collective-permute-start | bytes 196616 | tf_op jit(solution)/shard_map/ppermute | solution.py:34
  58.0 6.6 %collective-permute-start.24 = (bf16[128,256]{1,0:T(8,128)(2,1)S(1)}, bf16[128,256]{1,0:T(8,128)(2,1)S(1)}, u32[]{:S(2)}, u32[]{:S(2)}) collective-permute-start(bf16[128,256]{1,0:T(8,128)(2,1)S(1)} %get-tuple-element.81), channel_id=1, source_target_pairs={{0,3},{1,2},{2,1},{3,0},{4,7},{5,6},{6,5},{7,4},{8,11},{9,10},{10,... | collective-permute-start | bytes 196616 | tf_op jit(solution)/shard_map/ppermute | solution.py:34
  67.4 4.5 %collective-permute-start.28 = (bf16[4,256,512]{2,1,0:T(8,128)(2,1)S(1)}, bf16[4,256,512]{2,1,0:T(8,128)(2,1)S(1)}, u32[]{:S(2)}, u32[]{:S(2)}) collective-permute-start(bf16[4,256,512]{2,1,0:T(8,128)(2,1)S(1)} %back.3), channel_id=1, source_target_pairs={{0,4},{4,0},{8,12},{12,8},{16,20},{20,16},{24,28},{28,24},{1,5},{5... | collective-permute-start | bytes 3145736 | tf_op jit(solution)/shard_map/ppermute | solution.py:34
  67.5 9.4 %collective-permute-start.29 = (bf16[128,512]{1,0:T(8,128)(2,1)S(1)}, bf16[128,512]{1,0:T(8,128)(2,1)S(1)}, u32[]{:S(2)}, u32[]{:S(2)}) collective-permute-start(bf16[128,512]{1,0:T(8,128)(2,1)S(1)} %get-tuple-element.92), channel_id=1, source_target_pairs={{0,1},{1,0},{2,3},{3,2},{4,5},{5,4},{6,7},{7,6},{8,9},{9,8},{10,11... | collective-permute-start | bytes 393224 | tf_op jit(solution)/shard_map/ppermute | solution.py:34
  67.6 6.3 %collective-permute-start.30 = (bf16[128,256]{1,0:T(8,128)(2,1)S(1)}, bf16[128,256]{1,0:T(8,128)(2,1)S(1)}, u32[]{:S(2)}, u32[]{:S(2)}) collective-permute-start(bf16[128,256]{1,0:T(8,128)(2,1)S(1)} %get-tuple-element.94), channel_id=1, source_target_pairs={{0,2},{1,3},{2,0},{3,1},{4,6},{5,7},{6,4},{7,5},{8,10},{9,11},{10,... | collective-permute-start | bytes 196616 | tf_op jit(solution)/shard_map/ppermute | solution.py:34
  70.4 6.4 %collective-permute-start.31 = (bf16[128,256]{1,0:T(8,128)(2,1)S(1)}, bf16[128,256]{1,0:T(8,128)(2,1)S(1)}, u32[]{:S(2)}, u32[]{:S(2)}) collective-permute-start(bf16[128,256]{1,0:T(8,128)(2,1)S(1)} %get-tuple-element.95), channel_id=1, source_target_pairs={{0,3},{1,2},{2,1},{3,0},{4,7},{5,6},{6,5},{7,4},{8,11},{9,10},{10,... | collective-permute-start | bytes 196616 | tf_op jit(solution)/shard_map/ppermute | solution.py:34
  (12 other events, 23.0 us)
